TPU v7x, 32 devices: a whole 2x2x4 slice. The times are simulated.
32 devices in a mesh: parts: 2 (over y), blk: 4 (over z), op: 4 (over x, core).
Axes of the slice: x: 2, y: 2, z: 4, core: 2. Of those that a mesh axis runs over, the one named last changes fastest.
Arguments:
- psi: bfloat16 [16, 8, 128, 128], P(('parts', 'blk')), parts along dimension 0, may hold values from -6 to 6
- left_ops: bfloat16 [32, 8, 128, 128], P(('parts', 'op'), 'blk'), parts along dimension 0, may hold values from -0.5 to 0.5
- right_ops: bfloat16 [32, 8, 128, 128], P(('parts', 'op'), 'blk'), parts along dimension 0, may hold values from -0.1875 to 0.1875
- term_blocks: int32 [32, 8], P(('parts', 'op')), parts along dimension 0, may hold values from 0 to 1, as said below
- left_sizes: int32 [16], P('parts'), parts along dimension 0, may hold values from 1 to 128
- right_sizes: int32 [16], P('parts'), parts along dimension 0, may hold values from 1 to 128
Outputs:
- sigma: bfloat16 [16, 8, 128, 128], P(('parts', 'blk'), 'op'), parts along dimension 0
There are 2 independent parts, one for each index of `parts`. A program takes and returns all parts, laid end to end along the dimension named above; each array names one. Nothing has to cross between parts.
Inputs may be any that keep to these rules, and one draw needn't show every extreme that they name: `term_blocks`: terms come in consecutive groups of 4; within every group, exactly 2 terms act on each left sector.
All inputs are finite; a program needn't handle non-finite values.
Results may differ from a plain program's by a relative error of at most 0.0095.
Values may be sent and summed in bfloat16 or wider, within the bound.
No kernel may reach another device: no remote copies, remote signals or barrier semaphores. Data moves between devices by JAX's collectives and lax.ppermute only.
A program may use at most 128 MiB of HBM per device.

v0:
```python
import functools

import jax
import jax.numpy as jnp
from jax import lax
from jax.experimental import pallas as pl
from jax.experimental.pallas import tpu as pltpu
from jax.sharding import PartitionSpec as P

ANY = pl.BlockSpec(memory_space=pl.ANY)
SMEM = pl.BlockSpec(memory_space=pltpu.SMEM)
VMEM = pl.BlockSpec(memory_space=pltpu.VMEM)
PARAMS = pltpu.CompilerParams(vmem_limit_bytes=32 * 1024 * 1024)
ID_ROWS = 16


def acting_terms(blocks_ref, sector):
    first = jnp.int32(0)
    second = jnp.int32(0)
    for term in reversed(range(blocks_ref.shape[0])):
        acts = blocks_ref[term, sector] > 0
        second = jnp.where(acts, first, second)
        first = jnp.where(acts, term, first)
    return first, second


def place():
    op = lax.axis_index("op")
    return lax.axis_index("blk"), lax.shift_right_logical(op, 1), jnp.bitwise_and(op, 1)


def is_home():
    z, _, c = place()
    return c == jnp.bitwise_and(z, 1)


def pack_kernel(blocks_ref, psi_ref, left_ref, left_out, far_out, near_out, sem):
    z, x, _ = place()
    sectors, tile = psi_ref.shape[0], psi_ref.shape[-1]
    row = lax.broadcasted_iota(jnp.int32, (ID_ROWS, tile), 0)
    ids = jnp.zeros((ID_ROWS, tile), jnp.float32)
    copies = []
    for local in range(sectors):
        for term in acting_terms(blocks_ref, z * sectors + local):
            spot = len(copies)
            ids = jnp.where(row == spot, term.astype(jnp.float32), ids)
            copies.append(
                pltpu.make_async_copy(
                    left_ref.at[term, local], left_out.at[pl.ds(spot * tile, tile)], sem.at[spot]
                )
            )
    far = jnp.bitwise_xor(z, jnp.where(is_home(), 2, 3)) * sectors + x
    near = pl.ds(jnp.bitwise_xor(z, 1) * sectors, sectors)
    for columns, out in ((far, far_out), (near, near_out)):
        copies.append(pltpu.make_async_copy(psi_ref.at[:, columns], out, sem.at[len(copies)]))
    for copy in copies:
        copy.start()
    left_out[pl.ds(2 * sectors * tile, ID_ROWS)] = ids.astype(jnp.bfloat16)
    for copy in copies:
        copy.wait()


def partial_sums(z, distance, sizes, columns, psi, lefts, rights, store):
    lsize_ref, rsize_ref = sizes
    sectors = len(columns)
    owner = jnp.bitwise_xor(z, distance)
    for a in range(sectors):
        blocks = [psi(a, side) for side in range(sectors)]
        tile = blocks[0].shape[-1]
        rows = lax.broadcasted_iota(jnp.int32, (tile, tile), 0)
        lanes = lax.broadcasted_iota(jnp.int32, (tile, tile), 1)
        height = lsize_ref[owner * sectors + a]
        keeps = [(rows < height) & (lanes < rsize_ref[z * sectors + b]) for b in columns]
        wide = jnp.concatenate(
            [
                jnp.where(keep, block.astype(jnp.float32), 0.0).astype(jnp.bfloat16)
                for keep, block in zip(keeps, blocks)
            ],
            axis=1,
        )
        applied = []
        for left in lefts:
            both = jnp.dot(left(a), wide, preferred_element_type=jnp.float32).astype(jnp.bfloat16)
            applied += [both[:tile], both[tile:]]
        for side, b in enumerate(columns):
            picked = [right(a, slot, b) for right in rights for slot in range(2)]
            column = [part[:, side * tile : (side + 1) * tile] for part in applied]
            total = lax.dot_general(
                jnp.concatenate(column, axis=1),
                jnp.concatenate(picked, axis=1),
                (((1,), (1,)), ((), ())),
                preferred_element_type=jnp.float32,
            )
            store(b, a, jnp.where(keeps[side], total, 0.0))


def message(ref, right_ref):
    terms, sectors, tile = right_ref.shape[0], right_ref.shape[1], right_ref.shape[-1]
    ids = ref[pl.ds(2 * sectors * tile, ID_ROWS)].astype(jnp.float32)

    def left(a):
        return ref[pl.ds(2 * a * tile, 2 * tile)]

    def right(a, slot, b):
        spot = 2 * a + slot
        term = jnp.broadcast_to(ids[spot : spot + 1], (tile, tile))
        block = right_ref[0, b].astype(jnp.float32)
        for t in range(1, terms):
            block = jnp.where(term == t, right_ref[t, b].astype(jnp.float32), block)
        return block.astype(jnp.bfloat16)

    return left, right


def near_kernel(lsize_ref, rsize_ref, blocks_ref, *rest):
    psi_ref, left_ref, swapped, direct_a, direct_b, psi_near = rest[:6]
    right_own, right_other, out_ref = rest[6:]
    z, _, _ = place()
    sectors = out_ref.shape[0]
    sizes, columns = (lsize_ref, rsize_ref), range(sectors)

    def store(b, a, total):
        out_ref[b, a] = total

    @pl.when(is_home())
    def _():
        terms = [acting_terms(blocks_ref, z * sectors + a) for a in range(sectors)]
        left, right = message(swapped, right_other)
        partial_sums(
            z, 0, sizes, columns, lambda a, b: psi_ref[a, z * sectors + b],
            [lambda a: jnp.concatenate([left_ref[term, a] for term in terms[a]], axis=0), left],
            [lambda a, slot, b: right_own[terms[a][slot], b], right],
            store,
        )

    @pl.when(jnp.logical_not(is_home()))
    def _():
        pairs = [message(direct_b, right_own), message(direct_a, right_other)]
        lefts, rights = zip(*pairs)
        partial_sums(z, 1, sizes, columns, lambda a, b: psi_near[a, b], lefts, rights, store)


def far_kernel(at_home, lsize_ref, rsize_ref, *rest):
    first, second, psi_same, psi_other, right_own, right_other, near_ref = rest[:7]
    sent_ref, out_ref = rest[7:]
    z, x, _ = place()
    columns = (x, 1 - x)
    far_leaves = lax.shift_right_logical(z, 1) == x

    def psi(a, side):
        return (psi_same, psi_other)[side][a]

    def store_sent(b, a, total):
        sent_ref[b, a] = total.astype(sent_ref.dtype)

    def store_kept(b, a, total):
        out_ref[b, a] = total
        sent_ref[b, a] = near_ref[b, a].astype(sent_ref.dtype)

    for leaves, store in ((True, store_sent), (False, store_kept)):

        @pl.when((is_home() == at_home) & (far_leaves == leaves))
        def _(store=store):
            lefts, rights = zip(message(first, right_own), message(second, right_other))
            distance = 2 if at_home else 3
            partial_sums(z, distance, (lsize_ref, rsize_ref), columns, psi, lefts, rights, store)


def shards(psi, left_ops, right_ops, term_blocks, left_sizes, right_sizes):
    n = 4
    sectors, tile = psi.shape[0], psi.shape[-1]
    block = functools.partial(jax.ShapeDtypeStruct, dtype=jnp.bfloat16)
    out_shape = (sectors, sectors, tile, tile)

    def over_op(array, step):
        return lax.ppermute(array, "op", [(o, o ^ step) for o in range(n)])

    def over_both(array, target):
        pairs = []
        for z in range(n):
            for o in range(n):
                to = target(z, o >> 1, o & 1, o & 1 == z & 1)
                if to is not None:
                    pairs.append((z * n + o, to[0] * n + 2 * to[1] + to[2]))
        return lax.ppermute(array, ("blk", "op"), pairs)

    def over_z(array, home_step, other_step):
        def target(z, x, c, home):
            step = home_step if home else other_step
            return None if step is None else (z ^ step, x, z & 1)

        return over_both(array, target)

    left_sent, far_sent, near_sent = pl.pallas_call(
        pack_kernel,
        out_shape=[
            block((2 * sectors * tile + ID_ROWS, tile)),
            block((sectors, tile, tile)),
            block(out_shape),
        ],
        in_specs=[SMEM, ANY, ANY],
        out_specs=[VMEM] * 3,
        scratch_shapes=[pltpu.SemaphoreType.DMA((2 * sectors + 2,))],
        compiler_params=pltpu.CompilerParams(vmem_limit_bytes=60 * 1024 * 1024),
        name="pack",
    )(term_blocks, psi, left_ops)
    direct_a = over_z(left_sent, 2, 1)
    direct_b = over_z(left_sent, 1, 2)
    far_same = over_z(far_sent, 2, 3)
    far_other = over_op(far_same, 2)
    psi_near = over_z(near_sent, 1, None)
    passed_a = over_z(direct_a, 1, None)
    passed_b = over_z(direct_b, 1, None)
    swapped = over_op(left_sent, 1)
    held, _ = lax.optimization_barrier((right_ops, left_sent))
    rights = [right_ops, over_op(held, 1)]

    def apply(kernel, name, outs, scalars, *operands):
        return pl.pallas_call(
            kernel,
            out_shape=[jax.ShapeDtypeStruct(out_shape, dtype) for dtype in outs],
            in_specs=[SMEM] * len(scalars) + [VMEM] * len(operands),
            out_specs=[VMEM] * len(outs),
            compiler_params=PARAMS,
            cost_estimate=pl.CostEstimate(
                flops=64 * tile**3 * sectors**2, bytes_accessed=2**20, transcendentals=0
            ),
            name=name,
        )(*scalars, *operands)

    sizes = (left_sizes, right_sizes)
    (near,) = apply(
        near_kernel, "near", [jnp.float32], sizes + (term_blocks,),
        psi, left_ops, swapped, direct_a, direct_b, psi_near, *rights,
    )

    def far_part(at_home, first, second):
        sent, far = apply(
            functools.partial(far_kernel, at_home), "far_home" if at_home else "far_other",
            [jnp.bfloat16, jnp.float32], sizes, first, second, far_same, far_other, *rights, near,
        )
        arrived = over_both(
            sent, lambda z, x, c, home: (z, 1 - x, c) if home == at_home else None
        )
        return far, arrived

    home_far, home_arrived = far_part(True, direct_a, direct_b)
    other_far, other_arrived = far_part(False, passed_a, passed_b)
    z, op = lax.axis_index("blk"), lax.axis_index("op")
    home = z % 2 == op % 2
    far = jnp.where(home, home_far, other_far)
    arrived = jnp.where(home, home_arrived, other_arrived)
    kept = jnp.where(z // 2 == op // 2, near, far)
    return (kept + arrived.astype(jnp.float32)).astype(jnp.bfloat16)


def wide_shards(psi, left_ops, right_ops, term_blocks, left_sizes, right_sizes):
    sectors_here = psi.shape[0]
    tile_size = psi.shape[2]
    left_first = lax.axis_index("blk") * sectors_here
    positions = lax.broadcasted_iota(jnp.int32, (tile_size,), 0)
    left_local = lax.dynamic_slice_in_dim(left_sizes, left_first, sectors_here)
    left_keep = positions[None, :] < left_local[:, None]
    right_keep = positions[None, :] < right_sizes[:, None]
    keep_mask = (left_keep[:, None, :, None] & right_keep[None, :, None, :]).astype(jnp.bfloat16)
    masked = psi * keep_mask
    acting_count = left_ops.shape[0] // 2
    order = jnp.argsort(1 - term_blocks, axis=0, stable=True)[:acting_count]
    ids_local = lax.dynamic_slice_in_dim(order, left_first, sectors_here, 1)
    sector_index = lax.broadcasted_iota(jnp.int32, (acting_count, sectors_here), 1)
    picked = left_ops[ids_local, sector_index]
    applied = jnp.einsum(
        "kaim,abmj->kabij", picked, masked, preferred_element_type=jnp.float32
    ).astype(jnp.bfloat16)
    arrived = lax.all_to_all(applied, "blk", split_axis=2, concat_axis=1, tiled=True)
    right_picked = right_ops[order]
    partial_value = jnp.einsum(
        "kabij,kablj->bail", arrived, right_picked, preferred_element_type=jnp.float32
    )
    summed = lax.psum_scatter(
        partial_value.astype(jnp.bfloat16), "op", scatter_dimension=1, tiled=True
    ).astype(jnp.float32)
    row_count = summed.shape[1]
    op_first = lax.axis_index("op") * row_count
    left_share = lax.dynamic_slice_in_dim(left_sizes, op_first, row_count)
    right_local = lax.dynamic_slice_in_dim(right_sizes, left_first, sectors_here)
    rows_keep = positions[None, :] < left_share[:, None]
    cols_keep = positions[None, :] < right_local[:, None]
    out_keep = (cols_keep[:, None, None, :] & rows_keep[None, :, :, None]).astype(jnp.float32)
    return (summed * out_keep).astype(jnp.bfloat16)


def solution(mesh):
    in_specs = (
        P(("parts", "blk"), None, None, None),
        P(("parts", "op"), "blk", None, None),
        P(("parts", "op"), "blk", None, None),
        P(("parts", "op"), None),
        P("parts"),
        P("parts"),
    )
    out_specs = P(("parts", "blk"), "op", None, None)
    nz, no = mesh.shape["blk"], mesh.shape["op"]
    body = shards if nz == no == 4 else wide_shards
    return jax.shard_map(body, mesh=mesh, in_specs=in_specs, out_specs=out_specs, check_vma=False)
```

profile of v0, /device:TPU:0, one launch (start us, length us, event | category | flops | bytes accessed | tf_op | source)
XLA Modules:
  0.0 33.0 jit_solution(2537140377301137428)
XLA Ops:
  0.0 2.6 %pack.1 = (bf16[528,128]{1,0:T(8,128)(2,1)}, bf16[2,128,128]{2,1,0:T(8,128)(2,1)}, bf16[2,2,128,128]{3,2,1,0:T(8,128)(2,1)}) custom-call(s32[4,8]{1,0:T(4,128)} %blocks_ref.3, bf16[2,8,128,128]{3,2,1,0:T(8,128)(2,1)} %rest_0_.1, bf16[4,2,128,128]{3,2,1,0:T(8,128)(2,1)} %rest_1_.1), custom_call_target="tpu_custom_call" | custom-call | tf_op jit(solution)/shard_map/pack/pallas_call | solution.py:194
  2.6 0.0 copy-start.4
  2.7 0.5 %collective-permute-start.4 = (bf16[4,2,128,128]{3,2,1,0:T(8,128)(2,1)}, bf16[4,2,128,128]{3,2,1,0:T(8,128)(2,1)S(1)}, u32[]{:S(2)}, u32[]{:S(2)}) collective-permute-start(bf16[4,2,128,128]{3,2,1,0:T(8,128)(2,1)} %rest_4_.3), channel_id=1, source_target_pairs={{0,1},{1,0},{2,3},{3,2},{4,5},{5,4},{6,7},{7,6},{8,9},{9,8},{10,11... | collective-permute-start | bytes 786440 | tf_op jit(solution)/shard_map/ppermute | solution.py:176
  3.2 3.7 %collective-permute-start.5 = (bf16[2,128,128]{2,1,0:T(8,128)(2,1)}, bf16[2,128,128]{2,1,0:T(8,128)(2,1)S(1)}, u32[]{:S(2)}, u32[]{:S(2)}) collective-permute-start(bf16[2,128,128]{2,1,0:T(8,128)(2,1)} %get-tuple-element.16), channel_id=1, source_target_pairs={{0,8},{1,12},{2,10},{3,14},{4,9},{5,13},{6,11},{7,15},{8,0},{9,4},... | collective-permute-start | bytes 196616 | tf_op jit(solution)/shard_map/ppermute | solution.py:185
  6.9 0.1 collective-permute-start.1
  6.9 2.7 %collective-permute-start.2 = (bf16[528,128]{1,0:T(8,128)(2,1)}, bf16[528,128]{1,0:T(8,128)(2,1)S(1)}, u32[]{:S(2)}, u32[]{:S(2)}) collective-permute-start(bf16[528,128]{1,0:T(8,128)(2,1)} %get-tuple-element.13), channel_id=1, source_target_pairs={{0,4},{1,8},{2,6},{3,10},{4,13},{5,1},{6,15},{7,3},{8,12},{9,0},{1... | collective-permute-start | bytes 405512 | tf_op jit(solution)/shard_map/ppermute | solution.py:185
  9.6 3.1 %collective-permute-start.3 = (bf16[2,2,128,128]{3,2,1,0:T(8,128)(2,1)}, bf16[2,2,128,128]{3,2,1,0:T(8,128)(2,1)S(1)}, u32[]{:S(2)}, u32[]{:S(2)}) collective-permute-start(bf16[2,2,128,128]{3,2,1,0:T(8,128)(2,1)} %get-tuple-element.14), channel_id=1, source_target_pairs={{0,4},{2,6},{5,1},{7,3},{8,12},{10,14},{13,9},{15,11},{16,20},{18,... | collective-permute-start | bytes 393224 | tf_op jit(solution)/shard_map/ppermute | solution.py:185
  12.7 0.1 collective-permute-start
  12.8 4.4 %collective-permute-done.1.rest_3_.rest_0_ = bf16[528,128]{1,0:T(8,128)(2,1)S(1)} collective-permute-done((bf16[528,128]{1,0:T(8,128)(2,1)}, bf16[528,128]{1,0:T(8,128)(2,1)S(1)}, u32[]{:S(2)}, u32[]{:S(2)}) %collective-permute-start.1) | collective-permute-done | bytes 135200 | tf_op jit(solution)/shard_map/ppermute | solution.py:185
  17.2 1.3 %collective-permute-start.7 = (bf16[528,128]{1,0:T(8,128)(2,1)S(1)}, bf16[528,128]{1,0:T(8,128)(2,1)S(1)}, u32[]{:S(2)}, u32[]{:S(2)}) collective-permute-start(bf16[528,128]{1,0:T(8,128)(2,1)S(1)} %collective-permute-done.1.rest_3_.rest_0_), channel_id=1, source_target_pairs={{0,4},{2,6},{5,1},{7,3},{8,12},{10,14},{13,9},{15,11},{16,20},{18,... | collective-permute-start | bytes 405512 | tf_op jit(solution)/shard_map/ppermute | solution.py:185
  18.5 1.3 %collective-permute-start.8 = (bf16[528,128]{1,0:T(8,128)(2,1)S(1)}, bf16[528,128]{1,0:T(8,128)(2,1)S(1)}, u32[]{:S(2)}, u32[]{:S(2)}) collective-permute-start(bf16[528,128]{1,0:T(8,128)(2,1)S(1)} %collective-permute-done.2.rest_4_.rest_1_), channel_id=1, source_target_pairs={{0,4},{2,6},{5,1},{7,3},{8,12},{10,14},{13,9},{15,11},{16,20},{18,... | collective-permute-start | bytes 405512 | tf_op jit(solution)/shard_map/ppermute | solution.py:185
  19.8 1.6 %collective-permute-start.6 = (bf16[2,128,128]{2,1,0:T(8,128)(2,1)S(1)}, bf16[2,128,128]{2,1,0:T(8,128)(2,1)S(1)}, u32[]{:S(2)}, u32[]{:S(2)}) collective-permute-start(bf16[2,128,128]{2,1,0:T(8,128)(2,1)S(1)} %collective-permute-done.5.rest_2_), channel_id=1, source_target_pairs={{0,2},{1,3},{2,0},{3,1},{4,6},{5,7},{6,4},{7,5},{8,10},{9,11},{10,... | collective-permute-start | bytes 196616 | tf_op jit(solution)/shard_map/ppermute | solution.py:176
  21.4 0.0 collective-permute-done.rest_2_
  21.4 0.0 collective-permute-done.4.rest_7_.rest_5_
  21.4 0.0 copy-start.2
  21.4 0.9 %copy-done.2 = bf16[4,2,128,128]{3,2,1,0:T(8,128)(2,1)S(1)} copy-done((bf16[4,2,128,128]{3,2,1,0:T(8,128)(2,1)S(1)}, bf16[4,2,128,128]{3,2,1,0:T(8,128)(2,1)}, u32[]{:S(2)}) %copy-start.2) | copy-done | bytes 262168
  22.4 1.2 %near.1.rest_6_ = f32[2,2,128,128]{3,2,1,0:T(8,128)S(1)} custom-call(s32[8]{0:T(128)S(1)} %copy-done.5, s32[8]{0:T(128)S(1)} %copy-done.6, s32[4,8]{1,0:T(4,128)S(1)} %copy-done.4, bf16[2,8,128,128]{3,2,1,0:T(8,128)(2,1)S(1)} %copy-done, bf16[4,2,128,128]{3,2,1,0:T(8,128)(2,1)S(1)} %copy-done.1, bf16[528,128]{1,0:T(8,128)(2,1)S(1)} %collective-permute-done.rest_2_, ...), custom_call_target="tpu_custom_call" | custom-call | flops 536870912 | bytes 1048576 | tf_op jit(solution)/shard_map/near/pallas_call | solution.py:219
  23.6 0.5 %collective-permute-done.6.rest_3_ = bf16[2,128,128]{2,1,0:T(8,128)(2,1)S(1)} collective-permute-done((bf16[2,128,128]{2,1,0:T(8,128)(2,1)S(1)}, bf16[2,128,128]{2,1,0:T(8,128)(2,1)S(1)}, u32[]{:S(2)}, u32[]{:S(2)}) %collective-permute-start.6) | collective-permute-done | bytes 65568 | tf_op jit(solution)/shard_map/ppermute | solution.py:176
  24.1 1.2 %far_home.1 = (bf16[2,2,128,128]{3,2,1,0:T(8,128)(2,1)S(1)}, f32[2,2,128,128]{3,2,1,0:T(8,128)S(1)}) custom-call(s32[8]{0:T(128)S(1)} %copy-done.5, s32[8]{0:T(128)S(1)} %copy-done.6, bf16[528,128]{1,0:T(8,128)(2,1)S(1)} %collective-permute-done.1.rest_3_.rest_0_, bf16[528,128]{1,0:T(8,128)(2,1)S(1)} %collective-permute-done.2.rest_4_.rest_1_, ...), custom_call_target="tpu_custom_call" | custom-call | flops 536870912 | bytes 1048576 | tf_op jit(solution)/shard_map/far_home/pallas_call | solution.py:219
  25.4 3.4 %collective-permute-start.9 = (bf16[2,2,128,128]{3,2,1,0:T(8,128)(2,1)S(1)}, bf16[2,2,128,128]{3,2,1,0:T(8,128)(2,1)S(1)}, u32[]{:S(2)}, u32[]{:S(2)}) collective-permute-start(bf16[2,2,128,128]{3,2,1,0:T(8,128)(2,1)S(1)} %get-tuple-element.19), channel_id=1, source_target_pairs={{0,2},{2,0},{5,7},{7,5},{8,10},{10,8},{13,15},{15,13},{16,18},{18,... | collective-permute-start | bytes 393224 | tf_op jit(solution)/shard_map/ppermute | solution.py:185
  28.8 0.6 %far_other.1 = (bf16[2,2,128,128]{3,2,1,0:T(8,128)(2,1)S(1)}, f32[2,2,128,128]{3,2,1,0:T(8,128)S(1)}) custom-call(s32[8]{0:T(128)S(1)} %copy-done.5, s32[8]{0:T(128)S(1)} %copy-done.6, bf16[528,128]{1,0:T(8,128)(2,1)S(1)} %collective-permute-done.7.rest_0_, bf16[528,128]{1,0:T(8,128)(2,1)S(1)} %collective-permute-done.8.rest_1_, ...), custom_call_target="tpu_custom_call" | custom-call | flops 536870912 | bytes 1048576 | tf_op jit(solution)/shard_map/far_other/pallas_call | solution.py:219
  29.4 0.7 %collective-permute-start.10 = (bf16[2,2,128,128]{3,2,1,0:T(8,128)(2,1)S(1)}, bf16[2,2,128,128]{3,2,1,0:T(8,128)(2,1)S(1)}, u32[]{:S(2)}, u32[]{:S(2)}) collective-permute-start(bf16[2,2,128,128]{3,2,1,0:T(8,128)(2,1)S(1)} %get-tuple-element.20), channel_id=1, source_target_pairs={{1,3},{3,1},{4,6},{6,4},{9,11},{11,9},{12,14},{14,12},{17,19},{19,... | collective-permute-start | bytes 393224 | tf_op jit(solution)/shard_map/ppermute | solution.py:185
  30.1 2.1 %collective-permute-done.9 = bf16[2,2,128,128]{3,2,1,0:T(8,128)(2,1)S(1)} collective-permute-done((bf16[2,2,128,128]{3,2,1,0:T(8,128)(2,1)S(1)}, bf16[2,2,128,128]{3,2,1,0:T(8,128)(2,1)S(1)}, u32[]{:S(2)}, u32[]{:S(2)}) %collective-permute-start.9) | collective-permute-done | bytes 131104 | tf_op jit(solution)/shard_map/ppermute | solution.py:185
  32.2 0.7 %add_convert_fusion = bf16[2,2,128,128]{3,2,1,0:T(8,128)(2,1)} fusion(f32[2,2,128,128]{3,2,1,0:T(8,128)S(1)} %near.1.rest_6_, f32[2,2,128,128]{3,2,1,0:T(8,128)S(1)} %get-tuple-element.17, f32[2,2,128,128]{3,2,1,0:T(8,128)S(1)} %get-tuple-element.18, bf16[2,2,128,128]{3,2,1,0:T(8,128)(2,1)S(1)} %collective-permute-done.9, ...), kind=kLoop, calls=%fused_computation | loop fusion | flops 393216 | bytes 1179650 | tf_op jit(solution)/shard_map/convert_element_type | solution.py:254
  (17 shorter events, 0.0 us)
Async XLA Ops:
  0.0 21.4 %copy-start = (bf16[2,8,128,128]{3,2,1,0:T(8,128)(2,1)S(1)}, bf16[2,8,128,128]{3,2,1,0:T(8,128)(2,1)}, u32[]{:S(2)}) copy-start(bf16[2,8,128,128]{3,2,1,0:T(8,128)(2,1)} %rest_0_.1) | copy-start | bytes 1572868
  0.0 21.4 %copy-start.1 = (bf16[4,2,128,128]{3,2,1,0:T(8,128)(2,1)S(1)}, bf16[4,2,128,128]{3,2,1,0:T(8,128)(2,1)}, u32[]{:S(2)}) copy-start(bf16[4,2,128,128]{3,2,1,0:T(8,128)(2,1)} %rest_1_.1) | copy-start | bytes 786436
  2.6 18.8 %copy-start.4 = (s32[4,8]{1,0:T(4,128)S(1)}, s32[4,8]{1,0:T(4,128)}, u32[]{:S(2)}) copy-start(s32[4,8]{1,0:T(4,128)} %blocks_ref.3) | copy-start | bytes 388
  2.7 18.7 %collective-permute-start.4 = (bf16[4,2,128,128]{3,2,1,0:T(8,128)(2,1)}, bf16[4,2,128,128]{3,2,1,0:T(8,128)(2,1)S(1)}, u32[]{:S(2)}, u32[]{:S(2)}) collective-permute-start(bf16[4,2,128,128]{3,2,1,0:T(8,128)(2,1)} %rest_4_.3), channel_id=1, source_target_pairs={{0,1},{1,0},{2,3},{3,2},{4,5},{5,4},{6,7},{7,6},{8,9},{9,8},{10,11... | collective-permute-start | bytes 786440 | tf_op jit(solution)/shard_map/ppermute | solution.py:176
  3.2 18.2 %copy-start.5 = (s32[8]{0:T(128)S(1)}, s32[8]{0:T(128)}, u32[]{:S(2)}) copy-start(s32[8]{0:T(128)} %lsize_ref.5) | copy-start | bytes 100
  3.2 18.2 %copy-start.6 = (s32[8]{0:T(128)S(1)}, s32[8]{0:T(128)}, u32[]{:S(2)}) copy-start(s32[8]{0:T(128)} %rsize_ref.5) | copy-start | bytes 100
  3.2 9.6 %collective-permute-start.5 = (bf16[2,128,128]{2,1,0:T(8,128)(2,1)}, bf16[2,128,128]{2,1,0:T(8,128)(2,1)S(1)}, u32[]{:S(2)}, u32[]{:S(2)}) collective-permute-start(bf16[2,128,128]{2,1,0:T(8,128)(2,1)} %get-tuple-element.16), channel_id=1, source_target_pairs={{0,8},{1,12},{2,10},{3,14},{4,9},{5,13},{6,11},{7,15},{8,0},{9,4},... | collective-permute-start | bytes 196616 | tf_op jit(solution)/shard_map/ppermute | solution.py:185
  6.9 10.3 %collective-permute-start.1 = (bf16[528,128]{1,0:T(8,128)(2,1)}, bf16[528,128]{1,0:T(8,128)(2,1)S(1)}, u32[]{:S(2)}, u32[]{:S(2)}) collective-permute-start(bf16[528,128]{1,0:T(8,128)(2,1)} %get-tuple-element.13), channel_id=1, source_target_pairs={{0,8},{1,4},{2,10},{3,6},{4,1},{5,13},{6,3},{7,15},{8,0},{9,12},{1... | collective-permute-start | bytes 405512 | tf_op jit(solution)/shard_map/ppermute | solution.py:185
  6.9 11.5 %collective-permute-start.2 = (bf16[528,128]{1,0:T(8,128)(2,1)}, bf16[528,128]{1,0:T(8,128)(2,1)S(1)}, u32[]{:S(2)}, u32[]{:S(2)}) collective-permute-start(bf16[528,128]{1,0:T(8,128)(2,1)} %get-tuple-element.13), channel_id=1, source_target_pairs={{0,4},{1,8},{2,6},{3,10},{4,13},{5,1},{6,15},{7,3},{8,12},{9,0},{1... | collective-permute-start | bytes 405512 | tf_op jit(solution)/shard_map/ppermute | solution.py:185
  9.6 10.2 %collective-permute-start.3 = (bf16[2,2,128,128]{3,2,1,0:T(8,128)(2,1)}, bf16[2,2,128,128]{3,2,1,0:T(8,128)(2,1)S(1)}, u32[]{:S(2)}, u32[]{:S(2)}) collective-permute-start(bf16[2,2,128,128]{3,2,1,0:T(8,128)(2,1)} %get-tuple-element.14), channel_id=1, source_target_pairs={{0,4},{2,6},{5,1},{7,3},{8,12},{10,14},{13,9},{15,11},{16,20},{18,... | collective-permute-start | bytes 393224 | tf_op jit(solution)/shard_map/ppermute | solution.py:185
  12.7 8.6 %collective-permute-start = (bf16[528,128]{1,0:T(8,128)(2,1)}, bf16[528,128]{1,0:T(8,128)(2,1)S(1)}, u32[]{:S(2)}, u32[]{:S(2)}) collective-permute-start(bf16[528,128]{1,0:T(8,128)(2,1)} %get-tuple-element.13), channel_id=1, source_target_pairs={{0,1},{1,0},{2,3},{3,2},{4,5},{5,4},{6,7},{7,6},{8,9},{9,8},{10,11... | collective-permute-start | bytes 405512 | tf_op jit(solution)/shard_map/ppermute | solution.py:176
  17.2 11.6 %collective-permute-start.7 = (bf16[528,128]{1,0:T(8,128)(2,1)S(1)}, bf16[528,128]{1,0:T(8,128)(2,1)S(1)}, u32[]{:S(2)}, u32[]{:S(2)}) collective-permute-start(bf16[528,128]{1,0:T(8,128)(2,1)S(1)} %collective-permute-done.1.rest_3_.rest_0_), channel_id=1, source_target_pairs={{0,4},{2,6},{5,1},{7,3},{8,12},{10,14},{13,9},{15,11},{16,20},{18,... | collective-permute-start | bytes 405512 | tf_op jit(solution)/shard_map/ppermute | solution.py:185
  18.5 10.3 %collective-permute-start.8 = (bf16[528,128]{1,0:T(8,128)(2,1)S(1)}, bf16[528,128]{1,0:T(8,128)(2,1)S(1)}, u32[]{:S(2)}, u32[]{:S(2)}) collective-permute-start(bf16[528,128]{1,0:T(8,128)(2,1)S(1)} %collective-permute-done.2.rest_4_.rest_1_), channel_id=1, source_target_pairs={{0,4},{2,6},{5,1},{7,3},{8,12},{10,14},{13,9},{15,11},{16,20},{18,... | collective-permute-start | bytes 405512 | tf_op jit(solution)/shard_map/ppermute | solution.py:185
  19.8 4.3 %collective-permute-start.6 = (bf16[2,128,128]{2,1,0:T(8,128)(2,1)S(1)}, bf16[2,128,128]{2,1,0:T(8,128)(2,1)S(1)}, u32[]{:S(2)}, u32[]{:S(2)}) collective-permute-start(bf16[2,128,128]{2,1,0:T(8,128)(2,1)S(1)} %collective-permute-done.5.rest_2_), channel_id=1, source_target_pairs={{0,2},{1,3},{2,0},{3,1},{4,6},{5,7},{6,4},{7,5},{8,10},{9,11},{10,... | collective-permute-start | bytes 196616 | tf_op jit(solution)/shard_map/ppermute | solution.py:176
  21.4 1.0 %copy-start.2 = (bf16[4,2,128,128]{3,2,1,0:T(8,128)(2,1)S(1)}, bf16[4,2,128,128]{3,2,1,0:T(8,128)(2,1)}, u32[]{:S(2)}) copy-start(bf16[4,2,128,128]{3,2,1,0:T(8,128)(2,1)} %rest_4_.3) | copy-start | bytes 786436
  22.4 1.8 %copy-start.3 = (bf16[4,2,128,128]{3,2,1,0:T(8,128)(2,1)S(1)}, bf16[4,2,128,128]{3,2,1,0:T(8,128)(2,1)}, u32[]{:S(2)}) copy-start(bf16[4,2,128,128]{3,2,1,0:T(8,128)(2,1)} %rest_4_.3) | copy-start | bytes 786436
  25.4 6.9 %collective-permute-start.9 = (bf16[2,2,128,128]{3,2,1,0:T(8,128)(2,1)S(1)}, bf16[2,2,128,128]{3,2,1,0:T(8,128)(2,1)S(1)}, u32[]{:S(2)}, u32[]{:S(2)}) collective-permute-start(bf16[2,2,128,128]{3,2,1,0:T(8,128)(2,1)S(1)} %get-tuple-element.19), channel_id=1, source_target_pairs={{0,2},{2,0},{5,7},{7,5},{8,10},{10,8},{13,15},{15,13},{16,18},{18,... | collective-permute-start | bytes 393224 | tf_op jit(solution)/shard_map/ppermute | solution.py:185
  29.4 2.9 %collective-permute-start.10 = (bf16[2,2,128,128]{3,2,1,0:T(8,128)(2,1)S(1)}, bf16[2,2,128,128]{3,2,1,0:T(8,128)(2,1)S(1)}, u32[]{:S(2)}, u32[]{:S(2)}) collective-permute-start(bf16[2,2,128,128]{3,2,1,0:T(8,128)(2,1)S(1)} %get-tuple-element.20), channel_id=1, source_target_pairs={{1,3},{3,1},{4,6},{6,4},{9,11},{11,9},{12,14},{14,12},{17,19},{19,... | collective-permute-start | bytes 393224 | tf_op jit(solution)/shard_map/ppermute | solution.py:185
where the time goes:
time: 33.2 us; the launch traced here: 33 us
  starting transfers between devices  18.3 us (55%)
  waiting for transfers between devices  7.04 us (21%)
  Pallas kernels  5.67 us (17%)
  local copies, waits for them, and re-layouts  0.97 us (3%)
  other arithmetic  0.72 us (2%)
    ppermute x8, starting transfers between devices, over_both(): return lax.ppermute(array, ('blk', 'op'), pairs)  16.2 us
    ppermute x8, waiting for transfers between devices, over_both(): return lax.ppermute(array, ('blk', 'op'), pairs)  6.53 us
    pallas_call x3, Pallas kernels, apply(): pl.pallas_call(kernel, out_shape=[jax.ShapeDtypeStruct(out_shape, dtype)...  3.04 us
    pallas_call x1, Pallas kernels, shards(): pl.pallas_call(pack_kernel, out_shape=[block((2 * sectors * tile + ID_ROW...  2.63 us
    ppermute x3, starting transfers between devices, over_op(): return lax.ppermute(array, 'op', [(o, o ^ step) for o in range(n)])  2.15 us
    unnamed x14, local copies, waits for them, and re-layouts  0.97 us
    convert_element_type x1, other arithmetic, shards(): return (kept + arrived.astype(jnp.float32)).astype(jnp.bfloat16)  0.72 us
  transfers between devices with their start and end apart: 11, of which 3 were waited for; matrix products, arithmetic and copies ran while one was open for 0% of the time, Pallas kernels for 9%

commit v1 on v0

v1 whole, which is shorter than its diff:
```python
import functools

import jax
import jax.numpy as jnp
from jax import lax
from jax.experimental import pallas as pl
from jax.experimental.pallas import tpu as pltpu
from jax.sharding import PartitionSpec as P

ANY = pl.BlockSpec(memory_space=pl.ANY)
SMEM = pl.BlockSpec(memory_space=pltpu.SMEM)
VMEM = pl.BlockSpec(memory_space=pltpu.VMEM)
PARAMS = pltpu.CompilerParams(vmem_limit_bytes=32 * 1024 * 1024)
ID_ROWS = 16


def acting_terms(blocks_ref, sector):
    first = jnp.int32(0)
    second = jnp.int32(0)
    for term in reversed(range(blocks_ref.shape[0])):
        acts = blocks_ref[term, sector] > 0
        second = jnp.where(acts, first, second)
        first = jnp.where(acts, term, first)
    return first, second


def place():
    op = lax.axis_index("op")
    return lax.axis_index("blk"), lax.shift_right_logical(op, 1), jnp.bitwise_and(op, 1)


def is_home():
    z, _, c = place()
    return c == jnp.bitwise_and(z, 1)


def pack_kernel(blocks_ref, psi_ref, left_ref, left_out, side_out, far_out, sem):
    z, _, _ = place()
    sectors, tile = psi_ref.shape[0], psi_ref.shape[-1]
    count = 2 * sectors
    row = lax.broadcasted_iota(jnp.int32, (ID_ROWS, tile), 0)
    ids = jnp.zeros((ID_ROWS, tile), jnp.float32)
    picked = []
    for local in range(sectors):
        for term in acting_terms(blocks_ref, z * sectors + local):
            ids = jnp.where(row == len(picked), term.astype(jnp.float32), ids)
            picked.append(left_ref.at[term, local])
    near = jnp.bitwise_xor(z, 1) * sectors
    asked = [psi_ref.at[a, near + b] for a in range(sectors) for b in range(sectors)]

    def copies(sources, out, first):
        return [
            pltpu.make_async_copy(source, out.at[pl.ds(spot * tile, tile)], sem.at[first + spot])
            for spot, source in enumerate(sources)
        ]

    far = pl.ds(jnp.bitwise_xor(z, jnp.where(is_home(), 2, 3)) * sectors, sectors)
    plain = copies(picked, left_out, 0)
    plain.append(pltpu.make_async_copy(psi_ref.at[:, far], far_out, sem.at[2 * count]))
    for copy in plain:
        copy.start()
    for at_home, sources in ((True, asked), (False, picked)):

        @pl.when(is_home() == at_home)
        def _(sources=sources):
            for copy in copies(sources, side_out, count):
                copy.start()

    for out in (left_out, side_out):
        out[pl.ds(count * tile, ID_ROWS)] = ids.astype(jnp.bfloat16)
    for copy in plain + copies(picked, side_out, count):
        copy.wait()


def keep_mask(z, distance, sizes, a, b, sectors, tile):
    lsize_ref, rsize_ref = sizes
    rows = lax.broadcasted_iota(jnp.int32, (tile, tile), 0)
    lanes = lax.broadcasted_iota(jnp.int32, (tile, tile), 1)
    height = lsize_ref[jnp.bitwise_xor(z, distance) * sectors + a]
    return (rows < height) & (lanes < rsize_ref[z * sectors + b])


def wide_psi(z, distance, sizes, a, blocks):
    tile = blocks[0].shape[-1]
    cut = []
    for b, block in enumerate(blocks):
        keep = keep_mask(z, distance, sizes, a, b, len(blocks), tile)
        cut.append(jnp.where(keep, block.astype(jnp.float32), 0.0).astype(jnp.bfloat16))
    return jnp.concatenate(cut, axis=1)


def partial_sums(z, distance, sizes, sectors, psi, lefts, rights, store):
    for a in range(sectors):
        wide = psi(a)
        tile = wide.shape[0]
        applied = []
        for left in lefts:
            both = jnp.dot(left(a), wide, preferred_element_type=jnp.float32).astype(jnp.bfloat16)
            applied += [both[:tile], both[tile:]]
        for b in range(sectors):
            picked = [right(a, slot, b) for right in rights for slot in range(2)]
            column = [part[:, b * tile : (b + 1) * tile] for part in applied]
            total = lax.dot_general(
                jnp.concatenate(column, axis=1),
                jnp.concatenate(picked, axis=1),
                (((1,), (1,)), ((), ())),
                preferred_element_type=jnp.float32,
            )
            keep = keep_mask(z, distance, sizes, a, b, sectors, tile)
            store(b, a, jnp.where(keep, total, 0.0))


def message(ref, right_ref):
    terms, sectors, tile = right_ref.shape[0], right_ref.shape[1], right_ref.shape[-1]
    ids = ref[pl.ds(2 * sectors * tile, ID_ROWS)].astype(jnp.float32)

    def left(a):
        return ref[pl.ds(2 * a * tile, 2 * tile)]

    def right(a, slot, b):
        spot = 2 * a + slot
        term = jnp.broadcast_to(ids[spot : spot + 1], (tile, tile))
        block = right_ref[0, b].astype(jnp.float32)
        for t in range(1, terms):
            block = jnp.where(term == t, right_ref[t, b].astype(jnp.float32), block)
        return block.astype(jnp.bfloat16)

    return left, right


def near_kernel(lsize_ref, rsize_ref, blocks_ref, *rest):
    psi_ref, left_ref, side, direct_a, direct_b, psi_far, right_hbm, right_other = rest[:8]
    out_ref, wide_ref, right_own, sem = rest[8:]
    z, _, _ = place()
    sectors, tile = out_ref.shape[0], out_ref.shape[-1]
    sizes = (lsize_ref, rsize_ref)
    copy = pltpu.make_async_copy(right_hbm, right_own, sem)
    copy.start()
    distance = jnp.where(is_home(), 2, 3)
    for a in range(sectors):
        wide_ref[a] = wide_psi(z, distance, sizes, a, [psi_far[a, b] for b in range(sectors)])
    copy.wait()

    def store(b, a, total):
        out_ref[b, a] = total

    @pl.when(is_home())
    def _():
        terms = [acting_terms(blocks_ref, z * sectors + a) for a in range(sectors)]
        left, right = message(side, right_other)

        def psi(a):
            return wide_psi(z, 0, sizes, a, [psi_ref[a, z * sectors + b] for b in range(sectors)])

        partial_sums(
            z, 0, sizes, sectors, psi,
            [lambda a: jnp.concatenate([left_ref[term, a] for term in terms[a]], axis=0), left],
            [lambda a, slot, b: right_own[terms[a][slot], b], right],
            store,
        )

    @pl.when(jnp.logical_not(is_home()))
    def _():
        lefts, rights = zip(message(direct_b, right_own), message(direct_a, right_other))

        def psi(a):
            spots = [pl.ds((sectors * a + b) * tile, tile) for b in range(sectors)]
            return wide_psi(z, 1, sizes, a, [side[spot] for spot in spots])

        partial_sums(z, 1, sizes, sectors, psi, lefts, rights, store)


def far_kernel(lsize_ref, rsize_ref, *rest):
    direct_a, direct_b, passed_a, passed_b, wide_ref, right_own, right_other, near_ref = rest[:8]
    sent_ref, out_ref = rest[8:]
    z, x, _ = place()
    sectors = out_ref.shape[0]
    far_leaves = lax.shift_right_logical(z, 1) == x

    def store_sent(b, a, total):
        sent_ref[b, a] = total.astype(sent_ref.dtype)

    def store_kept(b, a, total):
        out_ref[b, a] = total
        sent_ref[b, a] = near_ref[b, a].astype(sent_ref.dtype)

    for leaves, store in ((True, store_sent), (False, store_kept)):
        for at_home, distance, first, second in (
            (True, 2, direct_a, direct_b),
            (False, 3, passed_a, passed_b),
        ):

            @pl.when((is_home() == at_home) & (far_leaves == leaves))
            def _(store=store, distance=distance, first=first, second=second):
                lefts, rights = zip(message(first, right_own), message(second, right_other))
                sizes = (lsize_ref, rsize_ref)
                partial_sums(
                    z, distance, sizes, sectors, lambda a: wide_ref[a], lefts, rights, store
                )


def shards(psi, left_ops, right_ops, term_blocks, left_sizes, right_sizes):
    n = 4
    sectors, tile = psi.shape[0], psi.shape[-1]
    block = functools.partial(jax.ShapeDtypeStruct, dtype=jnp.bfloat16)
    out_shape = (sectors, sectors, tile, tile)
    message_shape = (2 * sectors * tile + ID_ROWS, tile)

    def over_op(array, step):
        return lax.ppermute(array, "op", [(o, o ^ step) for o in range(n)])

    def over_z(array, home_step, other_step):
        pairs = []
        for z in range(n):
            for o in range(n):
                step = home_step if o & 1 == z & 1 else other_step
                pairs.append((z * n + o, (z ^ step) * n + (o & 2) + (z & 1)))
        return lax.ppermute(array, ("blk", "op"), pairs)

    psi_hbm, left_hbm, right_hbm, blocks_hbm = [
        pltpu.with_memory_space_constraint(array, pltpu.HBM)
        for array in (psi, left_ops, right_ops, term_blocks)
    ]
    left_sent, side_sent, far_sent = pl.pallas_call(
        pack_kernel,
        out_shape=[block(message_shape), block(message_shape), block(out_shape)],
        in_specs=[SMEM, ANY, ANY],
        out_specs=[VMEM] * 3,
        scratch_shapes=[pltpu.SemaphoreType.DMA((4 * sectors + 1,))],
        compiler_params=PARAMS,
        name="pack",
    )(blocks_hbm, psi_hbm, left_hbm)
    direct_a = over_z(left_sent, 2, 1)
    direct_b = over_z(left_sent, 1, 2)
    psi_far = over_z(far_sent, 2, 3)
    side = over_z(side_sent, 1, 0)
    passed_a = over_z(direct_a, 1, 0)
    passed_b = over_z(direct_b, 1, 0)
    held, _ = lax.optimization_barrier((right_ops, left_sent))
    right_other = over_op(held, 1)

    def apply(kernel, name, outs, scalars, operands, scratch):
        return pl.pallas_call(
            kernel,
            out_shape=outs,
            in_specs=[SMEM] * len(scalars) + [spec for _, spec in operands],
            out_specs=[VMEM] * len(outs),
            scratch_shapes=scratch,
            compiler_params=PARAMS,
            cost_estimate=pl.CostEstimate(
                flops=64 * tile**3 * sectors**2, bytes_accessed=2**20, transcendentals=0
            ),
            name=name,
        )(*scalars, *[array for array, _ in operands])

    sizes = (left_sizes, right_sizes)
    total = jax.ShapeDtypeStruct(out_shape, jnp.float32)
    inside = [psi, left_ops, side, direct_a, direct_b, psi_far]
    near, wide, right_own = apply(
        near_kernel, "near",
        [total, block((sectors, tile, sectors * tile)), block(right_ops.shape)],
        sizes + (term_blocks,),
        [(array, VMEM) for array in inside] + [(right_hbm, ANY), (right_other, VMEM)],
        [pltpu.SemaphoreType.DMA(())],
    )
    inside = [direct_a, direct_b, passed_a, passed_b, wide, right_own, right_other, near]
    sent, far = apply(
        far_kernel, "far", [block(out_shape), total], sizes,
        [(array, VMEM) for array in inside], [],
    )
    arrived = over_op(sent, 2)
    kept = jnp.where(lax.axis_index("blk") // 2 == lax.axis_index("op") // 2, near, far)
    return (kept + arrived.astype(jnp.float32)).astype(jnp.bfloat16)


def wide_shards(psi, left_ops, right_ops, term_blocks, left_sizes, right_sizes):
    sectors_here = psi.shape[0]
    tile_size = psi.shape[2]
    left_first = lax.axis_index("blk") * sectors_here
    positions = lax.broadcasted_iota(jnp.int32, (tile_size,), 0)
    left_local = lax.dynamic_slice_in_dim(left_sizes, left_first, sectors_here)
    left_keep = positions[None, :] < left_local[:, None]
    right_keep = positions[None, :] < right_sizes[:, None]
    keep_mask = (left_keep[:, None, :, None] & right_keep[None, :, None, :]).astype(jnp.bfloat16)
    masked = psi * keep_mask
    acting_count = left_ops.shape[0] // 2
    order = jnp.argsort(1 - term_blocks, axis=0, stable=True)[:acting_count]
    ids_local = lax.dynamic_slice_in_dim(order, left_first, sectors_here, 1)
    sector_index = lax.broadcasted_iota(jnp.int32, (acting_count, sectors_here), 1)
    picked = left_ops[ids_local, sector_index]
    applied = jnp.einsum(
        "kaim,abmj->kabij", picked, masked, preferred_element_type=jnp.float32
    ).astype(jnp.bfloat16)
    arrived = lax.all_to_all(applied, "blk", split_axis=2, concat_axis=1, tiled=True)
    right_picked = right_ops[order]
    partial_value = jnp.einsum(
        "kabij,kablj->bail", arrived, right_picked, preferred_element_type=jnp.float32
    )
    summed = lax.psum_scatter(
        partial_value.astype(jnp.bfloat16), "op", scatter_dimension=1, tiled=True
    ).astype(jnp.float32)
    row_count = summed.shape[1]
    op_first = lax.axis_index("op") * row_count
    left_share = lax.dynamic_slice_in_dim(left_sizes, op_first, row_count)
    right_local = lax.dynamic_slice_in_dim(right_sizes, left_first, sectors_here)
    rows_keep = positions[None, :] < left_share[:, None]
    cols_keep = positions[None, :] < right_local[:, None]
    out_keep = (cols_keep[:, None, None, :] & rows_keep[None, :, :, None]).astype(jnp.float32)
    return (summed * out_keep).astype(jnp.bfloat16)


def solution(mesh):
    in_specs = (
        P(("parts", "blk"), None, None, None),
        P(("parts", "op"), "blk", None, None),
        P(("parts", "op"), "blk", None, None),
        P(("parts", "op"), None),
        P("parts"),
        P("parts"),
    )
    out_specs = P(("parts", "blk"), "op", None, None)
    nz, no = mesh.shape["blk"], mesh.shape["op"]
    body = shards if nz == no == 4 else wide_shards
    return jax.shard_map(body, mesh=mesh, in_specs=in_specs, out_specs=out_specs, check_vma=False)
```

time: 33.2 us -> 28.6 us (0.86)
  starting transfers between devices: 18.3 us -> 13.3 us
  waiting for transfers between devices: 7.04 us -> 9 us
  local copies, waits for them, and re-layouts: 0.97 us -> 0.02 us
  Pallas kernels: 5.67 us -> 5.32 us
    ppermute x8 -> x6, starting transfers between devices: 16.2 us -> 11.2 us  [over_z(): return lax.ppermute(array, ('blk', 'op'), pairs)]
    ppermute x3 -> x2, waiting for transfers between devices: 0.51 us -> 3.46 us  [over_op(): return lax.ppermute(array, 'op', [(o, o ^ step) for o in range(n)])]
    ppermute x8 -> x6, waiting for transfers between devices: 6.53 us -> 5.55 us  [over_z(): return lax.ppermute(array, ('blk', 'op'), pairs)]
    unnamed x14 -> x10, local copies, waits for them, and re-layouts: 0.97 us -> 0.02 us
    pallas_call x4 -> x3, Pallas kernels: 5.67 us -> 5.32 us  [the longest x2 3.41 us: apply(): pl.pallas_call(kernel, out_shape=outs, in_specs=[SMEM] * len(scalars) + [...]
    ppermute x3 -> x2, starting transfers between devices: 2.15 us -> 2.1 us  [over_op(): return lax.ppermute(array, 'op', [(o, o ^ step) for o in range(n)])]
  transfers between devices with their start and end apart: 11 -> 8, of which waited for: 3 -> 4; matrix products, arithmetic and copies ran while one was open for 0% -> 0% of each run, Pallas kernels for 9% -> 8%
where the time goes in v1:
time: 28.6 us; the launch traced here: 28.4 us
  starting transfers between devices  13.3 us (47%)
  waiting for transfers between devices  9 us (31%)
  Pallas kernels  5.32 us (19%)
  other arithmetic  0.69 us (2%)
    ppermute x6, starting transfers between devices, over_z(): return lax.ppermute(array, ('blk', 'op'), pairs)  11.2 us
    ppermute x6, waiting for transfers between devices, over_z(): return lax.ppermute(array, ('blk', 'op'), pairs)  5.55 us
    ppermute x2, waiting for transfers between devices, over_op(): return lax.ppermute(array, 'op', [(o, o ^ step) for o in range(n)])  3.46 us
    pallas_call x2, Pallas kernels, apply(): pl.pallas_call(kernel, out_shape=outs, in_specs=[SMEM] * len(scalars) + [...  3.41 us
    ppermute x2, starting transfers between devices, over_op(): return lax.ppermute(array, 'op', [(o, o ^ step) for o in range(n)])  2.1 us
    pallas_call x1, Pallas kernels, shards(): pl.pallas_call(pack_kernel, out_shape=[block(message_shape), block(messag...  1.91 us
    convert_element_type x1, other arithmetic, shards(): return (kept + arrived.astype(jnp.float32)).astype(jnp.bfloat16)  0.69 us
  transfers between devices with their start and end apart: 8, of which 4 were waited for; matrix products, arithmetic and copies ran while one was open for 0% of the time, Pallas kernels for 8%

profile of v1, /device:TPU:0, one launch (start us, length us, event | category | flops | bytes accessed | tf_op | source)
XLA Modules:
  0.0 28.4 jit_solution(833322773819781234)
XLA Ops:
  0.0 1.9 %pack.1 = (bf16[528,128]{1,0:T(8,128)(2,1)S(1)}, bf16[528,128]{1,0:T(8,128)(2,1)S(1)}, bf16[2,2,128,128]{3,2,1,0:T(8,128)(2,1)S(1)}) custom-call(s32[4,8]{1,0:T(4,128)} %blocks_ref.3, bf16[2,8,128,128]{3,2,1,0:T(8,128)(2,1)} %rest_0_.1, bf16[4,2,128,128]{3,2,1,0:T(8,128)(2,1)} %rest_1_.1), custom_call_target="tpu_custom_call" | custom-call | tf_op jit(solution)/shard_map/pack/pallas_call | solution.py:224
  1.9 0.0 copy-start.2
  1.9 0.5 %collective-permute-start.4 = (bf16[4,2,128,128]{3,2,1,0:T(8,128)(2,1)}, bf16[4,2,128,128]{3,2,1,0:T(8,128)(2,1)S(1)}, u32[]{:S(2)}, u32[]{:S(2)}) collective-permute-start(bf16[4,2,128,128]{3,2,1,0:T(8,128)(2,1)} %rest_6_.1), channel_id=1, source_target_pairs={{0,1},{1,0},{2,3},{3,2},{4,5},{5,4},{6,7},{7,6},{8,9},{9,8},{10,11... | collective-permute-start | bytes 786440 | tf_op jit(solution)/shard_map/ppermute | solution.py:210
  2.5 3.7 %collective-permute-start.1 = (bf16[528,128]{1,0:T(8,128)(2,1)S(1)}, bf16[528,128]{1,0:T(8,128)(2,1)S(1)}, u32[]{:S(2)}, u32[]{:S(2)}) collective-permute-start(bf16[528,128]{1,0:T(8,128)(2,1)S(1)} %get-tuple-element.15), channel_id=1, source_target_pairs={{0,8},{1,4},{2,10},{3,6},{4,1},{5,13},{6,3},{7,15},{8,0},{9,12},{1... | collective-permute-start | bytes 405512 | tf_op jit(solution)/shard_map/ppermute | solution.py:218
  6.1 0.0 collective-permute-start.2
  6.1 1.7 %collective-permute-start = (bf16[528,128]{1,0:T(8,128)(2,1)S(1)}, bf16[528,128]{1,0:T(8,128)(2,1)S(1)}, u32[]{:S(2)}, u32[]{:S(2)}) collective-permute-start(bf16[528,128]{1,0:T(8,128)(2,1)S(1)} %get-tuple-element.14), channel_id=1, source_target_pairs={{0,4},{1,0},{2,6},{3,2},{4,5},{5,1},{6,7},{7,3},{8,12},{9,8},{10,1... | collective-permute-start | bytes 405512 | tf_op jit(solution)/shard_map/ppermute | solution.py:218
  7.8 2.6 %collective-permute-start.3 = (bf16[2,2,128,128]{3,2,1,0:T(8,128)(2,1)S(1)}, bf16[2,2,128,128]{3,2,1,0:T(8,128)(2,1)S(1)}, u32[]{:S(2)}, u32[]{:S(2)}) collective-permute-start(bf16[2,2,128,128]{3,2,1,0:T(8,128)(2,1)S(1)} %get-tuple-element.16), channel_id=1, source_target_pairs={{0,8},{1,12},{2,10},{3,14},{4,9},{5,13},{6,11},{7,15},{8,0},{9,4},... | collective-permute-start | bytes 393224 | tf_op jit(solution)/shard_map/ppermute | solution.py:218
  10.4 0.3 collective-permute-done.1.rest_3_.rest_0_
  10.6 0.0 collective-permute-start.5
  10.7 1.9 %collective-permute-done.2.rest_4_.rest_1_ = bf16[528,128]{1,0:T(8,128)(2,1)S(1)} collective-permute-done((bf16[528,128]{1,0:T(8,128)(2,1)S(1)}, bf16[528,128]{1,0:T(8,128)(2,1)S(1)}, u32[]{:S(2)}, u32[]{:S(2)}) %collective-permute-start.2) | collective-permute-done | bytes 135200 | tf_op jit(solution)/shard_map/ppermute | solution.py:218
  12.5 3.3 %collective-permute-start.6 = (bf16[528,128]{1,0:T(8,128)(2,1)S(1)}, bf16[528,128]{1,0:T(8,128)(2,1)S(1)}, u32[]{:S(2)}, u32[]{:S(2)}) collective-permute-start(bf16[528,128]{1,0:T(8,128)(2,1)S(1)} %collective-permute-done.2.rest_4_.rest_1_), channel_id=1, source_target_pairs={{0,4},{1,0},{2,6},{3,2},{4,5},{5,1},{6,7},{7,3},{8,12},{9,8},{10,1... | collective-permute-start | bytes 405512 | tf_op jit(solution)/shard_map/ppermute | solution.py:218
  15.8 3.4 %collective-permute-done.3.rest_5_ = bf16[2,2,128,128]{3,2,1,0:T(8,128)(2,1)S(1)} collective-permute-done((bf16[2,2,128,128]{3,2,1,0:T(8,128)(2,1)S(1)}, bf16[2,2,128,128]{3,2,1,0:T(8,128)(2,1)S(1)}, u32[]{:S(2)}, u32[]{:S(2)}) %collective-permute-start.3) | collective-permute-done | bytes 131104 | tf_op jit(solution)/shard_map/ppermute | solution.py:218
  19.2 0.0 collective-permute-done.rest_2_
  19.2 0.0 collective-permute-done.4.rest_7_.rest_6_
  19.2 0.0 copy-done
  19.2 0.0 copy-done.1
  19.2 0.0 copy-done.2
  19.3 2.2 %near.1 = (f32[2,2,128,128]{3,2,1,0:T(8,128)S(1)}, bf16[2,128,256]{2,1,0:T(8,128)(2,1)S(1)}, bf16[4,2,128,128]{3,2,1,0:T(8,128)(2,1)S(1)}) custom-call(s32[8]{0:T(128)S(1)} %copy-done.3, s32[8]{0:T(128)S(1)} %copy-done.4, s32[4,8]{1,0:T(4,128)S(1)} %copy-done.2, bf16[2,8,128,128]{3,2,1,0:T(8,128)(2,1)S(1)} %copy-done, ...), custom_call_target="tpu_custom_call" | custom-call | flops 536870912 | bytes 1048576 | tf_op jit(solution)/shard_map/near/pallas_call | solution.py:243
  21.5 0.0 collective-permute-done.5.rest_2_
  21.5 0.0 collective-permute-done.6.rest_3_
  21.5 1.2 %far.1 = (bf16[2,2,128,128]{3,2,1,0:T(8,128)(2,1)S(1)}, f32[2,2,128,128]{3,2,1,0:T(8,128)S(1)}) custom-call(s32[8]{0:T(128)S(1)} %copy-done.3, s32[8]{0:T(128)S(1)} %copy-done.4, bf16[528,128]{1,0:T(8,128)(2,1)S(1)} %collective-permute-done.1.rest_3_.rest_0_, bf16[528,128]{1,0:T(8,128)(2,1)S(1)} %collective-permute-done.2.rest_4_.rest_1_, ...), custom_call_target="tpu_custom_call" | custom-call | flops 536870912 | bytes 1048576 | tf_op jit(solution)/shard_map/far/pallas_call | solution.py:243
  22.7 1.6 %collective-permute-start.7 = (bf16[2,2,128,128]{3,2,1,0:T(8,128)(2,1)S(1)}, bf16[2,2,128,128]{3,2,1,0:T(8,128)(2,1)S(1)}, u32[]{:S(2)}, u32[]{:S(2)}) collective-permute-start(bf16[2,2,128,128]{3,2,1,0:T(8,128)(2,1)S(1)} %get-tuple-element.22), channel_id=1, source_target_pairs={{0,2},{1,3},{2,0},{3,1},{4,6},{5,7},{6,4},{7,5},{8,10},{9,11},{10,... | collective-permute-start | bytes 393224 | tf_op jit(solution)/shard_map/ppermute | solution.py:210
  24.3 3.5 %collective-permute-done.7 = bf16[2,2,128,128]{3,2,1,0:T(8,128)(2,1)S(1)} collective-permute-done((bf16[2,2,128,128]{3,2,1,0:T(8,128)(2,1)S(1)}, bf16[2,2,128,128]{3,2,1,0:T(8,128)(2,1)S(1)}, u32[]{:S(2)}, u32[]{:S(2)}) %collective-permute-start.7) | collective-permute-done | bytes 131104 | tf_op jit(solution)/shard_map/ppermute | solution.py:210
  27.8 0.7 %add_convert_fusion = bf16[2,2,128,128]{3,2,1,0:T(8,128)(2,1)} fusion(bf16[2,2,128,128]{3,2,1,0:T(8,128)(2,1)S(1)} %collective-permute-done.7, f32[2,2,128,128]{3,2,1,0:T(8,128)S(1)} %get-tuple-element.18.rest_7_, f32[2,2,128,128]{3,2,1,0:T(8,128)S(1)} %get-tuple-element.21, pred[]{:T(512)S(6)} %eq.3), kind=kLoop, calls=%fused_computation | loop fusion | flops 262144 | bytes 786433 | tf_op jit(solution)/shard_map/convert_element_type | solution.py:273
  (6 shorter events, 0.0 us)
Async XLA Ops:
  0.0 19.2 %copy-start = (bf16[2,8,128,128]{3,2,1,0:T(8,128)(2,1)S(1)}, bf16[2,8,128,128]{3,2,1,0:T(8,128)(2,1)}, u32[]{:S(2)}) copy-start(bf16[2,8,128,128]{3,2,1,0:T(8,128)(2,1)} %rest_0_.1) | copy-start | bytes 1572868
  0.0 19.2 %copy-start.1 = (bf16[4,2,128,128]{3,2,1,0:T(8,128)(2,1)S(1)}, bf16[4,2,128,128]{3,2,1,0:T(8,128)(2,1)}, u32[]{:S(2)}) copy-start(bf16[4,2,128,128]{3,2,1,0:T(8,128)(2,1)} %rest_1_.1) | copy-start | bytes 786436
  1.9 17.3 %copy-start.2 = (s32[4,8]{1,0:T(4,128)S(1)}, s32[4,8]{1,0:T(4,128)}, u32[]{:S(2)}) copy-start(s32[4,8]{1,0:T(4,128)} %blocks_ref.3) | copy-start | bytes 388
  1.9 17.3 %collective-permute-start.4 = (bf16[4,2,128,128]{3,2,1,0:T(8,128)(2,1)}, bf16[4,2,128,128]{3,2,1,0:T(8,128)(2,1)S(1)}, u32[]{:S(2)}, u32[]{:S(2)}) collective-permute-start(bf16[4,2,128,128]{3,2,1,0:T(8,128)(2,1)} %rest_6_.1), channel_id=1, source_target_pairs={{0,1},{1,0},{2,3},{3,2},{4,5},{5,4},{6,7},{7,6},{8,9},{9,8},{10,11... | collective-permute-start | bytes 786440 | tf_op jit(solution)/shard_map/ppermute | solution.py:210
  2.5 8.2 %collective-permute-start.1 = (bf16[528,128]{1,0:T(8,128)(2,1)S(1)}, bf16[528,128]{1,0:T(8,128)(2,1)S(1)}, u32[]{:S(2)}, u32[]{:S(2)}) collective-permute-start(bf16[528,128]{1,0:T(8,128)(2,1)S(1)} %get-tuple-element.15), channel_id=1, source_target_pairs={{0,8},{1,4},{2,10},{3,6},{4,1},{5,13},{6,3},{7,15},{8,0},{9,12},{1... | collective-permute-start | bytes 405512 | tf_op jit(solution)/shard_map/ppermute | solution.py:218
  6.1 6.4 %collective-permute-start.2 = (bf16[528,128]{1,0:T(8,128)(2,1)S(1)}, bf16[528,128]{1,0:T(8,128)(2,1)S(1)}, u32[]{:S(2)}, u32[]{:S(2)}) collective-permute-start(bf16[528,128]{1,0:T(8,128)(2,1)S(1)} %get-tuple-element.15), channel_id=1, source_target_pairs={{0,4},{1,8},{2,6},{3,10},{4,13},{5,1},{6,15},{7,3},{8,12},{9,0},{1... | collective-permute-start | bytes 405512 | tf_op jit(solution)/shard_map/ppermute | solution.py:218
  6.1 13.1 %copy-start.3 = (s32[8]{0:T(128)S(1)}, s32[8]{0:T(128)}, u32[]{:S(2)}) copy-start(s32[8]{0:T(128)} %lsize_ref.3) | copy-start | bytes 100
  6.1 13.1 %copy-start.4 = (s32[8]{0:T(128)S(1)}, s32[8]{0:T(128)}, u32[]{:S(2)}) copy-start(s32[8]{0:T(128)} %rsize_ref.3) | copy-start | bytes 100
  6.1 13.1 %collective-permute-start = (bf16[528,128]{1,0:T(8,128)(2,1)S(1)}, bf16[528,128]{1,0:T(8,128)(2,1)S(1)}, u32[]{:S(2)}, u32[]{:S(2)}) collective-permute-start(bf16[528,128]{1,0:T(8,128)(2,1)S(1)} %get-tuple-element.14), channel_id=1, source_target_pairs={{0,4},{1,0},{2,6},{3,2},{4,5},{5,1},{6,7},{7,3},{8,12},{9,8},{10,1... | collective-permute-start | bytes 405512 | tf_op jit(solution)/shard_map/ppermute | solution.py:218
  7.8 11.4 %collective-permute-start.3 = (bf16[2,2,128,128]{3,2,1,0:T(8,128)(2,1)S(1)}, bf16[2,2,128,128]{3,2,1,0:T(8,128)(2,1)S(1)}, u32[]{:S(2)}, u32[]{:S(2)}) collective-permute-start(bf16[2,2,128,128]{3,2,1,0:T(8,128)(2,1)S(1)} %get-tuple-element.16), channel_id=1, source_target_pairs={{0,8},{1,12},{2,10},{3,14},{4,9},{5,13},{6,11},{7,15},{8,0},{9,4},... | collective-permute-start | bytes 393224 | tf_op jit(solution)/shard_map/ppermute | solution.py:218
  10.6 10.8 %collective-permute-start.5 = (bf16[528,128]{1,0:T(8,128)(2,1)S(1)}, bf16[528,128]{1,0:T(8,128)(2,1)S(1)}, u32[]{:S(2)}, u32[]{:S(2)}) collective-permute-start(bf16[528,128]{1,0:T(8,128)(2,1)S(1)} %collective-permute-done.1.rest_3_.rest_0_), channel_id=1, source_target_pairs={{0,4},{1,0},{2,6},{3,2},{4,5},{5,1},{6,7},{7,3},{8,12},{9,8},{10,1... | collective-permute-start | bytes 405512 | tf_op jit(solution)/shard_map/ppermute | solution.py:218
  12.5 9.0 %collective-permute-start.6 = (bf16[528,128]{1,0:T(8,128)(2,1)S(1)}, bf16[528,128]{1,0:T(8,128)(2,1)S(1)}, u32[]{:S(2)}, u32[]{:S(2)}) collective-permute-start(bf16[528,128]{1,0:T(8,128)(2,1)S(1)} %collective-permute-done.2.rest_4_.rest_1_), channel_id=1, source_target_pairs={{0,4},{1,0},{2,6},{3,2},{4,5},{5,1},{6,7},{7,3},{8,12},{9,8},{10,1... | collective-permute-start | bytes 405512 | tf_op jit(solution)/shard_map/ppermute | solution.py:218
  22.7 5.0 %collective-permute-start.7 = (bf16[2,2,128,128]{3,2,1,0:T(8,128)(2,1)S(1)}, bf16[2,2,128,128]{3,2,1,0:T(8,128)(2,1)S(1)}, u32[]{:S(2)}, u32[]{:S(2)}) collective-permute-start(bf16[2,2,128,128]{3,2,1,0:T(8,128)(2,1)S(1)} %get-tuple-element.22), channel_id=1, source_target_pairs={{0,2},{1,3},{2,0},{3,1},{4,6},{5,7},{6,4},{7,5},{8,10},{9,11},{10,... | collective-permute-start | bytes 393224 | tf_op jit(solution)/shard_map/ppermute | solution.py:210

commit v2 on v1

--- a/solution.py
+++ b/solution.py
@@ -34,8 +34,9 @@
     return c == jnp.bitwise_and(z, 1)
 
 
-def pack_kernel(blocks_ref, psi_ref, left_ref, left_out, side_out, far_out, sem):
-    z, _, _ = place()
+def pack_kernel(blocks_ref, psi_ref, left_ref, right_ref, *rest):
+    left_out, side_out, far_out, right_out, sem = rest
+    z, x, _ = place()
     sectors, tile = psi_ref.shape[0], psi_ref.shape[-1]
     count = 2 * sectors
     row = lax.broadcasted_iota(jnp.int32, (ID_ROWS, tile), 0)
@@ -54,9 +55,10 @@
             for spot, source in enumerate(sources)
         ]
 
-    far = pl.ds(jnp.bitwise_xor(z, jnp.where(is_home(), 2, 3)) * sectors, sectors)
+    far = jnp.bitwise_xor(z, jnp.where(is_home(), 2, 3)) * sectors + x
     plain = copies(picked, left_out, 0)
     plain.append(pltpu.make_async_copy(psi_ref.at[:, far], far_out, sem.at[2 * count]))
+    plain.append(pltpu.make_async_copy(right_ref, right_out, sem.at[2 * count + 1]))
     for copy in plain:
         copy.start()
     for at_home, sources in ((True, asked), (False, picked)):
@@ -80,16 +82,17 @@
     return (rows < height) & (lanes < rsize_ref[z * sectors + b])
 
 
-def wide_psi(z, distance, sizes, a, blocks):
+def wide_psi(z, distance, sizes, a, columns, blocks):
     tile = blocks[0].shape[-1]
     cut = []
-    for b, block in enumerate(blocks):
+    for b, block in zip(columns, blocks):
         keep = keep_mask(z, distance, sizes, a, b, len(blocks), tile)
         cut.append(jnp.where(keep, block.astype(jnp.float32), 0.0).astype(jnp.bfloat16))
     return jnp.concatenate(cut, axis=1)
 
 
-def partial_sums(z, distance, sizes, sectors, psi, lefts, rights, store):
+def partial_sums(z, distance, sizes, columns, psi, lefts, rights, store):
+    sectors = len(columns)
     for a in range(sectors):
         wide = psi(a)
         tile = wide.shape[0]
@@ -97,9 +100,9 @@
         for left in lefts:
             both = jnp.dot(left(a), wide, preferred_element_type=jnp.float32).astype(jnp.bfloat16)
             applied += [both[:tile], both[tile:]]
-        for b in range(sectors):
+        for side, b in enumerate(columns):
             picked = [right(a, slot, b) for right in rights for slot in range(2)]
-            column = [part[:, b * tile : (b + 1) * tile] for part in applied]
+            column = [part[:, side * tile : (side + 1) * tile] for part in applied]
             total = lax.dot_general(
                 jnp.concatenate(column, axis=1),
                 jnp.concatenate(picked, axis=1),
@@ -128,32 +131,33 @@
     return left, right
 
 
+def mask_kernel(lsize_ref, rsize_ref, psi_same, psi_other, wide_ref):
+    z, x, _ = place()
+    far = jnp.where(is_home(), 2, 3)
+    for a in range(psi_same.shape[0]):
+        blocks = [psi_same[a], psi_other[a]]
+        wide_ref[a] = wide_psi(z, far, (lsize_ref, rsize_ref), a, (x, 1 - x), blocks)
+
+
 def near_kernel(lsize_ref, rsize_ref, blocks_ref, *rest):
-    psi_ref, left_ref, side, direct_a, direct_b, psi_far, right_hbm, right_other = rest[:8]
-    out_ref, wide_ref, right_own, sem = rest[8:]
+    psi_ref, left_ref, side, direct_a, direct_b, right_own, right_other, out_ref = rest
     z, _, _ = place()
     sectors, tile = out_ref.shape[0], out_ref.shape[-1]
-    sizes = (lsize_ref, rsize_ref)
-    copy = pltpu.make_async_copy(right_hbm, right_own, sem)
-    copy.start()
-    distance = jnp.where(is_home(), 2, 3)
-    for a in range(sectors):
-        wide_ref[a] = wide_psi(z, distance, sizes, a, [psi_far[a, b] for b in range(sectors)])
-    copy.wait()
+    sizes, columns = (lsize_ref, rsize_ref), range(sectors)
 
     def store(b, a, total):
         out_ref[b, a] = total
 
+    def masked(distance, a, blocks):
+        return wide_psi(z, distance, sizes, a, columns, blocks)
+
     @pl.when(is_home())
     def _():
-        terms = [acting_terms(blocks_ref, z * sectors + a) for a in range(sectors)]
+        terms = [acting_terms(blocks_ref, z * sectors + a) for a in columns]
         left, right = message(side, right_other)
-
-        def psi(a):
-            return wide_psi(z, 0, sizes, a, [psi_ref[a, z * sectors + b] for b in range(sectors)])
-
         partial_sums(
-            z, 0, sizes, sectors, psi,
+            z, 0, sizes, columns,
+            lambda a: masked(0, a, [psi_ref[a, z * sectors + b] for b in columns]),
             [lambda a: jnp.concatenate([left_ref[term, a] for term in terms[a]], axis=0), left],
             [lambda a, slot, b: right_own[terms[a][slot], b], right],
             store,
@@ -164,17 +168,16 @@
         lefts, rights = zip(message(direct_b, right_own), message(direct_a, right_other))
 
         def psi(a):
-            spots = [pl.ds((sectors * a + b) * tile, tile) for b in range(sectors)]
-            return wide_psi(z, 1, sizes, a, [side[spot] for spot in spots])
-
-        partial_sums(z, 1, sizes, sectors, psi, lefts, rights, store)
+            return masked(1, a, [side[pl.ds((sectors * a + b) * tile, tile)] for b in columns])
+
+        partial_sums(z, 1, sizes, columns, psi, lefts, rights, store)
 
 
 def far_kernel(lsize_ref, rsize_ref, *rest):
-    direct_a, direct_b, passed_a, passed_b, wide_ref, right_own, right_other, near_ref = rest[:8]
-    sent_ref, out_ref = rest[8:]
+    direct_a, direct_b, passed_a, passed_b, right_own, right_other = rest[:6]
+    near_ref, wide_ref, sent_ref, out_ref = rest[6:]
     z, x, _ = place()
-    sectors = out_ref.shape[0]
+    columns = (x, 1 - x)
     far_leaves = lax.shift_right_logical(z, 1) == x
 
     def store_sent(b, a, total):
@@ -195,7 +198,7 @@
                 lefts, rights = zip(message(first, right_own), message(second, right_other))
                 sizes = (lsize_ref, rsize_ref)
                 partial_sums(
-                    z, distance, sizes, sectors, lambda a: wide_ref[a], lefts, rights, store
+                    z, distance, sizes, columns, lambda a: wide_ref[a], lefts, rights, store
                 )
 
 
@@ -221,52 +224,56 @@
         pltpu.with_memory_space_constraint(array, pltpu.HBM)
         for array in (psi, left_ops, right_ops, term_blocks)
     ]
-    left_sent, side_sent, far_sent = pl.pallas_call(
+    left_sent, side_sent, far_sent, right_own = pl.pallas_call(
         pack_kernel,
-        out_shape=[block(message_shape), block(message_shape), block(out_shape)],
-        in_specs=[SMEM, ANY, ANY],
-        out_specs=[VMEM] * 3,
-        scratch_shapes=[pltpu.SemaphoreType.DMA((4 * sectors + 1,))],
+        out_shape=[
+            block(message_shape),
+            block(message_shape),
+            block((sectors, tile, tile)),
+            block(right_ops.shape),
+        ],
+        in_specs=[SMEM, ANY, ANY, ANY],
+        out_specs=[VMEM] * 4,
+        scratch_shapes=[pltpu.SemaphoreType.DMA((4 * sectors + 2,))],
         compiler_params=PARAMS,
         name="pack",
-    )(blocks_hbm, psi_hbm, left_hbm)
+    )(blocks_hbm, psi_hbm, left_hbm, right_hbm)
     direct_a = over_z(left_sent, 2, 1)
     direct_b = over_z(left_sent, 1, 2)
-    psi_far = over_z(far_sent, 2, 3)
+    far_same = over_z(far_sent, 2, 3)
+    far_other = over_op(far_same, 2)
     side = over_z(side_sent, 1, 0)
     passed_a = over_z(direct_a, 1, 0)
     passed_b = over_z(direct_b, 1, 0)
-    held, _ = lax.optimization_barrier((right_ops, left_sent))
-    right_other = over_op(held, 1)
-
-    def apply(kernel, name, outs, scalars, operands, scratch):
+    right_other = over_op(right_own, 1)
+
+    def apply(kernel, name, outs, scalars, operands):
         return pl.pallas_call(
             kernel,
             out_shape=outs,
-            in_specs=[SMEM] * len(scalars) + [spec for _, spec in operands],
+            in_specs=[SMEM] * len(scalars) + [VMEM] * len(operands),
             out_specs=[VMEM] * len(outs),
-            scratch_shapes=scratch,
             compiler_params=PARAMS,
             cost_estimate=pl.CostEstimate(
                 flops=64 * tile**3 * sectors**2, bytes_accessed=2**20, transcendentals=0
             ),
             name=name,
-        )(*scalars, *[array for array, _ in operands])
+        )(*scalars, *operands)
 
     sizes = (left_sizes, right_sizes)
+    rights = [right_own, right_other]
     total = jax.ShapeDtypeStruct(out_shape, jnp.float32)
-    inside = [psi, left_ops, side, direct_a, direct_b, psi_far]
-    near, wide, right_own = apply(
-        near_kernel, "near",
-        [total, block((sectors, tile, sectors * tile)), block(right_ops.shape)],
-        sizes + (term_blocks,),
-        [(array, VMEM) for array in inside] + [(right_hbm, ANY), (right_other, VMEM)],
-        [pltpu.SemaphoreType.DMA(())],
-    )
-    inside = [direct_a, direct_b, passed_a, passed_b, wide, right_own, right_other, near]
+    (near,) = apply(
+        near_kernel, "near", [total], sizes + (term_blocks,),
+        [psi, left_ops, side, direct_a, direct_b] + rights,
+    )
+    (wide,) = apply(
+        mask_kernel, "mask", [block((sectors, tile, sectors * tile))], sizes,
+        [far_same, far_other],
+    )
     sent, far = apply(
         far_kernel, "far", [block(out_shape), total], sizes,
-        [(array, VMEM) for array in inside], [],
+        [direct_a, direct_b, passed_a, passed_b] + rights + [near, wide],
     )
     arrived = over_op(sent, 2)
     kept = jnp.where(lax.axis_index("blk") // 2 == lax.axis_index("op") // 2, near, far)

time: 28.6 us -> 30.2 us (1.056)
  waiting for transfers between devices: 9 us -> 10.7 us
  Pallas kernels: 5.32 us -> 4.91 us
    ppermute x2 -> x3, waiting for transfers between devices: 3.46 us -> 5.21 us  [over_op(): return lax.ppermute(array, 'op', [(o, o ^ step) for o in range(n)])]
    ppermute x2 -> x3, starting transfers between devices: 2.1 us -> 3.02 us  [over_op(): return lax.ppermute(array, 'op', [(o, o ^ step) for o in range(n)])]
    ppermute x6, starting transfers between devices: 11.2 us -> 10.6 us  [over_z(): return lax.ppermute(array, ('blk', 'op'), pairs)]
    pallas_call x2 -> x3, Pallas kernels: 3.41 us -> 3.04 us  [apply(): pl.pallas_call(kernel, out_shape=outs, in_specs=[SMEM] * len(scalars) + [...]
  transfers between devices with their start and end apart: 8 -> 9, of which waited for: 4 -> 4; matrix products, arithmetic and copies ran while one was open for 0% -> 0% of each run, Pallas kernels for 8% -> 6%
where the time goes in v2:
time: 30.2 us; the launch traced here: 30 us
  starting transfers between devices  13.6 us (45%)
  waiting for transfers between devices  10.7 us (35%)
  Pallas kernels  4.91 us (16%)
  other arithmetic  0.69 us (2%)
    ppermute x6, starting transfers between devices, over_z(): return lax.ppermute(array, ('blk', 'op'), pairs)  10.6 us
    ppermute x6, waiting for transfers between devices, over_z(): return lax.ppermute(array, ('blk', 'op'), pairs)  5.52 us
    ppermute x3, waiting for transfers between devices, over_op(): return lax.ppermute(array, 'op', [(o, o ^ step) for o in range(n)])  5.21 us
    pallas_call x3, Pallas kernels, apply(): pl.pallas_call(kernel, out_shape=outs, in_specs=[SMEM] * len(scalars) + [...  3.04 us
    ppermute x3, starting transfers between devices, over_op(): return lax.ppermute(array, 'op', [(o, o ^ step) for o in range(n)])  3.02 us
    pallas_call x1, Pallas kernels, shards(): pl.pallas_call(pack_kernel, out_shape=[block(message_shape), block(messag...  1.86 us
    convert_element_type x1, other arithmetic, shards(): return (kept + arrived.astype(jnp.float32)).astype(jnp.bfloat16)  0.69 us
  transfers between devices with their start and end apart: 9, of which 4 were waited for; matrix products, arithmetic and copies ran while one was open for 0% of the time, Pallas kernels for 6%

profile of v2, /device:TPU:0, one launch (start us, length us, event | category | flops | bytes accessed | tf_op | source)
XLA Modules:
  0.0 30.0 jit_solution(8263097057175134664)
XLA Ops:
  0.0 1.9 %pack.1 = (bf16[528,128]{1,0:T(8,128)(2,1)S(1)}, bf16[528,128]{1,0:T(8,128)(2,1)S(1)}, bf16[2,128,128]{2,1,0:T(8,128)(2,1)S(1)}, bf16[4,2,128,128]{3,2,1,0:T(8,128)(2,1)S(1)}) custom-call(s32[4,8]{1,0:T(4,128)} %blocks_ref.3, bf16[2,8,128,128]{3,2,1,0:T(8,128)(2,1)} %rest_0_.1, bf16[4,2,128,128]{3,2,1,0:T(8,128)(2,1)} %rest_1_.1, ...), custom_call_target="tpu_custom_call" | custom-call | tf_op jit(solution)/shard_map/pack/pallas_call | solution.py:227
  1.9 0.5 %collective-permute-start.3 = (bf16[4,2,128,128]{3,2,1,0:T(8,128)(2,1)S(1)}, bf16[4,2,128,128]{3,2,1,0:T(8,128)(2,1)S(1)}, u32[]{:S(2)}, u32[]{:S(2)}) collective-permute-start(bf16[4,2,128,128]{3,2,1,0:T(8,128)(2,1)S(1)} %get-tuple-element.13.rest_5_.rest_4_), channel_id=1, source_target_pairs={{0,1},{1,0},{2,3},{3,2},{4,5},{5,4},{6,7},{7,6},{8,9},{9,8},{10,11... | collective-permute-start | bytes 786440 | tf_op jit(solution)/shard_map/ppermute | solution.py:213
  2.4 3.7 %collective-permute-start.1 = (bf16[528,128]{1,0:T(8,128)(2,1)S(1)}, bf16[528,128]{1,0:T(8,128)(2,1)S(1)}, u32[]{:S(2)}, u32[]{:S(2)}) collective-permute-start(bf16[528,128]{1,0:T(8,128)(2,1)S(1)} %get-tuple-element.12), channel_id=1, source_target_pairs={{0,8},{1,4},{2,10},{3,6},{4,1},{5,13},{6,3},{7,15},{8,0},{9,12},{1... | collective-permute-start | bytes 405512 | tf_op jit(solution)/shard_map/ppermute | solution.py:221
  6.1 0.0 collective-permute-start.2
  6.1 2.1 %collective-permute-start.6 = (bf16[2,128,128]{2,1,0:T(8,128)(2,1)S(1)}, bf16[2,128,128]{2,1,0:T(8,128)(2,1)S(1)}, u32[]{:S(2)}, u32[]{:S(2)}) collective-permute-start(bf16[2,128,128]{2,1,0:T(8,128)(2,1)S(1)} %get-tuple-element.14), channel_id=1, source_target_pairs={{0,8},{1,12},{2,10},{3,14},{4,9},{5,13},{6,11},{7,15},{8,0},{9,4},... | collective-permute-start | bytes 196616 | tf_op jit(solution)/shard_map/ppermute | solution.py:221
  8.1 1.1 %collective-permute-start = (bf16[528,128]{1,0:T(8,128)(2,1)S(1)}, bf16[528,128]{1,0:T(8,128)(2,1)S(1)}, u32[]{:S(2)}, u32[]{:S(2)}) collective-permute-start(bf16[528,128]{1,0:T(8,128)(2,1)S(1)} %get-tuple-element.11), channel_id=1, source_target_pairs={{0,4},{1,0},{2,6},{3,2},{4,5},{5,1},{6,7},{7,3},{8,12},{9,8},{10,1... | collective-permute-start | bytes 405512 | tf_op jit(solution)/shard_map/ppermute | solution.py:221
  9.3 3.5 %collective-permute-done.6.psi_same = bf16[2,128,128]{2,1,0:T(8,128)(2,1)S(1)} collective-permute-done((bf16[2,128,128]{2,1,0:T(8,128)(2,1)S(1)}, bf16[2,128,128]{2,1,0:T(8,128)(2,1)S(1)}, u32[]{:S(2)}, u32[]{:S(2)}) %collective-permute-start.6) | collective-permute-done | bytes 65568 | tf_op jit(solution)/shard_map/ppermute | solution.py:221
  12.8 2.2 %collective-permute-start.7 = (bf16[2,128,128]{2,1,0:T(8,128)(2,1)S(1)}, bf16[2,128,128]{2,1,0:T(8,128)(2,1)S(1)}, u32[]{:S(2)}, u32[]{:S(2)}) collective-permute-start(bf16[2,128,128]{2,1,0:T(8,128)(2,1)S(1)} %collective-permute-done.6.psi_same), channel_id=1, source_target_pairs={{0,2},{1,3},{2,0},{3,1},{4,6},{5,7},{6,4},{7,5},{8,10},{9,11},{10,... | collective-permute-start | bytes 196616 | tf_op jit(solution)/shard_map/ppermute | solution.py:213
  15.0 0.0 collective-permute-done.1.rest_3_.rest_0_
  15.0 3.6 %collective-permute-start.4 = (bf16[528,128]{1,0:T(8,128)(2,1)S(1)}, bf16[528,128]{1,0:T(8,128)(2,1)S(1)}, u32[]{:S(2)}, u32[]{:S(2)}) collective-permute-start(bf16[528,128]{1,0:T(8,128)(2,1)S(1)} %collective-permute-done.1.rest_3_.rest_0_), channel_id=1, source_target_pairs={{0,4},{1,0},{2,6},{3,2},{4,5},{5,1},{6,7},{7,3},{8,12},{9,8},{10,1... | collective-permute-start | bytes 405512 | tf_op jit(solution)/shard_map/ppermute | solution.py:221
  18.6 0.0 collective-permute-done.2.rest_4_.rest_1_
  18.6 0.1 collective-permute-start.5
  18.7 0.0 collective-permute-done.7.psi_other
  18.7 0.0 copy-done.4
  18.7 0.6 %mask.1.rest_7_ = bf16[2,128,256]{2,1,0:T(8,128)(2,1)S(1)} custom-call(s32[8]{0:T(128)S(1)} %copy-done.3, s32[8]{0:T(128)S(1)} %copy-done.4, bf16[2,128,128]{2,1,0:T(8,128)(2,1)S(1)} %collective-permute-done.6.psi_same, bf16[2,128,128]{2,1,0:T(8,128)(2,1)S(1)} %collective-permute-done.7.psi_other), custom_call_target="tpu_custom_call" | custom-call | flops 536870912 | bytes 1048576 | tf_op jit(solution)/shard_map/mask/pallas_call | solution.py:251
  19.3 0.0 collective-permute-done.rest_2_
  19.3 0.0 collective-permute-done.3.rest_6_.rest_5_
  19.4 1.2 %near.1.rest_6_ = f32[2,2,128,128]{3,2,1,0:T(8,128)S(1)} custom-call(s32[8]{0:T(128)S(1)} %copy-done.3, s32[8]{0:T(128)S(1)} %copy-done.4, s32[4,8]{1,0:T(4,128)S(1)} %copy-done.2, bf16[2,8,128,128]{3,2,1,0:T(8,128)(2,1)S(1)} %copy-done, bf16[4,2,128,128]{3,2,1,0:T(8,128)(2,1)S(1)} %copy-done.1, bf16[528,128]{1,0:T(8,128)(2,1)S(1)} %collective-permute-done.rest_2_, ...), custom_call_target="tpu_custom_call" | custom-call | flops 536870912 | bytes 1048576 | tf_op jit(solution)/shard_map/near/pallas_call | solution.py:251
  20.6 0.6 %collective-permute-done.4.rest_2_ = bf16[528,128]{1,0:T(8,128)(2,1)S(1)} collective-permute-done((bf16[528,128]{1,0:T(8,128)(2,1)S(1)}, bf16[528,128]{1,0:T(8,128)(2,1)S(1)}, u32[]{:S(2)}, u32[]{:S(2)}) %collective-permute-start.4) | collective-permute-done | bytes 135200 | tf_op jit(solution)/shard_map/ppermute | solution.py:221
  21.2 1.4 %collective-permute-done.5.rest_3_ = bf16[528,128]{1,0:T(8,128)(2,1)S(1)} collective-permute-done((bf16[528,128]{1,0:T(8,128)(2,1)S(1)}, bf16[528,128]{1,0:T(8,128)(2,1)S(1)}, u32[]{:S(2)}, u32[]{:S(2)}) %collective-permute-start.5) | collective-permute-done | bytes 135200 | tf_op jit(solution)/shard_map/ppermute | solution.py:221
  22.6 1.2 %far.1 = (bf16[2,2,128,128]{3,2,1,0:T(8,128)(2,1)S(1)}, f32[2,2,128,128]{3,2,1,0:T(8,128)S(1)}) custom-call(s32[8]{0:T(128)S(1)} %copy-done.3, s32[8]{0:T(128)S(1)} %copy-done.4, bf16[528,128]{1,0:T(8,128)(2,1)S(1)} %collective-permute-done.1.rest_3_.rest_0_, bf16[528,128]{1,0:T(8,128)(2,1)S(1)} %collective-permute-done.2.rest_4_.rest_1_, ...), custom_call_target="tpu_custom_call" | custom-call | flops 536870912 | bytes 1048576 | tf_op jit(solution)/shard_map/far/pallas_call | solution.py:251
  23.8 0.3 collective-permute-start.8
  24.1 5.2 %collective-permute-done.8 = bf16[2,2,128,128]{3,2,1,0:T(8,128)(2,1)S(1)} collective-permute-done((bf16[2,2,128,128]{3,2,1,0:T(8,128)(2,1)S(1)}, bf16[2,2,128,128]{3,2,1,0:T(8,128)(2,1)S(1)}, u32[]{:S(2)}, u32[]{:S(2)}) %collective-permute-start.8) | collective-permute-done | bytes 131104 | tf_op jit(solution)/shard_map/ppermute | solution.py:213
  29.3 0.7 %add_convert_fusion = bf16[2,2,128,128]{3,2,1,0:T(8,128)(2,1)} fusion(bf16[2,2,128,128]{3,2,1,0:T(8,128)(2,1)S(1)} %collective-permute-done.8, f32[2,2,128,128]{3,2,1,0:T(8,128)S(1)} %near.1.rest_6_, f32[2,2,128,128]{3,2,1,0:T(8,128)S(1)} %get-tuple-element.15, pred[]{:T(512)S(6)} %eq.3), kind=kLoop, calls=%fused_computation | loop fusion | flops 262144 | bytes 786433 | tf_op jit(solution)/shard_map/convert_element_type | solution.py:280
  (9 shorter events, 0.0 us)
Async XLA Ops:
  1.9 17.5 %collective-permute-start.3 = (bf16[4,2,128,128]{3,2,1,0:T(8,128)(2,1)S(1)}, bf16[4,2,128,128]{3,2,1,0:T(8,128)(2,1)S(1)}, u32[]{:S(2)}, u32[]{:S(2)}) collective-permute-start(bf16[4,2,128,128]{3,2,1,0:T(8,128)(2,1)S(1)} %get-tuple-element.13.rest_5_.rest_4_), channel_id=1, source_target_pairs={{0,1},{1,0},{2,3},{3,2},{4,5},{5,4},{6,7},{7,6},{8,9},{9,8},{10,11... | collective-permute-start | bytes 786440 | tf_op jit(solution)/shard_map/ppermute | solution.py:213
  2.4 12.6 %collective-permute-start.1 = (bf16[528,128]{1,0:T(8,128)(2,1)S(1)}, bf16[528,128]{1,0:T(8,128)(2,1)S(1)}, u32[]{:S(2)}, u32[]{:S(2)}) collective-permute-start(bf16[528,128]{1,0:T(8,128)(2,1)S(1)} %get-tuple-element.12), channel_id=1, source_target_pairs={{0,8},{1,4},{2,10},{3,6},{4,1},{5,13},{6,3},{7,15},{8,0},{9,12},{1... | collective-permute-start | bytes 405512 | tf_op jit(solution)/shard_map/ppermute | solution.py:221
  6.1 12.6 %collective-permute-start.2 = (bf16[528,128]{1,0:T(8,128)(2,1)S(1)}, bf16[528,128]{1,0:T(8,128)(2,1)S(1)}, u32[]{:S(2)}, u32[]{:S(2)}) collective-permute-start(bf16[528,128]{1,0:T(8,128)(2,1)S(1)} %get-tuple-element.12), channel_id=1, source_target_pairs={{0,4},{1,8},{2,6},{3,10},{4,13},{5,1},{6,15},{7,3},{8,12},{9,0},{1... | collective-permute-start | bytes 405512 | tf_op jit(solution)/shard_map/ppermute | solution.py:221
  6.1 12.7 %copy-start.3 = (s32[8]{0:T(128)S(1)}, s32[8]{0:T(128)}, u32[]{:S(2)}) copy-start(s32[8]{0:T(128)} %lsize_ref.5) | copy-start | bytes 100
  6.1 12.7 %copy-start.4 = (s32[8]{0:T(128)S(1)}, s32[8]{0:T(128)}, u32[]{:S(2)}) copy-start(s32[8]{0:T(128)} %rsize_ref.5) | copy-start | bytes 100
  6.1 6.7 %collective-permute-start.6 = (bf16[2,128,128]{2,1,0:T(8,128)(2,1)S(1)}, bf16[2,128,128]{2,1,0:T(8,128)(2,1)S(1)}, u32[]{:S(2)}, u32[]{:S(2)}) collective-permute-start(bf16[2,128,128]{2,1,0:T(8,128)(2,1)S(1)} %get-tuple-element.14), channel_id=1, source_target_pairs={{0,8},{1,12},{2,10},{3,14},{4,9},{5,13},{6,11},{7,15},{8,0},{9,4},... | collective-permute-start | bytes 196616 | tf_op jit(solution)/shard_map/ppermute | solution.py:221
  8.1 11.2 %copy-start = (bf16[2,8,128,128]{3,2,1,0:T(8,128)(2,1)S(1)}, bf16[2,8,128,128]{3,2,1,0:T(8,128)(2,1)}, u32[]{:S(2)}) copy-start(bf16[2,8,128,128]{3,2,1,0:T(8,128)(2,1)} %rest_0_.1) | copy-start | bytes 1572868
  8.1 11.2 %copy-start.1 = (bf16[4,2,128,128]{3,2,1,0:T(8,128)(2,1)S(1)}, bf16[4,2,128,128]{3,2,1,0:T(8,128)(2,1)}, u32[]{:S(2)}) copy-start(bf16[4,2,128,128]{3,2,1,0:T(8,128)(2,1)} %rest_1_.1) | copy-start | bytes 786436
  8.1 11.2 %copy-start.2 = (s32[4,8]{1,0:T(4,128)S(1)}, s32[4,8]{1,0:T(4,128)}, u32[]{:S(2)}) copy-start(s32[4,8]{1,0:T(4,128)} %blocks_ref.3) | copy-start | bytes 388
  8.1 11.2 %collective-permute-start = (bf16[528,128]{1,0:T(8,128)(2,1)S(1)}, bf16[528,128]{1,0:T(8,128)(2,1)S(1)}, u32[]{:S(2)}, u32[]{:S(2)}) collective-permute-start(bf16[528,128]{1,0:T(8,128)(2,1)S(1)} %get-tuple-element.11), channel_id=1, source_target_pairs={{0,4},{1,0},{2,6},{3,2},{4,5},{5,1},{6,7},{7,3},{8,12},{9,8},{10,1... | collective-permute-start | bytes 405512 | tf_op jit(solution)/shard_map/ppermute | solution.py:221
  12.8 5.9 %collective-permute-start.7 = (bf16[2,128,128]{2,1,0:T(8,128)(2,1)S(1)}, bf16[2,128,128]{2,1,0:T(8,128)(2,1)S(1)}, u32[]{:S(2)}, u32[]{:S(2)}) collective-permute-start(bf16[2,128,128]{2,1,0:T(8,128)(2,1)S(1)} %collective-permute-done.6.psi_same), channel_id=1, source_target_pairs={{0,2},{1,3},{2,0},{3,1},{4,6},{5,7},{6,4},{7,5},{8,10},{9,11},{10,... | collective-permute-start | bytes 196616 | tf_op jit(solution)/shard_map/ppermute | solution.py:213
  15.0 6.2 %collective-permute-start.4 = (bf16[528,128]{1,0:T(8,128)(2,1)S(1)}, bf16[528,128]{1,0:T(8,128)(2,1)S(1)}, u32[]{:S(2)}, u32[]{:S(2)}) collective-permute-start(bf16[528,128]{1,0:T(8,128)(2,1)S(1)} %collective-permute-done.1.rest_3_.rest_0_), channel_id=1, source_target_pairs={{0,4},{1,0},{2,6},{3,2},{4,5},{5,1},{6,7},{7,3},{8,12},{9,8},{10,1... | collective-permute-start | bytes 405512 | tf_op jit(solution)/shard_map/ppermute | solution.py:221
  18.6 4.0 %collective-permute-start.5 = (bf16[528,128]{1,0:T(8,128)(2,1)S(1)}, bf16[528,128]{1,0:T(8,128)(2,1)S(1)}, u32[]{:S(2)}, u32[]{:S(2)}) collective-permute-start(bf16[528,128]{1,0:T(8,128)(2,1)S(1)} %collective-permute-done.2.rest_4_.rest_1_), channel_id=1, source_target_pairs={{0,4},{1,0},{2,6},{3,2},{4,5},{5,1},{6,7},{7,3},{8,12},{9,8},{10,1... | collective-permute-start | bytes 405512 | tf_op jit(solution)/shard_map/ppermute | solution.py:221
  23.8 5.5 %collective-permute-start.8 = (bf16[2,2,128,128]{3,2,1,0:T(8,128)(2,1)S(1)}, bf16[2,2,128,128]{3,2,1,0:T(8,128)(2,1)S(1)}, u32[]{:S(2)}, u32[]{:S(2)}) collective-permute-start(bf16[2,2,128,128]{3,2,1,0:T(8,128)(2,1)S(1)} %get-tuple-element.16), channel_id=1, source_target_pairs={{0,2},{1,3},{2,0},{3,1},{4,6},{5,7},{6,4},{7,5},{8,10},{9,11},{10,... | collective-permute-start | bytes 393224 | tf_op jit(solution)/shard_map/ppermute | solution.py:213

commit v3 on v2

--- a/solution.py
+++ b/solution.py
@@ -36,7 +36,7 @@
 
 def pack_kernel(blocks_ref, psi_ref, left_ref, right_ref, *rest):
     left_out, side_out, far_out, right_out, sem = rest
-    z, x, _ = place()
+    z, _, _ = place()
     sectors, tile = psi_ref.shape[0], psi_ref.shape[-1]
     count = 2 * sectors
     row = lax.broadcasted_iota(jnp.int32, (ID_ROWS, tile), 0)
@@ -55,7 +55,7 @@
             for spot, source in enumerate(sources)
         ]
 
-    far = jnp.bitwise_xor(z, jnp.where(is_home(), 2, 3)) * sectors + x
+    far = pl.ds(jnp.bitwise_xor(z, jnp.where(is_home(), 2, 3)) * sectors, sectors)
     plain = copies(picked, left_out, 0)
     plain.append(pltpu.make_async_copy(psi_ref.at[:, far], far_out, sem.at[2 * count]))
     plain.append(pltpu.make_async_copy(right_ref, right_out, sem.at[2 * count + 1]))
@@ -131,12 +131,13 @@
     return left, right
 
 
-def mask_kernel(lsize_ref, rsize_ref, psi_same, psi_other, wide_ref):
-    z, x, _ = place()
+def mask_kernel(lsize_ref, rsize_ref, psi_ref, wide_ref):
+    z, _, _ = place()
     far = jnp.where(is_home(), 2, 3)
-    for a in range(psi_same.shape[0]):
-        blocks = [psi_same[a], psi_other[a]]
-        wide_ref[a] = wide_psi(z, far, (lsize_ref, rsize_ref), a, (x, 1 - x), blocks)
+    columns = range(psi_ref.shape[1])
+    for a in range(psi_ref.shape[0]):
+        blocks = [psi_ref[a, b] for b in columns]
+        wide_ref[a] = wide_psi(z, far, (lsize_ref, rsize_ref), a, columns, blocks)
 
 
 def near_kernel(lsize_ref, rsize_ref, blocks_ref, *rest):
@@ -177,7 +178,7 @@
     direct_a, direct_b, passed_a, passed_b, right_own, right_other = rest[:6]
     near_ref, wide_ref, sent_ref, out_ref = rest[6:]
     z, x, _ = place()
-    columns = (x, 1 - x)
+    columns = range(out_ref.shape[0])
     far_leaves = lax.shift_right_logical(z, 1) == x
 
     def store_sent(b, a, total):
@@ -229,7 +230,7 @@
         out_shape=[
             block(message_shape),
             block(message_shape),
-            block((sectors, tile, tile)),
+            block(out_shape),
             block(right_ops.shape),
         ],
         in_specs=[SMEM, ANY, ANY, ANY],
@@ -240,8 +241,7 @@
     )(blocks_hbm, psi_hbm, left_hbm, right_hbm)
     direct_a = over_z(left_sent, 2, 1)
     direct_b = over_z(left_sent, 1, 2)
-    far_same = over_z(far_sent, 2, 3)
-    far_other = over_op(far_same, 2)
+    psi_far = over_z(far_sent, 2, 3)
     side = over_z(side_sent, 1, 0)
     passed_a = over_z(direct_a, 1, 0)
     passed_b = over_z(direct_b, 1, 0)
@@ -267,9 +267,10 @@
         near_kernel, "near", [total], sizes + (term_blocks,),
         [psi, left_ops, side, direct_a, direct_b] + rights,
     )
+    psi_turn, near = lax.optimization_barrier((psi_far, near))
     (wide,) = apply(
         mask_kernel, "mask", [block((sectors, tile, sectors * tile))], sizes,
-        [far_same, far_other],
+        [psi_turn],
     )
     sent, far = apply(
         far_kernel, "far", [block(out_shape), total], sizes,

time: 30.2 us -> 27.7 us (0.917)
  waiting for transfers between devices: 10.7 us -> 8.38 us
    ppermute x6, waiting for transfers between devices: 5.52 us -> 4.27 us  [over_z(): return lax.ppermute(array, ('blk', 'op'), pairs)]
    ppermute x3 -> x2, waiting for transfers between devices: 5.21 us -> 4.1 us  [over_op(): return lax.ppermute(array, 'op', [(o, o ^ step) for o in range(n)])]
    ppermute x3 -> x2, starting transfers between devices: 3.02 us -> 2.09 us  [over_op(): return lax.ppermute(array, 'op', [(o, o ^ step) for o in range(n)])]
    ppermute x6, starting transfers between devices: 10.6 us -> 11.2 us  [over_z(): return lax.ppermute(array, ('blk', 'op'), pairs)]
  transfers between devices with their start and end apart: 9 -> 8, of which waited for: 4 -> 4; matrix products, arithmetic and copies ran while one was open for 0% -> 0% of each run, Pallas kernels for 6% -> 7%
where the time goes in v3:
time: 27.7 us; the launch traced here: 27.6 us
  starting transfers between devices  13.3 us (48%)
  waiting for transfers between devices  8.38 us (30%)
  Pallas kernels  5.07 us (18%)
  other arithmetic  0.69 us (2%)
    ppermute x6, starting transfers between devices, over_z(): return lax.ppermute(array, ('blk', 'op'), pairs)  11.2 us
    ppermute x6, waiting for transfers between devices, over_z(): return lax.ppermute(array, ('blk', 'op'), pairs)  4.27 us
    ppermute x2, waiting for transfers between devices, over_op(): return lax.ppermute(array, 'op', [(o, o ^ step) for o in range(n)])  4.1 us
    pallas_call x3, Pallas kernels, apply(): pl.pallas_call(kernel, out_shape=outs, in_specs=[SMEM] * len(scalars) + [...  3.04 us
    ppermute x2, starting transfers between devices, over_op(): return lax.ppermute(array, 'op', [(o, o ^ step) for o in range(n)])  2.09 us
    pallas_call x1, Pallas kernels, shards(): pl.pallas_call(pack_kernel, out_shape=[block(message_shape), block(messag...  2.03 us
    convert_element_type x1, other arithmetic, shards(): return (kept + arrived.astype(jnp.float32)).astype(jnp.bfloat16)  0.69 us
  transfers between devices with their start and end apart: 8, of which 4 were waited for; matrix products, arithmetic and copies ran while one was open for 0% of the time, Pallas kernels for 7%

profile of v3, /device:TPU:0, one launch (start us, length us, event | category | flops | bytes accessed | tf_op | source)
XLA Modules:
  0.0 27.6 jit_solution(8432746236564249065)
XLA Ops:
  0.0 2.0 %pack.1 = (bf16[528,128]{1,0:T(8,128)(2,1)S(1)}, bf16[528,128]{1,0:T(8,128)(2,1)S(1)}, bf16[2,2,128,128]{3,2,1,0:T(8,128)(2,1)S(1)}, bf16[4,2,128,128]{3,2,1,0:T(8,128)(2,1)S(1)}) custom-call(s32[4,8]{1,0:T(4,128)} %blocks_ref.3, bf16[2,8,128,128]{3,2,1,0:T(8,128)(2,1)} %rest_0_.1, bf16[4,2,128,128]{3,2,1,0:T(8,128)(2,1)} %rest_1_.1, ...), custom_call_target="tpu_custom_call" | custom-call | tf_op jit(solution)/shard_map/pack/pallas_call | solution.py:228
  2.0 0.5 %collective-permute-start.4 = (bf16[4,2,128,128]{3,2,1,0:T(8,128)(2,1)S(1)}, bf16[4,2,128,128]{3,2,1,0:T(8,128)(2,1)S(1)}, u32[]{:S(2)}, u32[]{:S(2)}) collective-permute-start(bf16[4,2,128,128]{3,2,1,0:T(8,128)(2,1)S(1)} %get-tuple-element.16.rest_5_.rest_4_), channel_id=1, source_target_pairs={{0,1},{1,0},{2,3},{3,2},{4,5},{5,4},{6,7},{7,6},{8,9},{9,8},{10,11... | collective-permute-start | bytes 786440 | tf_op jit(solution)/shard_map/ppermute | solution.py:214
  2.6 3.7 %collective-permute-start.2 = (bf16[528,128]{1,0:T(8,128)(2,1)S(1)}, bf16[528,128]{1,0:T(8,128)(2,1)S(1)}, u32[]{:S(2)}, u32[]{:S(2)}) collective-permute-start(bf16[528,128]{1,0:T(8,128)(2,1)S(1)} %get-tuple-element.15), channel_id=1, source_target_pairs={{0,8},{1,4},{2,10},{3,6},{4,1},{5,13},{6,3},{7,15},{8,0},{9,12},{1... | collective-permute-start | bytes 405512 | tf_op jit(solution)/shard_map/ppermute | solution.py:222
  6.2 0.0 collective-permute-start.3
  6.2 1.7 %collective-permute-start.1 = (bf16[528,128]{1,0:T(8,128)(2,1)S(1)}, bf16[528,128]{1,0:T(8,128)(2,1)S(1)}, u32[]{:S(2)}, u32[]{:S(2)}) collective-permute-start(bf16[528,128]{1,0:T(8,128)(2,1)S(1)} %get-tuple-element.14), channel_id=1, source_target_pairs={{0,4},{1,0},{2,6},{3,2},{4,5},{5,1},{6,7},{7,3},{8,12},{9,8},{10,1... | collective-permute-start | bytes 405512 | tf_op jit(solution)/shard_map/ppermute | solution.py:222
  7.9 2.6 %collective-permute-start = (bf16[2,2,128,128]{3,2,1,0:T(8,128)(2,1)S(1)}, bf16[2,2,128,128]{3,2,1,0:T(8,128)(2,1)S(1)}, u32[]{:S(2)}, u32[]{:S(2)}) collective-permute-start(bf16[2,2,128,128]{3,2,1,0:T(8,128)(2,1)S(1)} %get-tuple-element.13), channel_id=1, source_target_pairs={{0,8},{1,12},{2,10},{3,14},{4,9},{5,13},{6,11},{7,15},{8,0},{9,4},... | collective-permute-start | bytes 393224 | tf_op jit(solution)/shard_map/ppermute | solution.py:222
  10.5 0.3 %collective-permute-done.2.rest_3_.rest_0_ = bf16[528,128]{1,0:T(8,128)(2,1)S(1)} collective-permute-done((bf16[528,128]{1,0:T(8,128)(2,1)S(1)}, bf16[528,128]{1,0:T(8,128)(2,1)S(1)}, u32[]{:S(2)}, u32[]{:S(2)}) %collective-permute-start.2) | collective-permute-done | bytes 135200 | tf_op jit(solution)/shard_map/ppermute | solution.py:222
  10.8 0.0 collective-permute-start.5
  10.8 1.8 %collective-permute-done.3.rest_4_.rest_1_ = bf16[528,128]{1,0:T(8,128)(2,1)S(1)} collective-permute-done((bf16[528,128]{1,0:T(8,128)(2,1)S(1)}, bf16[528,128]{1,0:T(8,128)(2,1)S(1)}, u32[]{:S(2)}, u32[]{:S(2)}) %collective-permute-start.3) | collective-permute-done | bytes 135200 | tf_op jit(solution)/shard_map/ppermute | solution.py:222
  12.6 3.3 %collective-permute-start.6 = (bf16[528,128]{1,0:T(8,128)(2,1)S(1)}, bf16[528,128]{1,0:T(8,128)(2,1)S(1)}, u32[]{:S(2)}, u32[]{:S(2)}) collective-permute-start(bf16[528,128]{1,0:T(8,128)(2,1)S(1)} %collective-permute-done.3.rest_4_.rest_1_), channel_id=1, source_target_pairs={{0,4},{1,0},{2,6},{3,2},{4,5},{5,1},{6,7},{7,3},{8,12},{9,8},{10,1... | collective-permute-start | bytes 405512 | tf_op jit(solution)/shard_map/ppermute | solution.py:222
  15.9 0.0 collective-permute-done.1.rest_2_
  15.9 0.0 collective-permute-done.4.rest_6_.rest_5_
  15.9 0.0 copy-done.1
  15.9 0.0 copy-done.2
  16.0 0.0 copy-done.3
  16.0 1.2 %near.1.rest_6_ = f32[2,2,128,128]{3,2,1,0:T(8,128)S(1)} custom-call(s32[8]{0:T(128)S(1)} %copy-done.3, s32[8]{0:T(128)S(1)} %copy-done.4, s32[4,8]{1,0:T(4,128)S(1)} %copy-done.2, bf16[2,8,128,128]{3,2,1,0:T(8,128)(2,1)S(1)} %copy-done, bf16[4,2,128,128]{3,2,1,0:T(8,128)(2,1)S(1)} %copy-done.1, bf16[528,128]{1,0:T(8,128)(2,1)S(1)} %collective-permute-done.1.rest_2_, ...), custom_call_target="tpu_custom_call" | custom-call | flops 536870912 | bytes 1048576 | tf_op jit(solution)/shard_map/near/pallas_call | solution.py:251
  17.2 2.1 %collective-permute-done.psi_ref = bf16[2,2,128,128]{3,2,1,0:T(8,128)(2,1)S(1)} collective-permute-done((bf16[2,2,128,128]{3,2,1,0:T(8,128)(2,1)S(1)}, bf16[2,2,128,128]{3,2,1,0:T(8,128)(2,1)S(1)}, u32[]{:S(2)}, u32[]{:S(2)}) %collective-permute-start) | collective-permute-done | bytes 131104 | tf_op jit(solution)/shard_map/ppermute | solution.py:222
  19.3 0.6 %mask.1.rest_7_ = bf16[2,128,256]{2,1,0:T(8,128)(2,1)S(1)} custom-call(s32[8]{0:T(128)S(1)} %copy-done.3, s32[8]{0:T(128)S(1)} %copy-done.4, bf16[2,2,128,128]{3,2,1,0:T(8,128)(2,1)S(1)} %collective-permute-done.psi_ref), custom_call_target="tpu_custom_call" | custom-call | flops 536870912 | bytes 1048576 | tf_op jit(solution)/shard_map/mask/pallas_call | solution.py:251
  19.9 0.0 collective-permute-done.5.rest_2_
  19.9 0.0 collective-permute-done.6.rest_3_
  20.0 1.2 %far.1 = (bf16[2,2,128,128]{3,2,1,0:T(8,128)(2,1)S(1)}, f32[2,2,128,128]{3,2,1,0:T(8,128)S(1)}) custom-call(s32[8]{0:T(128)S(1)} %copy-done.3, s32[8]{0:T(128)S(1)} %copy-done.4, bf16[528,128]{1,0:T(8,128)(2,1)S(1)} %collective-permute-done.2.rest_3_.rest_0_, bf16[528,128]{1,0:T(8,128)(2,1)S(1)} %collective-permute-done.3.rest_4_.rest_1_, ...), custom_call_target="tpu_custom_call" | custom-call | flops 536870912 | bytes 1048576 | tf_op jit(solution)/shard_map/far/pallas_call | solution.py:251
  21.2 1.6 %collective-permute-start.7 = (bf16[2,2,128,128]{3,2,1,0:T(8,128)(2,1)S(1)}, bf16[2,2,128,128]{3,2,1,0:T(8,128)(2,1)S(1)}, u32[]{:S(2)}, u32[]{:S(2)}) collective-permute-start(bf16[2,2,128,128]{3,2,1,0:T(8,128)(2,1)S(1)} %get-tuple-element.20), channel_id=1, source_target_pairs={{0,2},{1,3},{2,0},{3,1},{4,6},{5,7},{6,4},{7,5},{8,10},{9,11},{10,... | collective-permute-start | bytes 393224 | tf_op jit(solution)/shard_map/ppermute | solution.py:214
  22.8 4.1 %collective-permute-done.7 = bf16[2,2,128,128]{3,2,1,0:T(8,128)(2,1)S(1)} collective-permute-done((bf16[2,2,128,128]{3,2,1,0:T(8,128)(2,1)S(1)}, bf16[2,2,128,128]{3,2,1,0:T(8,128)(2,1)S(1)}, u32[]{:S(2)}, u32[]{:S(2)}) %collective-permute-start.7) | collective-permute-done | bytes 131104 | tf_op jit(solution)/shard_map/ppermute | solution.py:214
  26.9 0.7 %add_convert_fusion = bf16[2,2,128,128]{3,2,1,0:T(8,128)(2,1)} fusion(bf16[2,2,128,128]{3,2,1,0:T(8,128)(2,1)S(1)} %collective-permute-done.7, f32[2,2,128,128]{3,2,1,0:T(8,128)S(1)} %near.1.rest_6_, f32[2,2,128,128]{3,2,1,0:T(8,128)S(1)} %get-tuple-element.19, pred[]{:T(512)S(6)} %eq.3), kind=kLoop, calls=%fused_computation | loop fusion | flops 262144 | bytes 786433 | tf_op jit(solution)/shard_map/convert_element_type | solution.py:281
  (7 shorter events, 0.0 us)
Async XLA Ops:
  0.0 15.9 %copy-start = (bf16[2,8,128,128]{3,2,1,0:T(8,128)(2,1)S(1)}, bf16[2,8,128,128]{3,2,1,0:T(8,128)(2,1)}, u32[]{:S(2)}) copy-start(bf16[2,8,128,128]{3,2,1,0:T(8,128)(2,1)} %rest_0_.1) | copy-start | bytes 1572868
  0.0 15.9 %copy-start.1 = (bf16[4,2,128,128]{3,2,1,0:T(8,128)(2,1)S(1)}, bf16[4,2,128,128]{3,2,1,0:T(8,128)(2,1)}, u32[]{:S(2)}) copy-start(bf16[4,2,128,128]{3,2,1,0:T(8,128)(2,1)} %rest_1_.1) | copy-start | bytes 786436
  2.0 13.9 %collective-permute-start.4 = (bf16[4,2,128,128]{3,2,1,0:T(8,128)(2,1)S(1)}, bf16[4,2,128,128]{3,2,1,0:T(8,128)(2,1)S(1)}, u32[]{:S(2)}, u32[]{:S(2)}) collective-permute-start(bf16[4,2,128,128]{3,2,1,0:T(8,128)(2,1)S(1)} %get-tuple-element.16.rest_5_.rest_4_), channel_id=1, source_target_pairs={{0,1},{1,0},{2,3},{3,2},{4,5},{5,4},{6,7},{7,6},{8,9},{9,8},{10,11... | collective-permute-start | bytes 786440 | tf_op jit(solution)/shard_map/ppermute | solution.py:214
  2.6 13.4 %copy-start.2 = (s32[4,8]{1,0:T(4,128)S(1)}, s32[4,8]{1,0:T(4,128)}, u32[]{:S(2)}) copy-start(s32[4,8]{1,0:T(4,128)} %blocks_ref.3) | copy-start | bytes 388
  2.6 8.2 %collective-permute-start.2 = (bf16[528,128]{1,0:T(8,128)(2,1)S(1)}, bf16[528,128]{1,0:T(8,128)(2,1)S(1)}, u32[]{:S(2)}, u32[]{:S(2)}) collective-permute-start(bf16[528,128]{1,0:T(8,128)(2,1)S(1)} %get-tuple-element.15), channel_id=1, source_target_pairs={{0,8},{1,4},{2,10},{3,6},{4,1},{5,13},{6,3},{7,15},{8,0},{9,12},{1... | collective-permute-start | bytes 405512 | tf_op jit(solution)/shard_map/ppermute | solution.py:222
  6.2 6.4 %collective-permute-start.3 = (bf16[528,128]{1,0:T(8,128)(2,1)S(1)}, bf16[528,128]{1,0:T(8,128)(2,1)S(1)}, u32[]{:S(2)}, u32[]{:S(2)}) collective-permute-start(bf16[528,128]{1,0:T(8,128)(2,1)S(1)} %get-tuple-element.15), channel_id=1, source_target_pairs={{0,4},{1,8},{2,6},{3,10},{4,13},{5,1},{6,15},{7,3},{8,12},{9,0},{1... | collective-permute-start | bytes 405512 | tf_op jit(solution)/shard_map/ppermute | solution.py:222
  6.2 9.7 %copy-start.3 = (s32[8]{0:T(128)S(1)}, s32[8]{0:T(128)}, u32[]{:S(2)}) copy-start(s32[8]{0:T(128)} %lsize_ref.5) | copy-start | bytes 100
  6.2 9.7 %copy-start.4 = (s32[8]{0:T(128)S(1)}, s32[8]{0:T(128)}, u32[]{:S(2)}) copy-start(s32[8]{0:T(128)} %rsize_ref.5) | copy-start | bytes 100
  6.2 9.7 %collective-permute-start.1 = (bf16[528,128]{1,0:T(8,128)(2,1)S(1)}, bf16[528,128]{1,0:T(8,128)(2,1)S(1)}, u32[]{:S(2)}, u32[]{:S(2)}) collective-permute-start(bf16[528,128]{1,0:T(8,128)(2,1)S(1)} %get-tuple-element.14), channel_id=1, source_target_pairs={{0,4},{1,0},{2,6},{3,2},{4,5},{5,1},{6,7},{7,3},{8,12},{9,8},{10,1... | collective-permute-start | bytes 405512 | tf_op jit(solution)/shard_map/ppermute | solution.py:222
  7.9 11.4 %collective-permute-start = (bf16[2,2,128,128]{3,2,1,0:T(8,128)(2,1)S(1)}, bf16[2,2,128,128]{3,2,1,0:T(8,128)(2,1)S(1)}, u32[]{:S(2)}, u32[]{:S(2)}) collective-permute-start(bf16[2,2,128,128]{3,2,1,0:T(8,128)(2,1)S(1)} %get-tuple-element.13), channel_id=1, source_target_pairs={{0,8},{1,12},{2,10},{3,14},{4,9},{5,13},{6,11},{7,15},{8,0},{9,4},... | collective-permute-start | bytes 393224 | tf_op jit(solution)/shard_map/ppermute | solution.py:222
  10.8 9.2 %collective-permute-start.5 = (bf16[528,128]{1,0:T(8,128)(2,1)S(1)}, bf16[528,128]{1,0:T(8,128)(2,1)S(1)}, u32[]{:S(2)}, u32[]{:S(2)}) collective-permute-start(bf16[528,128]{1,0:T(8,128)(2,1)S(1)} %collective-permute-done.2.rest_3_.rest_0_), channel_id=1, source_target_pairs={{0,4},{1,0},{2,6},{3,2},{4,5},{5,1},{6,7},{7,3},{8,12},{9,8},{10,1... | collective-permute-start | bytes 405512 | tf_op jit(solution)/shard_map/ppermute | solution.py:222
  12.6 7.3 %collective-permute-start.6 = (bf16[528,128]{1,0:T(8,128)(2,1)S(1)}, bf16[528,128]{1,0:T(8,128)(2,1)S(1)}, u32[]{:S(2)}, u32[]{:S(2)}) collective-permute-start(bf16[528,128]{1,0:T(8,128)(2,1)S(1)} %collective-permute-done.3.rest_4_.rest_1_), channel_id=1, source_target_pairs={{0,4},{1,0},{2,6},{3,2},{4,5},{5,1},{6,7},{7,3},{8,12},{9,8},{10,1... | collective-permute-start | bytes 405512 | tf_op jit(solution)/shard_map/ppermute | solution.py:222
  21.2 5.7 %collective-permute-start.7 = (bf16[2,2,128,128]{3,2,1,0:T(8,128)(2,1)S(1)}, bf16[2,2,128,128]{3,2,1,0:T(8,128)(2,1)S(1)}, u32[]{:S(2)}, u32[]{:S(2)}) collective-permute-start(bf16[2,2,128,128]{3,2,1,0:T(8,128)(2,1)S(1)} %get-tuple-element.20), channel_id=1, source_target_pairs={{0,2},{1,3},{2,0},{3,1},{4,6},{5,7},{6,4},{7,5},{8,10},{9,11},{10,... | collective-permute-start | bytes 393224 | tf_op jit(solution)/shard_map/ppermute | solution.py:214

commit v4 on v3

--- a/solution.py
+++ b/solution.py
@@ -141,13 +141,15 @@
 
 
 def near_kernel(lsize_ref, rsize_ref, blocks_ref, *rest):
-    psi_ref, left_ref, side, direct_a, direct_b, right_own, right_other, out_ref = rest
+    psi_ref, left_ref, side, direct_a, direct_b, right_own, right_other = rest[:7]
+    out_ref, sent_ref = rest[7:]
     z, _, _ = place()
     sectors, tile = out_ref.shape[0], out_ref.shape[-1]
     sizes, columns = (lsize_ref, rsize_ref), range(sectors)
 
     def store(b, a, total):
         out_ref[b, a] = total
+        sent_ref[b, a] = total.astype(sent_ref.dtype)
 
     def masked(distance, a, blocks):
         return wide_psi(z, distance, sizes, a, columns, blocks)
@@ -175,32 +177,25 @@
 
 
 def far_kernel(lsize_ref, rsize_ref, *rest):
-    direct_a, direct_b, passed_a, passed_b, right_own, right_other = rest[:6]
-    near_ref, wide_ref, sent_ref, out_ref = rest[6:]
-    z, x, _ = place()
+    direct_a, direct_b, passed_a, passed_b, right_own, right_other, wide_ref = rest[:7]
+    out_ref, sent_ref = rest[7:]
+    z, _, _ = place()
     columns = range(out_ref.shape[0])
-    far_leaves = lax.shift_right_logical(z, 1) == x
-
-    def store_sent(b, a, total):
+
+    def store(b, a, total):
+        out_ref[b, a] = total
         sent_ref[b, a] = total.astype(sent_ref.dtype)
 
-    def store_kept(b, a, total):
-        out_ref[b, a] = total
-        sent_ref[b, a] = near_ref[b, a].astype(sent_ref.dtype)
-
-    for leaves, store in ((True, store_sent), (False, store_kept)):
-        for at_home, distance, first, second in (
-            (True, 2, direct_a, direct_b),
-            (False, 3, passed_a, passed_b),
-        ):
-
-            @pl.when((is_home() == at_home) & (far_leaves == leaves))
-            def _(store=store, distance=distance, first=first, second=second):
-                lefts, rights = zip(message(first, right_own), message(second, right_other))
-                sizes = (lsize_ref, rsize_ref)
-                partial_sums(
-                    z, distance, sizes, columns, lambda a: wide_ref[a], lefts, rights, store
-                )
+    for at_home, distance, first, second in (
+        (True, 2, direct_a, direct_b),
+        (False, 3, passed_a, passed_b),
+    ):
+
+        @pl.when(is_home() == at_home)
+        def _(distance=distance, first=first, second=second):
+            lefts, rights = zip(message(first, right_own), message(second, right_other))
+            sizes = (lsize_ref, rsize_ref)
+            partial_sums(z, distance, sizes, columns, lambda a: wide_ref[a], lefts, rights, store)
 
 
 def shards(psi, left_ops, right_ops, term_blocks, left_sizes, right_sizes):
@@ -262,22 +257,27 @@
 
     sizes = (left_sizes, right_sizes)
     rights = [right_own, right_other]
-    total = jax.ShapeDtypeStruct(out_shape, jnp.float32)
-    (near,) = apply(
-        near_kernel, "near", [total], sizes + (term_blocks,),
+    sums = [jax.ShapeDtypeStruct(out_shape, jnp.float32), block(out_shape)]
+    near, near_sent = apply(
+        near_kernel, "near", sums, sizes + (term_blocks,),
         [psi, left_ops, side, direct_a, direct_b] + rights,
     )
-    psi_turn, near = lax.optimization_barrier((psi_far, near))
+    near_arrived = over_op(near_sent, 2)
+    psi_turn, _ = lax.optimization_barrier((psi_far, near_sent))
     (wide,) = apply(
-        mask_kernel, "mask", [block((sectors, tile, sectors * tile))], sizes,
-        [psi_turn],
-    )
-    sent, far = apply(
-        far_kernel, "far", [block(out_shape), total], sizes,
-        [direct_a, direct_b, passed_a, passed_b] + rights + [near, wide],
-    )
-    arrived = over_op(sent, 2)
-    kept = jnp.where(lax.axis_index("blk") // 2 == lax.axis_index("op") // 2, near, far)
+        mask_kernel, "mask", [block((sectors, tile, sectors * tile))], sizes, [psi_turn]
+    )
+    far, far_sent_on = apply(
+        far_kernel, "far", sums, sizes,
+        [direct_a, direct_b, passed_a, passed_b] + rights + [wide],
+    )
+    pairs = [
+        (z * n + 2 * (z // 2) + c, z * n + 2 * (1 - z // 2) + c) for z in range(n) for c in range(2)
+    ]
+    far_arrived = lax.ppermute(far_sent_on, ("blk", "op"), pairs)
+    owns_near = lax.axis_index("blk") // 2 == lax.axis_index("op") // 2
+    kept = jnp.where(owns_near, near, far)
+    arrived = jnp.where(owns_near, near_arrived, far_arrived)
     return (kept + arrived.astype(jnp.float32)).astype(jnp.bfloat16)
 
 

time: 27.7 us -> 28.6 us (1.032)
  starting transfers between devices: 13.3 us -> 16.7 us
  waiting for transfers between devices: 8.38 us -> 5.75 us
    ppermute x2, waiting for transfers between devices: 4.1 us -> 0.01 us  [over_op(): return lax.ppermute(array, 'op', [(o, o ^ step) for o in range(n)])]
    ppermute x0 -> x1, starting transfers between devices: none -> 3.42 us  [shards(): far_arrived = lax.ppermute(far_sent_on, ('blk', 'op'), pairs)]
    ppermute x0 -> x1, waiting for transfers between devices: none -> 3.04 us  [shards(): far_arrived = lax.ppermute(far_sent_on, ('blk', 'op'), pairs)]
    ppermute x6, waiting for transfers between devices: 4.27 us -> 2.7 us  [over_z(): return lax.ppermute(array, ('blk', 'op'), pairs)]
  transfers between devices with their start and end apart: 8 -> 9, of which waited for: 4 -> 4; matrix products, arithmetic and copies ran while one was open for 0% -> 0% of each run, Pallas kernels for 7% -> 11%
where the time goes in v4:
time: 28.6 us; the launch traced here: 28.4 us
  starting transfers between devices  16.7 us (58%)
  waiting for transfers between devices  5.75 us (20%)
  Pallas kernels  5.07 us (18%)
  other arithmetic  0.71 us (2%)
    ppermute x6, starting transfers between devices, over_z(): return lax.ppermute(array, ('blk', 'op'), pairs)  11.2 us
    ppermute x1, starting transfers between devices, shards(): far_arrived = lax.ppermute(far_sent_on, ('blk', 'op'), pairs)  3.42 us
    pallas_call x3, Pallas kernels, apply(): pl.pallas_call(kernel, out_shape=outs, in_specs=[SMEM] * len(scalars) + [...  3.05 us
    ppermute x1, waiting for transfers between devices, shards(): far_arrived = lax.ppermute(far_sent_on, ('blk', 'op'), pairs)  3.04 us
    ppermute x6, waiting for transfers between devices, over_z(): return lax.ppermute(array, ('blk', 'op'), pairs)  2.7 us
    ppermute x2, starting transfers between devices, over_op(): return lax.ppermute(array, 'op', [(o, o ^ step) for o in range(n)])  2.08 us
    pallas_call x1, Pallas kernels, shards(): pl.pallas_call(pack_kernel, out_shape=[block(message_shape), block(messag...  2.03 us
    convert_element_type x1, other arithmetic, shards(): return (kept + arrived.astype(jnp.float32)).astype(jnp.bfloat16)  0.71 us
  transfers between devices with their start and end apart: 9, of which 4 were waited for; matrix products, arithmetic and copies ran while one was open for 0% of the time, Pallas kernels for 11%

profile of v4, /device:TPU:0, one launch (start us, length us, event | category | flops | bytes accessed | tf_op | source)
XLA Modules:
  0.0 28.4 jit_solution(15334561965511669180)
XLA Ops:
  0.0 2.0 %pack.1 = (bf16[528,128]{1,0:T(8,128)(2,1)S(1)}, bf16[528,128]{1,0:T(8,128)(2,1)S(1)}, bf16[2,2,128,128]{3,2,1,0:T(8,128)(2,1)S(1)}, bf16[4,2,128,128]{3,2,1,0:T(8,128)(2,1)S(1)}) custom-call(s32[4,8]{1,0:T(4,128)} %blocks_ref.3, bf16[2,8,128,128]{3,2,1,0:T(8,128)(2,1)} %rest_0_.1, bf16[4,2,128,128]{3,2,1,0:T(8,128)(2,1)} %rest_1_.1, ...), custom_call_target="tpu_custom_call" | custom-call | tf_op jit(solution)/shard_map/pack/pallas_call | solution.py:223
  2.0 0.5 %collective-permute-start.3 = (bf16[4,2,128,128]{3,2,1,0:T(8,128)(2,1)S(1)}, bf16[4,2,128,128]{3,2,1,0:T(8,128)(2,1)S(1)}, u32[]{:S(2)}, u32[]{:S(2)}) collective-permute-start(bf16[4,2,128,128]{3,2,1,0:T(8,128)(2,1)S(1)} %get-tuple-element.16.rest_5_.rest_4_), channel_id=1, source_target_pairs={{0,1},{1,0},{2,3},{3,2},{4,5},{5,4},{6,7},{7,6},{8,9},{9,8},{10,11... | collective-permute-start | bytes 786440 | tf_op jit(solution)/shard_map/ppermute | solution.py:209
  2.6 3.7 %collective-permute-start.1 = (bf16[528,128]{1,0:T(8,128)(2,1)S(1)}, bf16[528,128]{1,0:T(8,128)(2,1)S(1)}, u32[]{:S(2)}, u32[]{:S(2)}) collective-permute-start(bf16[528,128]{1,0:T(8,128)(2,1)S(1)} %get-tuple-element.15), channel_id=1, source_target_pairs={{0,8},{1,4},{2,10},{3,6},{4,1},{5,13},{6,3},{7,15},{8,0},{9,12},{1... | collective-permute-start | bytes 405512 | tf_op jit(solution)/shard_map/ppermute | solution.py:217
  6.2 0.0 collective-permute-start.2
  6.2 1.7 %collective-permute-start = (bf16[528,128]{1,0:T(8,128)(2,1)S(1)}, bf16[528,128]{1,0:T(8,128)(2,1)S(1)}, u32[]{:S(2)}, u32[]{:S(2)}) collective-permute-start(bf16[528,128]{1,0:T(8,128)(2,1)S(1)} %get-tuple-element.14), channel_id=1, source_target_pairs={{0,4},{1,0},{2,6},{3,2},{4,5},{5,1},{6,7},{7,3},{8,12},{9,8},{10,1... | collective-permute-start | bytes 405512 | tf_op jit(solution)/shard_map/ppermute | solution.py:217
  7.9 2.6 %collective-permute-start.6 = (bf16[2,2,128,128]{3,2,1,0:T(8,128)(2,1)S(1)}, bf16[2,2,128,128]{3,2,1,0:T(8,128)(2,1)S(1)}, u32[]{:S(2)}, u32[]{:S(2)}) collective-permute-start(bf16[2,2,128,128]{3,2,1,0:T(8,128)(2,1)S(1)} %get-tuple-element.18), channel_id=1, source_target_pairs={{0,8},{1,12},{2,10},{3,14},{4,9},{5,13},{6,11},{7,15},{8,0},{9,4},... | collective-permute-start | bytes 393224 | tf_op jit(solution)/shard_map/ppermute | solution.py:217
  10.5 0.3 %collective-permute-done.1.rest_3_.rest_0_ = bf16[528,128]{1,0:T(8,128)(2,1)S(1)} collective-permute-done((bf16[528,128]{1,0:T(8,128)(2,1)S(1)}, bf16[528,128]{1,0:T(8,128)(2,1)S(1)}, u32[]{:S(2)}, u32[]{:S(2)}) %collective-permute-start.1) | collective-permute-done | bytes 135200 | tf_op jit(solution)/shard_map/ppermute | solution.py:217
  10.8 0.0 collective-permute-start.4
  10.8 1.8 %collective-permute-done.2.rest_4_.rest_1_ = bf16[528,128]{1,0:T(8,128)(2,1)S(1)} collective-permute-done((bf16[528,128]{1,0:T(8,128)(2,1)S(1)}, bf16[528,128]{1,0:T(8,128)(2,1)S(1)}, u32[]{:S(2)}, u32[]{:S(2)}) %collective-permute-start.2) | collective-permute-done | bytes 135200 | tf_op jit(solution)/shard_map/ppermute | solution.py:217
  12.6 3.3 %collective-permute-start.5 = (bf16[528,128]{1,0:T(8,128)(2,1)S(1)}, bf16[528,128]{1,0:T(8,128)(2,1)S(1)}, u32[]{:S(2)}, u32[]{:S(2)}) collective-permute-start(bf16[528,128]{1,0:T(8,128)(2,1)S(1)} %collective-permute-done.2.rest_4_.rest_1_), channel_id=1, source_target_pairs={{0,4},{1,0},{2,6},{3,2},{4,5},{5,1},{6,7},{7,3},{8,12},{9,8},{10,1... | collective-permute-start | bytes 405512 | tf_op jit(solution)/shard_map/ppermute | solution.py:217
  15.9 0.0 collective-permute-done.rest_2_
  15.9 0.0 collective-permute-done.3.rest_6_.rest_5_
  15.9 0.0 copy-done
  16.0 1.2 %near.1 = (f32[2,2,128,128]{3,2,1,0:T(8,128)S(1)}, bf16[2,2,128,128]{3,2,1,0:T(8,128)(2,1)S(1)}) custom-call(s32[8]{0:T(128)S(1)} %copy-done.3, s32[8]{0:T(128)S(1)} %copy-done.4, s32[4,8]{1,0:T(4,128)S(1)} %copy-done.2, bf16[2,8,128,128]{3,2,1,0:T(8,128)(2,1)S(1)} %copy-done, bf16[4,2,128,128]{3,2,1,0:T(8,128)(2,1)S(1)} %copy-done.1, ...), custom_call_target="tpu_custom_call" | custom-call | flops 536870912 | bytes 1048576 | tf_op jit(solution)/shard_map/near/pallas_call | solution.py:246
  17.2 1.6 %collective-permute-start.7 = (bf16[2,2,128,128]{3,2,1,0:T(8,128)(2,1)S(1)}, bf16[2,2,128,128]{3,2,1,0:T(8,128)(2,1)S(1)}, u32[]{:S(2)}, u32[]{:S(2)}) collective-permute-start(bf16[2,2,128,128]{3,2,1,0:T(8,128)(2,1)S(1)} %get-tuple-element.19), channel_id=1, source_target_pairs={{0,2},{1,3},{2,0},{3,1},{4,6},{5,7},{6,4},{7,5},{8,10},{9,11},{10,... | collective-permute-start | bytes 393224 | tf_op jit(solution)/shard_map/ppermute | solution.py:209
  18.8 0.6 %collective-permute-done.6.psi_ref = bf16[2,2,128,128]{3,2,1,0:T(8,128)(2,1)S(1)} collective-permute-done((bf16[2,2,128,128]{3,2,1,0:T(8,128)(2,1)S(1)}, bf16[2,2,128,128]{3,2,1,0:T(8,128)(2,1)S(1)}, u32[]{:S(2)}, u32[]{:S(2)}) %collective-permute-start.6) | collective-permute-done | bytes 131104 | tf_op jit(solution)/shard_map/ppermute | solution.py:217
  19.3 0.6 %mask.1.rest_6_ = bf16[2,128,256]{2,1,0:T(8,128)(2,1)S(1)} custom-call(s32[8]{0:T(128)S(1)} %copy-done.3, s32[8]{0:T(128)S(1)} %copy-done.4, bf16[2,2,128,128]{3,2,1,0:T(8,128)(2,1)S(1)} %collective-permute-done.6.psi_ref), custom_call_target="tpu_custom_call" | custom-call | flops 536870912 | bytes 1048576 | tf_op jit(solution)/shard_map/mask/pallas_call | solution.py:246
  19.9 0.0 collective-permute-done.4.rest_2_
  19.9 0.0 collective-permute-done.5.rest_3_
  20.0 1.2 %far.1 = (f32[2,2,128,128]{3,2,1,0:T(8,128)S(1)}, bf16[2,2,128,128]{3,2,1,0:T(8,128)(2,1)S(1)}) custom-call(s32[8]{0:T(128)S(1)} %copy-done.3, s32[8]{0:T(128)S(1)} %copy-done.4, bf16[528,128]{1,0:T(8,128)(2,1)S(1)} %collective-permute-done.1.rest_3_.rest_0_, bf16[528,128]{1,0:T(8,128)(2,1)S(1)} %collective-permute-done.2.rest_4_.rest_1_, ...), custom_call_target="tpu_custom_call" | custom-call | flops 536870912 | bytes 1048576 | tf_op jit(solution)/shard_map/far/pallas_call | solution.py:246
  21.2 3.4 %collective-permute-start.8 = (bf16[2,2,128,128]{3,2,1,0:T(8,128)(2,1)S(1)}, bf16[2,2,128,128]{3,2,1,0:T(8,128)(2,1)S(1)}, u32[]{:S(2)}, u32[]{:S(2)}) collective-permute-start(bf16[2,2,128,128]{3,2,1,0:T(8,128)(2,1)S(1)} %get-tuple-element.22), channel_id=1, source_target_pairs={{0,2},{1,3},{4,6},{5,7},{10,8},{11,9},{14,12},{15,13},{16,18},{17,... | collective-permute-start | bytes 393224 | tf_op jit(solution)/shard_map/ppermute | solution.py:277
  24.6 0.0 collective-permute-done.7
  24.6 3.0 %collective-permute-done.8 = bf16[2,2,128,128]{3,2,1,0:T(8,128)(2,1)S(1)} collective-permute-done((bf16[2,2,128,128]{3,2,1,0:T(8,128)(2,1)S(1)}, bf16[2,2,128,128]{3,2,1,0:T(8,128)(2,1)S(1)}, u32[]{:S(2)}, u32[]{:S(2)}) %collective-permute-start.8) | collective-permute-done | bytes 131104 | tf_op jit(solution)/shard_map/ppermute | solution.py:277
  27.7 0.7 %add_convert_fusion = bf16[2,2,128,128]{3,2,1,0:T(8,128)(2,1)} fusion(f32[2,2,128,128]{3,2,1,0:T(8,128)S(1)} %get-tuple-element.17, f32[2,2,128,128]{3,2,1,0:T(8,128)S(1)} %get-tuple-element.21, bf16[2,2,128,128]{3,2,1,0:T(8,128)(2,1)S(1)} %collective-permute-done.7, bf16[2,2,128,128]{3,2,1,0:T(8,128)(2,1)S(1)} %collective-permute-done.8, pred[]{:T(512)S(6)} %eq.3), kind=kLoop, calls=%fused_computation | loop fusion | flops 327680 | bytes 917505 | tf_op jit(solution)/shard_map/convert_element_type | solution.py:281
  (9 shorter events, 0.0 us)
Async XLA Ops:
  0.0 15.9 %copy-start = (bf16[2,8,128,128]{3,2,1,0:T(8,128)(2,1)S(1)}, bf16[2,8,128,128]{3,2,1,0:T(8,128)(2,1)}, u32[]{:S(2)}) copy-start(bf16[2,8,128,128]{3,2,1,0:T(8,128)(2,1)} %rest_0_.1) | copy-start | bytes 1572868
  0.0 15.9 %copy-start.1 = (bf16[4,2,128,128]{3,2,1,0:T(8,128)(2,1)S(1)}, bf16[4,2,128,128]{3,2,1,0:T(8,128)(2,1)}, u32[]{:S(2)}) copy-start(bf16[4,2,128,128]{3,2,1,0:T(8,128)(2,1)} %rest_1_.1) | copy-start | bytes 786436
  2.0 13.9 %collective-permute-start.3 = (bf16[4,2,128,128]{3,2,1,0:T(8,128)(2,1)S(1)}, bf16[4,2,128,128]{3,2,1,0:T(8,128)(2,1)S(1)}, u32[]{:S(2)}, u32[]{:S(2)}) collective-permute-start(bf16[4,2,128,128]{3,2,1,0:T(8,128)(2,1)S(1)} %get-tuple-element.16.rest_5_.rest_4_), channel_id=1, source_target_pairs={{0,1},{1,0},{2,3},{3,2},{4,5},{5,4},{6,7},{7,6},{8,9},{9,8},{10,11... | collective-permute-start | bytes 786440 | tf_op jit(solution)/shard_map/ppermute | solution.py:209
  2.6 13.4 %copy-start.2 = (s32[4,8]{1,0:T(4,128)S(1)}, s32[4,8]{1,0:T(4,128)}, u32[]{:S(2)}) copy-start(s32[4,8]{1,0:T(4,128)} %blocks_ref.3) | copy-start | bytes 388
  2.6 8.2 %collective-permute-start.1 = (bf16[528,128]{1,0:T(8,128)(2,1)S(1)}, bf16[528,128]{1,0:T(8,128)(2,1)S(1)}, u32[]{:S(2)}, u32[]{:S(2)}) collective-permute-start(bf16[528,128]{1,0:T(8,128)(2,1)S(1)} %get-tuple-element.15), channel_id=1, source_target_pairs={{0,8},{1,4},{2,10},{3,6},{4,1},{5,13},{6,3},{7,15},{8,0},{9,12},{1... | collective-permute-start | bytes 405512 | tf_op jit(solution)/shard_map/ppermute | solution.py:217
  6.2 6.4 %collective-permute-start.2 = (bf16[528,128]{1,0:T(8,128)(2,1)S(1)}, bf16[528,128]{1,0:T(8,128)(2,1)S(1)}, u32[]{:S(2)}, u32[]{:S(2)}) collective-permute-start(bf16[528,128]{1,0:T(8,128)(2,1)S(1)} %get-tuple-element.15), channel_id=1, source_target_pairs={{0,4},{1,8},{2,6},{3,10},{4,13},{5,1},{6,15},{7,3},{8,12},{9,0},{1... | collective-permute-start | bytes 405512 | tf_op jit(solution)/shard_map/ppermute | solution.py:217
  6.2 9.7 %copy-start.3 = (s32[8]{0:T(128)S(1)}, s32[8]{0:T(128)}, u32[]{:S(2)}) copy-start(s32[8]{0:T(128)} %lsize_ref.5) | copy-start | bytes 100
  6.2 9.7 %copy-start.4 = (s32[8]{0:T(128)S(1)}, s32[8]{0:T(128)}, u32[]{:S(2)}) copy-start(s32[8]{0:T(128)} %rsize_ref.5) | copy-start | bytes 100
  6.2 9.7 %collective-permute-start = (bf16[528,128]{1,0:T(8,128)(2,1)S(1)}, bf16[528,128]{1,0:T(8,128)(2,1)S(1)}, u32[]{:S(2)}, u32[]{:S(2)}) collective-permute-start(bf16[528,128]{1,0:T(8,128)(2,1)S(1)} %get-tuple-element.14), channel_id=1, source_target_pairs={{0,4},{1,0},{2,6},{3,2},{4,5},{5,1},{6,7},{7,3},{8,12},{9,8},{10,1... | collective-permute-start | bytes 405512 | tf_op jit(solution)/shard_map/ppermute | solution.py:217
  7.9 11.4 %collective-permute-start.6 = (bf16[2,2,128,128]{3,2,1,0:T(8,128)(2,1)S(1)}, bf16[2,2,128,128]{3,2,1,0:T(8,128)(2,1)S(1)}, u32[]{:S(2)}, u32[]{:S(2)}) collective-permute-start(bf16[2,2,128,128]{3,2,1,0:T(8,128)(2,1)S(1)} %get-tuple-element.18), channel_id=1, source_target_pairs={{0,8},{1,12},{2,10},{3,14},{4,9},{5,13},{6,11},{7,15},{8,0},{9,4},... | collective-permute-start | bytes 393224 | tf_op jit(solution)/shard_map/ppermute | solution.py:217
  10.8 9.2 %collective-permute-start.4 = (bf16[528,128]{1,0:T(8,128)(2,1)S(1)}, bf16[528,128]{1,0:T(8,128)(2,1)S(1)}, u32[]{:S(2)}, u32[]{:S(2)}) collective-permute-start(bf16[528,128]{1,0:T(8,128)(2,1)S(1)} %collective-permute-done.1.rest_3_.rest_0_), channel_id=1, source_target_pairs={{0,4},{1,0},{2,6},{3,2},{4,5},{5,1},{6,7},{7,3},{8,12},{9,8},{10,1... | collective-permute-start | bytes 405512 | tf_op jit(solution)/shard_map/ppermute | solution.py:217
  12.6 7.3 %collective-permute-start.5 = (bf16[528,128]{1,0:T(8,128)(2,1)S(1)}, bf16[528,128]{1,0:T(8,128)(2,1)S(1)}, u32[]{:S(2)}, u32[]{:S(2)}) collective-permute-start(bf16[528,128]{1,0:T(8,128)(2,1)S(1)} %collective-permute-done.2.rest_4_.rest_1_), channel_id=1, source_target_pairs={{0,4},{1,0},{2,6},{3,2},{4,5},{5,1},{6,7},{7,3},{8,12},{9,8},{10,1... | collective-permute-start | bytes 405512 | tf_op jit(solution)/shard_map/ppermute | solution.py:217
  17.2 7.4 %collective-permute-start.7 = (bf16[2,2,128,128]{3,2,1,0:T(8,128)(2,1)S(1)}, bf16[2,2,128,128]{3,2,1,0:T(8,128)(2,1)S(1)}, u32[]{:S(2)}, u32[]{:S(2)}) collective-permute-start(bf16[2,2,128,128]{3,2,1,0:T(8,128)(2,1)S(1)} %get-tuple-element.19), channel_id=1, source_target_pairs={{0,2},{1,3},{2,0},{3,1},{4,6},{5,7},{6,4},{7,5},{8,10},{9,11},{10,... | collective-permute-start | bytes 393224 | tf_op jit(solution)/shard_map/ppermute | solution.py:209
  21.2 6.5 %collective-permute-start.8 = (bf16[2,2,128,128]{3,2,1,0:T(8,128)(2,1)S(1)}, bf16[2,2,128,128]{3,2,1,0:T(8,128)(2,1)S(1)}, u32[]{:S(2)}, u32[]{:S(2)}) collective-permute-start(bf16[2,2,128,128]{3,2,1,0:T(8,128)(2,1)S(1)} %get-tuple-element.22), channel_id=1, source_target_pairs={{0,2},{1,3},{4,6},{5,7},{10,8},{11,9},{14,12},{15,13},{16,18},{17,... | collective-permute-start | bytes 393224 | tf_op jit(solution)/shard_map/ppermute | solution.py:277

commit v5 on v2

--- a/solution.py
+++ b/solution.py
@@ -267,9 +267,10 @@
         near_kernel, "near", [total], sizes + (term_blocks,),
         [psi, left_ops, side, direct_a, direct_b] + rights,
     )
+    other_turn, near = lax.optimization_barrier((far_other, near))
     (wide,) = apply(
         mask_kernel, "mask", [block((sectors, tile, sectors * tile))], sizes,
-        [far_same, far_other],
+        [far_same, other_turn],
     )
     sent, far = apply(
         far_kernel, "far", [block(out_shape), total], sizes,

time: 30.2 us -> 28.4 us (0.940)
  waiting for transfers between devices: 10.7 us -> 7.81 us
  starting transfers between devices: 13.6 us -> 14.6 us
    ppermute x6, waiting for transfers between devices: 5.52 us -> 1.79 us  [over_z(): return lax.ppermute(array, ('blk', 'op'), pairs)]
    ppermute x3, waiting for transfers between devices: 5.21 us -> 6.02 us  [over_op(): return lax.ppermute(array, 'op', [(o, o ^ step) for o in range(n)])]
    ppermute x3, starting transfers between devices: 3.02 us -> 3.71 us  [over_op(): return lax.ppermute(array, 'op', [(o, o ^ step) for o in range(n)])]
    ppermute x6, starting transfers between devices: 10.6 us -> 10.9 us  [over_z(): return lax.ppermute(array, ('blk', 'op'), pairs)]
  transfers between devices with their start and end apart: 9 -> 9, of which waited for: 4 -> 4; matrix products, arithmetic and copies ran while one was open for 0% -> 0% of each run, Pallas kernels for 6% -> 7%
where the time goes in v5:
time: 28.4 us; the launch traced here: 28.2 us
  starting transfers between devices  14.6 us (51%)
  waiting for transfers between devices  7.81 us (28%)
  Pallas kernels  5.05 us (18%)
  other arithmetic  0.69 us (2%)
    ppermute x6, starting transfers between devices, over_z(): return lax.ppermute(array, ('blk', 'op'), pairs)  10.9 us
    ppermute x3, waiting for transfers between devices, over_op(): return lax.ppermute(array, 'op', [(o, o ^ step) for o in range(n)])  6.02 us
    ppermute x3, starting transfers between devices, over_op(): return lax.ppermute(array, 'op', [(o, o ^ step) for o in range(n)])  3.71 us
    pallas_call x3, Pallas kernels, apply(): pl.pallas_call(kernel, out_shape=outs, in_specs=[SMEM] * len(scalars) + [...  3.05 us
    pallas_call x1, Pallas kernels, shards(): pl.pallas_call(pack_kernel, out_shape=[block(message_shape), block(messag...  2 us
    ppermute x6, waiting for transfers between devices, over_z(): return lax.ppermute(array, ('blk', 'op'), pairs)  1.79 us
    convert_element_type x1, other arithmetic, shards(): return (kept + arrived.astype(jnp.float32)).astype(jnp.bfloat16)  0.69 us
  transfers between devices with their start and end apart: 9, of which 4 were waited for; matrix products, arithmetic and copies ran while one was open for 0% of the time, Pallas kernels for 7%

profile of v5, /device:TPU:0, one launch (start us, length us, event | category | flops | bytes accessed | tf_op | source)
XLA Modules:
  0.0 28.2 jit_solution(9929457884253966034)
XLA Ops:
  0.0 2.0 %pack.1 = (bf16[528,128]{1,0:T(8,128)(2,1)S(1)}, bf16[528,128]{1,0:T(8,128)(2,1)S(1)}, bf16[2,128,128]{2,1,0:T(8,128)(2,1)S(1)}, bf16[4,2,128,128]{3,2,1,0:T(8,128)(2,1)S(1)}) custom-call(s32[4,8]{1,0:T(4,128)} %blocks_ref.3, bf16[2,8,128,128]{3,2,1,0:T(8,128)(2,1)} %rest_0_.1, bf16[4,2,128,128]{3,2,1,0:T(8,128)(2,1)} %rest_1_.1, ...), custom_call_target="tpu_custom_call" | custom-call | tf_op jit(solution)/shard_map/pack/pallas_call | solution.py:227
  2.0 0.5 %collective-permute-start.5 = (bf16[4,2,128,128]{3,2,1,0:T(8,128)(2,1)S(1)}, bf16[4,2,128,128]{3,2,1,0:T(8,128)(2,1)S(1)}, u32[]{:S(2)}, u32[]{:S(2)}) collective-permute-start(bf16[4,2,128,128]{3,2,1,0:T(8,128)(2,1)S(1)} %get-tuple-element.16.rest_5_.rest_4_), channel_id=1, source_target_pairs={{0,1},{1,0},{2,3},{3,2},{4,5},{5,4},{6,7},{7,6},{8,9},{9,8},{10,11... | collective-permute-start | bytes 786440 | tf_op jit(solution)/shard_map/ppermute | solution.py:213
  2.5 3.7 %collective-permute-start.3 = (bf16[528,128]{1,0:T(8,128)(2,1)S(1)}, bf16[528,128]{1,0:T(8,128)(2,1)S(1)}, u32[]{:S(2)}, u32[]{:S(2)}) collective-permute-start(bf16[528,128]{1,0:T(8,128)(2,1)S(1)} %get-tuple-element.15), channel_id=1, source_target_pairs={{0,8},{1,4},{2,10},{3,6},{4,1},{5,13},{6,3},{7,15},{8,0},{9,12},{1... | collective-permute-start | bytes 405512 | tf_op jit(solution)/shard_map/ppermute | solution.py:221
  6.2 0.0 collective-permute-start.4
  6.2 1.7 %collective-permute-start.2 = (bf16[528,128]{1,0:T(8,128)(2,1)S(1)}, bf16[528,128]{1,0:T(8,128)(2,1)S(1)}, u32[]{:S(2)}, u32[]{:S(2)}) collective-permute-start(bf16[528,128]{1,0:T(8,128)(2,1)S(1)} %get-tuple-element.14), channel_id=1, source_target_pairs={{0,4},{1,0},{2,6},{3,2},{4,5},{5,1},{6,7},{7,3},{8,12},{9,8},{10,1... | collective-permute-start | bytes 405512 | tf_op jit(solution)/shard_map/ppermute | solution.py:221
  7.9 2.6 %collective-permute-start = (bf16[2,128,128]{2,1,0:T(8,128)(2,1)S(1)}, bf16[2,128,128]{2,1,0:T(8,128)(2,1)S(1)}, u32[]{:S(2)}, u32[]{:S(2)}) collective-permute-start(bf16[2,128,128]{2,1,0:T(8,128)(2,1)S(1)} %get-tuple-element.13), channel_id=1, source_target_pairs={{0,8},{1,12},{2,10},{3,14},{4,9},{5,13},{6,11},{7,15},{8,0},{9,4},... | collective-permute-start | bytes 196616 | tf_op jit(solution)/shard_map/ppermute | solution.py:221
  10.5 0.3 %collective-permute-done.3.rest_3_.rest_0_ = bf16[528,128]{1,0:T(8,128)(2,1)S(1)} collective-permute-done((bf16[528,128]{1,0:T(8,128)(2,1)S(1)}, bf16[528,128]{1,0:T(8,128)(2,1)S(1)}, u32[]{:S(2)}, u32[]{:S(2)}) %collective-permute-start.3) | collective-permute-done | bytes 135200 | tf_op jit(solution)/shard_map/ppermute | solution.py:221
  10.8 0.0 collective-permute-start.6
  10.8 1.5 %collective-permute-done.4.rest_4_.rest_1_ = bf16[528,128]{1,0:T(8,128)(2,1)S(1)} collective-permute-done((bf16[528,128]{1,0:T(8,128)(2,1)S(1)}, bf16[528,128]{1,0:T(8,128)(2,1)S(1)}, u32[]{:S(2)}, u32[]{:S(2)}) %collective-permute-start.4) | collective-permute-done | bytes 135200 | tf_op jit(solution)/shard_map/ppermute | solution.py:221
  12.2 3.0 %collective-permute-start.7 = (bf16[528,128]{1,0:T(8,128)(2,1)S(1)}, bf16[528,128]{1,0:T(8,128)(2,1)S(1)}, u32[]{:S(2)}, u32[]{:S(2)}) collective-permute-start(bf16[528,128]{1,0:T(8,128)(2,1)S(1)} %collective-permute-done.4.rest_4_.rest_1_), channel_id=1, source_target_pairs={{0,4},{1,0},{2,6},{3,2},{4,5},{5,1},{6,7},{7,3},{8,12},{9,8},{10,1... | collective-permute-start | bytes 405512 | tf_op jit(solution)/shard_map/ppermute | solution.py:221
  15.2 0.0 collective-permute-done.psi_same
  15.2 1.6 %collective-permute-start.1 = (bf16[2,128,128]{2,1,0:T(8,128)(2,1)S(1)}, bf16[2,128,128]{2,1,0:T(8,128)(2,1)S(1)}, u32[]{:S(2)}, u32[]{:S(2)}) collective-permute-start(bf16[2,128,128]{2,1,0:T(8,128)(2,1)S(1)} %collective-permute-done.psi_same), channel_id=1, source_target_pairs={{0,2},{1,3},{2,0},{3,1},{4,6},{5,7},{6,4},{7,5},{8,10},{9,11},{10,... | collective-permute-start | bytes 196616 | tf_op jit(solution)/shard_map/ppermute | solution.py:213
  16.7 0.0 collective-permute-done.2.rest_2_
  16.8 0.0 collective-permute-done.5.rest_6_.rest_5_
  16.8 0.0 copy-done
  16.8 1.2 %near.1.rest_6_ = f32[2,2,128,128]{3,2,1,0:T(8,128)S(1)} custom-call(s32[8]{0:T(128)S(1)} %copy-done.3, s32[8]{0:T(128)S(1)} %copy-done.4, s32[4,8]{1,0:T(4,128)S(1)} %copy-done.2, bf16[2,8,128,128]{3,2,1,0:T(8,128)(2,1)S(1)} %copy-done, bf16[4,2,128,128]{3,2,1,0:T(8,128)(2,1)S(1)} %copy-done.1, bf16[528,128]{1,0:T(8,128)(2,1)S(1)} %collective-permute-done.2.rest_2_, ...), custom_call_target="tpu_custom_call" | custom-call | flops 536870912 | bytes 1048576 | tf_op jit(solution)/shard_map/near/pallas_call | solution.py:251
  18.0 2.1 %collective-permute-done.1.psi_other = bf16[2,128,128]{2,1,0:T(8,128)(2,1)S(1)} collective-permute-done((bf16[2,128,128]{2,1,0:T(8,128)(2,1)S(1)}, bf16[2,128,128]{2,1,0:T(8,128)(2,1)S(1)}, u32[]{:S(2)}, u32[]{:S(2)}) %collective-permute-start.1) | collective-permute-done | bytes 65568 | tf_op jit(solution)/shard_map/ppermute | solution.py:213
  20.1 0.6 %mask.1.rest_7_ = bf16[2,128,256]{2,1,0:T(8,128)(2,1)S(1)} custom-call(s32[8]{0:T(128)S(1)} %copy-done.3, s32[8]{0:T(128)S(1)} %copy-done.4, bf16[2,128,128]{2,1,0:T(8,128)(2,1)S(1)} %collective-permute-done.psi_same, bf16[2,128,128]{2,1,0:T(8,128)(2,1)S(1)} %collective-permute-done.1.psi_other), custom_call_target="tpu_custom_call" | custom-call | flops 536870912 | bytes 1048576 | tf_op jit(solution)/shard_map/mask/pallas_call | solution.py:251
  20.7 0.0 collective-permute-done.6.rest_2_
  20.7 0.0 collective-permute-done.7.rest_3_
  20.7 1.2 %far.1 = (bf16[2,2,128,128]{3,2,1,0:T(8,128)(2,1)S(1)}, f32[2,2,128,128]{3,2,1,0:T(8,128)S(1)}) custom-call(s32[8]{0:T(128)S(1)} %copy-done.3, s32[8]{0:T(128)S(1)} %copy-done.4, bf16[528,128]{1,0:T(8,128)(2,1)S(1)} %collective-permute-done.3.rest_3_.rest_0_, bf16[528,128]{1,0:T(8,128)(2,1)S(1)} %collective-permute-done.4.rest_4_.rest_1_, ...), custom_call_target="tpu_custom_call" | custom-call | flops 536870912 | bytes 1048576 | tf_op jit(solution)/shard_map/far/pallas_call | solution.py:251
  22.0 1.6 %collective-permute-start.8 = (bf16[2,2,128,128]{3,2,1,0:T(8,128)(2,1)S(1)}, bf16[2,2,128,128]{3,2,1,0:T(8,128)(2,1)S(1)}, u32[]{:S(2)}, u32[]{:S(2)}) collective-permute-start(bf16[2,2,128,128]{3,2,1,0:T(8,128)(2,1)S(1)} %get-tuple-element.20), channel_id=1, source_target_pairs={{0,2},{1,3},{2,0},{3,1},{4,6},{5,7},{6,4},{7,5},{8,10},{9,11},{10,... | collective-permute-start | bytes 393224 | tf_op jit(solution)/shard_map/ppermute | solution.py:213
  23.6 4.0 %collective-permute-done.8 = bf16[2,2,128,128]{3,2,1,0:T(8,128)(2,1)S(1)} collective-permute-done((bf16[2,2,128,128]{3,2,1,0:T(8,128)(2,1)S(1)}, bf16[2,2,128,128]{3,2,1,0:T(8,128)(2,1)S(1)}, u32[]{:S(2)}, u32[]{:S(2)}) %collective-permute-start.8) | collective-permute-done | bytes 131104 | tf_op jit(solution)/shard_map/ppermute | solution.py:213
  27.5 0.7 %add_convert_fusion = bf16[2,2,128,128]{3,2,1,0:T(8,128)(2,1)} fusion(bf16[2,2,128,128]{3,2,1,0:T(8,128)(2,1)S(1)} %collective-permute-done.8, f32[2,2,128,128]{3,2,1,0:T(8,128)S(1)} %near.1.rest_6_, f32[2,2,128,128]{3,2,1,0:T(8,128)S(1)} %get-tuple-element.19, pred[]{:T(512)S(6)} %eq.3), kind=kLoop, calls=%fused_computation | loop fusion | flops 262144 | bytes 786433 | tf_op jit(solution)/shard_map/convert_element_type | solution.py:281
  (9 shorter events, 0.0 us)
Async XLA Ops:
  0.0 16.8 %copy-start = (bf16[2,8,128,128]{3,2,1,0:T(8,128)(2,1)S(1)}, bf16[2,8,128,128]{3,2,1,0:T(8,128)(2,1)}, u32[]{:S(2)}) copy-start(bf16[2,8,128,128]{3,2,1,0:T(8,128)(2,1)} %rest_0_.1) | copy-start | bytes 1572868
  0.0 16.8 %copy-start.1 = (bf16[4,2,128,128]{3,2,1,0:T(8,128)(2,1)S(1)}, bf16[4,2,128,128]{3,2,1,0:T(8,128)(2,1)}, u32[]{:S(2)}) copy-start(bf16[4,2,128,128]{3,2,1,0:T(8,128)(2,1)} %rest_1_.1) | copy-start | bytes 786436
  2.0 14.7 %collective-permute-start.5 = (bf16[4,2,128,128]{3,2,1,0:T(8,128)(2,1)S(1)}, bf16[4,2,128,128]{3,2,1,0:T(8,128)(2,1)S(1)}, u32[]{:S(2)}, u32[]{:S(2)}) collective-permute-start(bf16[4,2,128,128]{3,2,1,0:T(8,128)(2,1)S(1)} %get-tuple-element.16.rest_5_.rest_4_), channel_id=1, source_target_pairs={{0,1},{1,0},{2,3},{3,2},{4,5},{5,4},{6,7},{7,6},{8,9},{9,8},{10,11... | collective-permute-start | bytes 786440 | tf_op jit(solution)/shard_map/ppermute | solution.py:213
  2.5 14.2 %copy-start.2 = (s32[4,8]{1,0:T(4,128)S(1)}, s32[4,8]{1,0:T(4,128)}, u32[]{:S(2)}) copy-start(s32[4,8]{1,0:T(4,128)} %blocks_ref.3) | copy-start | bytes 388
  2.5 8.2 %collective-permute-start.3 = (bf16[528,128]{1,0:T(8,128)(2,1)S(1)}, bf16[528,128]{1,0:T(8,128)(2,1)S(1)}, u32[]{:S(2)}, u32[]{:S(2)}) collective-permute-start(bf16[528,128]{1,0:T(8,128)(2,1)S(1)} %get-tuple-element.15), channel_id=1, source_target_pairs={{0,8},{1,4},{2,10},{3,6},{4,1},{5,13},{6,3},{7,15},{8,0},{9,12},{1... | collective-permute-start | bytes 405512 | tf_op jit(solution)/shard_map/ppermute | solution.py:221
  6.2 6.0 %collective-permute-start.4 = (bf16[528,128]{1,0:T(8,128)(2,1)S(1)}, bf16[528,128]{1,0:T(8,128)(2,1)S(1)}, u32[]{:S(2)}, u32[]{:S(2)}) collective-permute-start(bf16[528,128]{1,0:T(8,128)(2,1)S(1)} %get-tuple-element.15), channel_id=1, source_target_pairs={{0,4},{1,8},{2,6},{3,10},{4,13},{5,1},{6,15},{7,3},{8,12},{9,0},{1... | collective-permute-start | bytes 405512 | tf_op jit(solution)/shard_map/ppermute | solution.py:221
  6.2 10.6 %copy-start.3 = (s32[8]{0:T(128)S(1)}, s32[8]{0:T(128)}, u32[]{:S(2)}) copy-start(s32[8]{0:T(128)} %lsize_ref.5) | copy-start | bytes 100
  6.2 10.6 %copy-start.4 = (s32[8]{0:T(128)S(1)}, s32[8]{0:T(128)}, u32[]{:S(2)}) copy-start(s32[8]{0:T(128)} %rsize_ref.5) | copy-start | bytes 100
  6.2 10.5 %collective-permute-start.2 = (bf16[528,128]{1,0:T(8,128)(2,1)S(1)}, bf16[528,128]{1,0:T(8,128)(2,1)S(1)}, u32[]{:S(2)}, u32[]{:S(2)}) collective-permute-start(bf16[528,128]{1,0:T(8,128)(2,1)S(1)} %get-tuple-element.14), channel_id=1, source_target_pairs={{0,4},{1,0},{2,6},{3,2},{4,5},{5,1},{6,7},{7,3},{8,12},{9,8},{10,1... | collective-permute-start | bytes 405512 | tf_op jit(solution)/shard_map/ppermute | solution.py:221
  7.9 7.3 %collective-permute-start = (bf16[2,128,128]{2,1,0:T(8,128)(2,1)S(1)}, bf16[2,128,128]{2,1,0:T(8,128)(2,1)S(1)}, u32[]{:S(2)}, u32[]{:S(2)}) collective-permute-start(bf16[2,128,128]{2,1,0:T(8,128)(2,1)S(1)} %get-tuple-element.13), channel_id=1, source_target_pairs={{0,8},{1,12},{2,10},{3,14},{4,9},{5,13},{6,11},{7,15},{8,0},{9,4},... | collective-permute-start | bytes 196616 | tf_op jit(solution)/shard_map/ppermute | solution.py:221
  10.8 10.0 %collective-permute-start.6 = (bf16[528,128]{1,0:T(8,128)(2,1)S(1)}, bf16[528,128]{1,0:T(8,128)(2,1)S(1)}, u32[]{:S(2)}, u32[]{:S(2)}) collective-permute-start(bf16[528,128]{1,0:T(8,128)(2,1)S(1)} %collective-permute-done.3.rest_3_.rest_0_), channel_id=1, source_target_pairs={{0,4},{1,0},{2,6},{3,2},{4,5},{5,1},{6,7},{7,3},{8,12},{9,8},{10,1... | collective-permute-start | bytes 405512 | tf_op jit(solution)/shard_map/ppermute | solution.py:221
  12.2 8.5 %collective-permute-start.7 = (bf16[528,128]{1,0:T(8,128)(2,1)S(1)}, bf16[528,128]{1,0:T(8,128)(2,1)S(1)}, u32[]{:S(2)}, u32[]{:S(2)}) collective-permute-start(bf16[528,128]{1,0:T(8,128)(2,1)S(1)} %collective-permute-done.4.rest_4_.rest_1_), channel_id=1, source_target_pairs={{0,4},{1,0},{2,6},{3,2},{4,5},{5,1},{6,7},{7,3},{8,12},{9,8},{10,1... | collective-permute-start | bytes 405512 | tf_op jit(solution)/shard_map/ppermute | solution.py:221
  15.2 4.9 %collective-permute-start.1 = (bf16[2,128,128]{2,1,0:T(8,128)(2,1)S(1)}, bf16[2,128,128]{2,1,0:T(8,128)(2,1)S(1)}, u32[]{:S(2)}, u32[]{:S(2)}) collective-permute-start(bf16[2,128,128]{2,1,0:T(8,128)(2,1)S(1)} %collective-permute-done.psi_same), channel_id=1, source_target_pairs={{0,2},{1,3},{2,0},{3,1},{4,6},{5,7},{6,4},{7,5},{8,10},{9,11},{10,... | collective-permute-start | bytes 196616 | tf_op jit(solution)/shard_map/ppermute | solution.py:213
  22.0 5.6 %collective-permute-start.8 = (bf16[2,2,128,128]{3,2,1,0:T(8,128)(2,1)S(1)}, bf16[2,2,128,128]{3,2,1,0:T(8,128)(2,1)S(1)}, u32[]{:S(2)}, u32[]{:S(2)}) collective-permute-start(bf16[2,2,128,128]{3,2,1,0:T(8,128)(2,1)S(1)} %get-tuple-element.20), channel_id=1, source_target_pairs={{0,2},{1,3},{2,0},{3,1},{4,6},{5,7},{6,4},{7,5},{8,10},{9,11},{10,... | collective-permute-start | bytes 393224 | tf_op jit(solution)/shard_map/ppermute | solution.py:213

commit v6 on v3

--- a/solution.py
+++ b/solution.py
@@ -12,6 +12,7 @@
 VMEM = pl.BlockSpec(memory_space=pltpu.VMEM)
 PARAMS = pltpu.CompilerParams(vmem_limit_bytes=32 * 1024 * 1024)
 ID_ROWS = 16
+TERMS = 4
 
 
 def acting_terms(blocks_ref, sector):
@@ -35,42 +36,39 @@
 
 
 def pack_kernel(blocks_ref, psi_ref, left_ref, right_ref, *rest):
-    left_out, side_out, far_out, right_out, sem = rest
+    left_out, both_out, swap_out, far_out, sem = rest
     z, _, _ = place()
     sectors, tile = psi_ref.shape[0], psi_ref.shape[-1]
     count = 2 * sectors
+    begin = right_ref.shape[0]
+    copies = []
+
+    def bring(source, out, spot, rows):
+        copies.append(
+            pltpu.make_async_copy(source, out.at[pl.ds(spot, rows)], sem.at[len(copies)])
+        )
+
+    bring(right_ref, swap_out, 0, begin)
     row = lax.broadcasted_iota(jnp.int32, (ID_ROWS, tile), 0)
     ids = jnp.zeros((ID_ROWS, tile), jnp.float32)
-    picked = []
     for local in range(sectors):
-        for term in acting_terms(blocks_ref, z * sectors + local):
-            ids = jnp.where(row == len(picked), term.astype(jnp.float32), ids)
-            picked.append(left_ref.at[term, local])
-    near = jnp.bitwise_xor(z, 1) * sectors
-    asked = [psi_ref.at[a, near + b] for a in range(sectors) for b in range(sectors)]
-
-    def copies(sources, out, first):
-        return [
-            pltpu.make_async_copy(source, out.at[pl.ds(spot * tile, tile)], sem.at[first + spot])
-            for spot, source in enumerate(sources)
-        ]
-
-    far = pl.ds(jnp.bitwise_xor(z, jnp.where(is_home(), 2, 3)) * sectors, sectors)
-    plain = copies(picked, left_out, 0)
-    plain.append(pltpu.make_async_copy(psi_ref.at[:, far], far_out, sem.at[2 * count]))
-    plain.append(pltpu.make_async_copy(right_ref, right_out, sem.at[2 * count + 1]))
-    for copy in plain:
+        for slot, term in enumerate(acting_terms(blocks_ref, z * sectors + local)):
+            spot = 2 * local + slot
+            ids = jnp.where(row == spot, term.astype(jnp.float32), ids)
+            for out, first in ((left_out, 0), (both_out, 0), (swap_out, begin)):
+                bring(left_ref.at[term, local], out, first + spot * tile, tile)
+    beside = jnp.bitwise_xor(z, jnp.where(is_home(), 1, 2)) * sectors
+    far = jnp.bitwise_xor(z, 3) * sectors
+    for a in range(sectors):
+        for b in range(sectors):
+            spot = (sectors * a + b) * tile
+            bring(psi_ref.at[a, beside + b], both_out, count * tile + ID_ROWS + spot, tile)
+            bring(psi_ref.at[a, far + b], far_out, spot, tile)
+    for copy in copies:
         copy.start()
-    for at_home, sources in ((True, asked), (False, picked)):
-
-        @pl.when(is_home() == at_home)
-        def _(sources=sources):
-            for copy in copies(sources, side_out, count):
-                copy.start()
-
-    for out in (left_out, side_out):
-        out[pl.ds(count * tile, ID_ROWS)] = ids.astype(jnp.bfloat16)
-    for copy in plain + copies(picked, side_out, count):
+    for out, first in ((left_out, 0), (both_out, 0), (swap_out, begin)):
+        out[pl.ds(first + count * tile, ID_ROWS)] = ids.astype(jnp.bfloat16)
+    for copy in copies:
         copy.wait()
 
 
@@ -113,72 +111,81 @@
             store(b, a, jnp.where(keep, total, 0.0))
 
 
-def message(ref, right_ref):
-    terms, sectors, tile = right_ref.shape[0], right_ref.shape[1], right_ref.shape[-1]
-    ids = ref[pl.ds(2 * sectors * tile, ID_ROWS)].astype(jnp.float32)
+def message(ref, first, sectors, right_ref, terms=TERMS):
+    tile = ref.shape[-1]
+    ids = ref[pl.ds(first + 2 * sectors * tile, ID_ROWS)].astype(jnp.float32)
 
     def left(a):
-        return ref[pl.ds(2 * a * tile, 2 * tile)]
+        return ref[pl.ds(first + 2 * a * tile, 2 * tile)]
 
     def right(a, slot, b):
         spot = 2 * a + slot
         term = jnp.broadcast_to(ids[spot : spot + 1], (tile, tile))
-        block = right_ref[0, b].astype(jnp.float32)
-        for t in range(1, terms):
-            block = jnp.where(term == t, right_ref[t, b].astype(jnp.float32), block)
+        block = None
+        for t in range(terms):
+            other = right_ref[pl.ds((t * sectors + b) * tile, tile)].astype(jnp.float32)
+            block = other if block is None else jnp.where(term == t, other, block)
         return block.astype(jnp.bfloat16)
 
     return left, right
 
 
-def mask_kernel(lsize_ref, rsize_ref, psi_ref, wide_ref):
-    z, _, _ = place()
-    far = jnp.where(is_home(), 2, 3)
-    columns = range(psi_ref.shape[1])
-    for a in range(psi_ref.shape[0]):
-        blocks = [psi_ref[a, b] for b in columns]
-        wide_ref[a] = wide_psi(z, far, (lsize_ref, rsize_ref), a, columns, blocks)
-
-
-def near_kernel(lsize_ref, rsize_ref, blocks_ref, *rest):
-    psi_ref, left_ref, side, direct_a, direct_b, right_own, right_other, out_ref = rest
+def psi_rows(ref, first, a, sectors):
+    tile = ref.shape[-1]
+    return [ref[pl.ds(first + (sectors * a + b) * tile, tile)] for b in range(sectors)]
+
+
+def near_kernel(lsize_ref, rsize_ref, *rest):
+    psi_ref, left_own, swap_own, swapped, direct_a, direct_b, out_ref = rest
     z, _, _ = place()
     sectors, tile = out_ref.shape[0], out_ref.shape[-1]
     sizes, columns = (lsize_ref, rsize_ref), range(sectors)
+    begin = swap_own.shape[0] - left_own.shape[0]
 
     def store(b, a, total):
         out_ref[b, a] = total
 
-    def masked(distance, a, blocks):
-        return wide_psi(z, distance, sizes, a, columns, blocks)
-
-    @pl.when(is_home())
-    def _():
-        terms = [acting_terms(blocks_ref, z * sectors + a) for a in columns]
-        left, right = message(side, right_other)
-        partial_sums(
-            z, 0, sizes, columns,
-            lambda a: masked(0, a, [psi_ref[a, z * sectors + b] for b in columns]),
-            [lambda a: jnp.concatenate([left_ref[term, a] for term in terms[a]], axis=0), left],
-            [lambda a, slot, b: right_own[terms[a][slot], b], right],
-            store,
-        )
-
-    @pl.when(jnp.logical_not(is_home()))
-    def _():
-        lefts, rights = zip(message(direct_b, right_own), message(direct_a, right_other))
-
-        def psi(a):
-            return masked(1, a, [side[pl.ds((sectors * a + b) * tile, tile)] for b in columns])
-
-        partial_sums(z, 1, sizes, columns, psi, lefts, rights, store)
+    for at_home in (True, False):
+
+        @pl.when(is_home() == at_home)
+        def _(at_home=at_home):
+            if at_home:
+                pair = [(left_own, 0, sectors, swap_own), (swapped, begin, sectors, swapped)]
+            else:
+                pair = [(direct_b, 0, sectors, swap_own), (direct_a, 0, sectors, swapped)]
+
+            def psi(a):
+                if at_home:
+                    blocks = [psi_ref[a, z * sectors + b] for b in columns]
+                else:
+                    blocks = psi_rows(direct_b, left_own.shape[0], a, sectors)
+                return wide_psi(z, 0 if at_home else 1, sizes, a, columns, blocks)
+
+            lefts, rights = zip(*[message(*one) for one in pair])
+            distance = 0 if at_home else 1
+            partial_sums(z, distance, sizes, columns, psi, lefts, rights, store)
+
+
+def mask_kernel(lsize_ref, rsize_ref, direct_b, psi_far, wide_ref):
+    z, _, _ = place()
+    sectors = wide_ref.shape[0]
+    columns = range(sectors)
+    sizes = (lsize_ref, rsize_ref)
+    first = direct_b.shape[0] - psi_far.shape[0]
+    for at_home, distance, ref, begin in ((True, 2, direct_b, first), (False, 3, psi_far, 0)):
+
+        @pl.when(is_home() == at_home)
+        def _(distance=distance, ref=ref, begin=begin):
+            for a in columns:
+                blocks = psi_rows(ref, begin, a, sectors)
+                wide_ref[a] = wide_psi(z, distance, sizes, a, columns, blocks)
 
 
 def far_kernel(lsize_ref, rsize_ref, *rest):
-    direct_a, direct_b, passed_a, passed_b, right_own, right_other = rest[:6]
+    direct_a, direct_b, passed_a, passed_b, swap_own, swapped = rest[:6]
     near_ref, wide_ref, sent_ref, out_ref = rest[6:]
     z, x, _ = place()
-    columns = range(out_ref.shape[0])
+    sectors = out_ref.shape[0]
     far_leaves = lax.shift_right_logical(z, 1) == x
 
     def store_sent(b, a, total):
@@ -196,8 +203,9 @@
 
             @pl.when((is_home() == at_home) & (far_leaves == leaves))
             def _(store=store, distance=distance, first=first, second=second):
-                lefts, rights = zip(message(first, right_own), message(second, right_other))
-                sizes = (lsize_ref, rsize_ref)
+                pair = ((first, 0, sectors, swap_own), (second, 0, sectors, swapped))
+                lefts, rights = zip(*[message(*one) for one in pair])
+                sizes, columns = (lsize_ref, rsize_ref), range(sectors)
                 partial_sums(
                     z, distance, sizes, columns, lambda a: wide_ref[a], lefts, rights, store
                 )
@@ -208,7 +216,6 @@
     sectors, tile = psi.shape[0], psi.shape[-1]
     block = functools.partial(jax.ShapeDtypeStruct, dtype=jnp.bfloat16)
     out_shape = (sectors, sectors, tile, tile)
-    message_shape = (2 * sectors * tile + ID_ROWS, tile)
 
     def over_op(array, step):
         return lax.ppermute(array, "op", [(o, o ^ step) for o in range(n)])
@@ -221,31 +228,41 @@
                 pairs.append((z * n + o, (z ^ step) * n + (o & 2) + (z & 1)))
         return lax.ppermute(array, ("blk", "op"), pairs)
 
-    psi_hbm, left_hbm, right_hbm, blocks_hbm = [
+    def to_third(array):
+        pairs = []
+        for z in range(n):
+            for o in range(n):
+                to = (z, o) if o & 1 == z & 1 else (z ^ 3, (o & 2) + (z & 1))
+                pairs.append((z * n + o, to[0] * n + to[1]))
+        return lax.ppermute(array, ("blk", "op"), pairs)
+
+    rights = right_ops.reshape(-1, tile)
+    inputs = [
         pltpu.with_memory_space_constraint(array, pltpu.HBM)
-        for array in (psi, left_ops, right_ops, term_blocks)
+        for array in (term_blocks, psi, left_ops, rights)
     ]
-    left_sent, side_sent, far_sent, right_own = pl.pallas_call(
+    rows, right_rows = 2 * sectors * tile + ID_ROWS, rights.shape[0]
+    psi_count = sectors * sectors
+    left_sent, both_sent, swap_sent, far_sent = pl.pallas_call(
         pack_kernel,
         out_shape=[
-            block(message_shape),
-            block(message_shape),
-            block(out_shape),
-            block(right_ops.shape),
+            block((rows, tile)),
+            block((rows + psi_count * tile, tile)),
+            block((right_rows + rows, tile)),
+            block((psi_count * tile, tile)),
         ],
         in_specs=[SMEM, ANY, ANY, ANY],
         out_specs=[VMEM] * 4,
-        scratch_shapes=[pltpu.SemaphoreType.DMA((4 * sectors + 2,))],
+        scratch_shapes=[pltpu.SemaphoreType.DMA((1 + 6 * sectors + 2 * psi_count,))],
         compiler_params=PARAMS,
         name="pack",
-    )(blocks_hbm, psi_hbm, left_hbm, right_hbm)
+    )(*inputs)
     direct_a = over_z(left_sent, 2, 1)
-    direct_b = over_z(left_sent, 1, 2)
-    psi_far = over_z(far_sent, 2, 3)
-    side = over_z(side_sent, 1, 0)
+    direct_b = over_z(both_sent, 1, 2)
+    psi_far = to_third(far_sent)
+    swapped = over_op(swap_sent, 1)
     passed_a = over_z(direct_a, 1, 0)
-    passed_b = over_z(direct_b, 1, 0)
-    right_other = over_op(right_own, 1)
+    passed_b = over_z(direct_b[:rows], 1, 0)
 
     def apply(kernel, name, outs, scalars, operands):
         return pl.pallas_call(
@@ -261,20 +278,19 @@
         )(*scalars, *operands)
 
     sizes = (left_sizes, right_sizes)
-    rights = [right_own, right_other]
     total = jax.ShapeDtypeStruct(out_shape, jnp.float32)
     (near,) = apply(
-        near_kernel, "near", [total], sizes + (term_blocks,),
-        [psi, left_ops, side, direct_a, direct_b] + rights,
+        near_kernel, "near", [total], sizes,
+        [psi, left_sent, swap_sent, swapped, direct_a, direct_b],
     )
     psi_turn, near = lax.optimization_barrier((psi_far, near))
     (wide,) = apply(
         mask_kernel, "mask", [block((sectors, tile, sectors * tile))], sizes,
-        [psi_turn],
+        [direct_b, psi_turn],
     )
     sent, far = apply(
         far_kernel, "far", [block(out_shape), total], sizes,
-        [direct_a, direct_b, passed_a, passed_b] + rights + [near, wide],
+        [direct_a, direct_b, passed_a, passed_b, swap_sent, swapped, near, wide],
     )
     arrived = over_op(sent, 2)
     kept = jnp.where(lax.axis_index("blk") // 2 == lax.axis_index("op") // 2, near, far)

time: 27.7 us -> 29.1 us (1.051)
  waiting for transfers between devices: 8.38 us -> 12.7 us
  starting transfers between devices: 13.3 us -> 10.4 us
    ppermute x6 -> x4, waiting for transfers between devices: 4.27 us -> 8.69 us  [over_z(): return lax.ppermute(array, ('blk', 'op'), pairs)]
    ppermute x6 -> x4, starting transfers between devices: 11.2 us -> 7.44 us  [over_z(): return lax.ppermute(array, ('blk', 'op'), pairs)]
    ppermute x0 -> x1, starting transfers between devices: none -> 0.79 us  [to_third(): return lax.ppermute(array, ('blk', 'op'), pairs)]
  transfers between devices with their start and end apart: 8 -> 7, of which waited for: 4 -> 3; matrix products, arithmetic and copies ran while one was open for 0% -> 0% of each run, Pallas kernels for 7% -> 6%
where the time goes in v6:
time: 29.1 us; the launch traced here: 29 us
  waiting for transfers between devices  12.7 us (44%)
  starting transfers between devices  10.4 us (36%)
  Pallas kernels  5.12 us (18%)
  other arithmetic  0.69 us (2%)
    ppermute x4, waiting for transfers between devices, over_z(): return lax.ppermute(array, ('blk', 'op'), pairs)  8.69 us
    ppermute x4, starting transfers between devices, over_z(): return lax.ppermute(array, ('blk', 'op'), pairs)  7.44 us
    ppermute x2, waiting for transfers between devices, over_op(): return lax.ppermute(array, 'op', [(o, o ^ step) for o in range(n)])  4 us
    pallas_call x3, Pallas kernels, apply(): pl.pallas_call(kernel, out_shape=outs, in_specs=[SMEM] * len(scalars) + [...  3 us
    ppermute x2, starting transfers between devices, over_op(): return lax.ppermute(array, 'op', [(o, o ^ step) for o in range(n)])  2.19 us
    pallas_call x1, Pallas kernels, shards(): pl.pallas_call(pack_kernel, out_shape=[block((rows, tile)), block((rows +...  2.11 us
    ppermute x1, starting transfers between devices, to_third(): return lax.ppermute(array, ('blk', 'op'), pairs)  0.79 us
    convert_element_type x1, other arithmetic, shards(): return (kept + arrived.astype(jnp.float32)).astype(jnp.bfloat16)  0.69 us
  transfers between devices with their start and end apart: 7, of which 3 were waited for; matrix products, arithmetic and copies ran while one was open for 0% of the time, Pallas kernels for 6%

profile of v6, /device:TPU:0, one launch (start us, length us, event | category | flops | bytes accessed | tf_op | source)
XLA Modules:
  0.0 29.0 jit_solution(7089810376875317598)
XLA Ops:
  0.0 0.0 copy-start
  0.0 2.1 %pack.1 = (bf16[528,128]{1,0:T(8,128)(2,1)S(1)}, bf16[1040,128]{1,0:T(8,128)(2,1)S(1)}, bf16[1552,128]{1,0:T(8,128)(2,1)S(1)}, bf16[512,128]{1,0:T(8,128)(2,1)S(1)}) custom-call(s32[4,8]{1,0:T(4,128)} %blocks_ref.1, bf16[2,8,128,128]{3,2,1,0:T(8,128)(2,1)} %rest_0_.1, bf16[4,2,128,128]{3,2,1,0:T(8,128)(2,1)} %left_ref.1, bf16[1024,128]{1,0:T(8,128)(2,1)} %bitcast.1), custom_call_target="tpu_custom_call" | custom-call | tf_op jit(solution)/shard_map/pack/pallas_call | solution.py:246
  2.1 0.6 %collective-permute-start.1 = (bf16[1552,128]{1,0:T(8,128)(2,1)S(1)}, bf16[1552,128]{1,0:T(8,128)(2,1)S(1)}, u32[]{:S(2)}, u32[]{:S(2)}) collective-permute-start(bf16[1552,128]{1,0:T(8,128)(2,1)S(1)} %get-tuple-element.15.rest_2_.rest_4_), channel_id=1, source_target_pairs={{0,1},{1,0},{2,3},{3,2},{4,5},{5,4},{6,7},{7,6},{8,9},{9,8},{10,11... | collective-permute-start | bytes 1191944 | tf_op jit(solution)/shard_map/ppermute | solution.py:221
  2.7 2.6 %collective-permute-start.3 = (bf16[1040,128]{1,0:T(8,128)(2,1)S(1)}, bf16[1040,128]{1,0:T(8,128)(2,1)S(1)}, u32[]{:S(2)}, u32[]{:S(2)}) collective-permute-start(bf16[1040,128]{1,0:T(8,128)(2,1)S(1)} %get-tuple-element.16), channel_id=1, source_target_pairs={{0,4},{1,8},{2,6},{3,10},{4,13},{5,1},{6,15},{7,3},{8,12},{9,0},{1... | collective-permute-start | bytes 798728 | tf_op jit(solution)/shard_map/ppermute | solution.py:229
  5.3 2.6 %collective-permute-start.2 = (bf16[528,128]{1,0:T(8,128)(2,1)S(1)}, bf16[528,128]{1,0:T(8,128)(2,1)S(1)}, u32[]{:S(2)}, u32[]{:S(2)}) collective-permute-start(bf16[528,128]{1,0:T(8,128)(2,1)S(1)} %get-tuple-element.14.rest_1_), channel_id=1, source_target_pairs={{0,8},{1,4},{2,10},{3,6},{4,1},{5,13},{6,3},{7,15},{8,0},{9,12},{1... | collective-permute-start | bytes 405512 | tf_op jit(solution)/shard_map/ppermute | solution.py:229
  7.9 0.0 copy-start.1
  7.9 0.8 %collective-permute-start = (bf16[512,128]{1,0:T(8,128)(2,1)S(1)}, bf16[512,128]{1,0:T(8,128)(2,1)S(1)}, u32[]{:S(2)}, u32[]{:S(2)}) collective-permute-start(bf16[512,128]{1,0:T(8,128)(2,1)S(1)} %get-tuple-element.13), channel_id=1, source_target_pairs={{0,0},{1,12},{2,2},{3,14},{4,9},{5,5},{6,11},{7,7},{8,8},{9,4},{10... | collective-permute-start | bytes 393224 | tf_op jit(solution)/shard_map/ppermute | solution.py:237
  8.7 7.7 %collective-permute-done.2.rest_4_.rest_0_ = bf16[528,128]{1,0:T(8,128)(2,1)S(1)} collective-permute-done((bf16[528,128]{1,0:T(8,128)(2,1)S(1)}, bf16[528,128]{1,0:T(8,128)(2,1)S(1)}, u32[]{:S(2)}, u32[]{:S(2)}) %collective-permute-start.2) | collective-permute-done | bytes 135200 | tf_op jit(solution)/shard_map/ppermute | solution.py:229
  16.4 1.1 %collective-permute-start.4 = (bf16[528,128]{1,0:T(8,128)(2,1)S(1)}, bf16[528,128]{1,0:T(8,128)(2,1)S(1)}, u32[]{:S(2)}, u32[]{:S(2)}) collective-permute-start(bf16[528,128]{1,0:T(8,128)(2,1)S(1)} %collective-permute-done.2.rest_4_.rest_0_), channel_id=1, source_target_pairs={{0,4},{1,0},{2,6},{3,2},{4,5},{5,1},{6,7},{7,3},{8,12},{9,8},{10,1... | collective-permute-start | bytes 405512 | tf_op jit(solution)/shard_map/ppermute | solution.py:229
  17.5 0.0 collective-permute-done.3.rest_5_.direct_b.rest_1_
  17.5 1.1 %collective-permute-start.5 = (bf16[528,128]{1,0:T(8,128)(2,1)S(1)}, bf16[528,128]{1,0:T(8,128)(2,1)S(1)}, u32[]{:S(2)}, u32[]{:S(2)}) collective-permute-start(bf16[528,128]{1,0:T(8,128)(2,1)S(1)} %slice.4), channel_id=1, source_target_pairs={{0,4},{1,0},{2,6},{3,2},{4,5},{5,1},{6,7},{7,3},{8,12},{9,8},{10,1... | collective-permute-start | bytes 405512 | tf_op jit(solution)/shard_map/ppermute | solution.py:229
  18.6 0.0 collective-permute-done.1.rest_3_.rest_5_
  18.6 0.0 copy-done
  18.6 0.0 copy-done.1
  18.6 0.0 copy-done.2
  18.6 1.2 %near.1.rest_6_ = f32[2,2,128,128]{3,2,1,0:T(8,128)S(1)} custom-call(s32[8]{0:T(128)S(1)} %copy-done.1, s32[8]{0:T(128)S(1)} %copy-done.2, bf16[2,8,128,128]{3,2,1,0:T(8,128)(2,1)S(1)} %copy-done, bf16[528,128]{1,0:T(8,128)(2,1)S(1)} %get-tuple-element.14.rest_1_, bf16[1552,128]{1,0:T(8,128)(2,1)S(1)} %get-tuple-element.15.rest_2_.rest_4_, ...), custom_call_target="tpu_custom_call" | custom-call | flops 536870912 | bytes 1048576 | tf_op jit(solution)/shard_map/near/pallas_call | solution.py:268
  19.8 0.0 collective-permute-done.psi_far
  19.8 0.6 %mask.1.rest_7_ = bf16[2,128,256]{2,1,0:T(8,128)(2,1)S(1)} custom-call(s32[8]{0:T(128)S(1)} %copy-done.1, s32[8]{0:T(128)S(1)} %copy-done.2, bf16[1040,128]{1,0:T(8,128)(2,1)S(1)} %collective-permute-done.3.rest_5_.direct_b.rest_1_, bf16[512,128]{1,0:T(8,128)(2,1)S(1)} %collective-permute-done.psi_far), custom_call_target="tpu_custom_call" | custom-call | flops 536870912 | bytes 1048576 | tf_op jit(solution)/shard_map/mask/pallas_call | solution.py:268
  20.4 0.0 collective-permute-done.4.rest_2_
  20.5 1.0 %collective-permute-done.5.rest_3_ = bf16[528,128]{1,0:T(8,128)(2,1)S(1)} collective-permute-done((bf16[528,128]{1,0:T(8,128)(2,1)S(1)}, bf16[528,128]{1,0:T(8,128)(2,1)S(1)}, u32[]{:S(2)}, u32[]{:S(2)}) %collective-permute-start.5) | collective-permute-done | bytes 135200 | tf_op jit(solution)/shard_map/ppermute | solution.py:229
  21.5 1.2 %far.1 = (bf16[2,2,128,128]{3,2,1,0:T(8,128)(2,1)S(1)}, f32[2,2,128,128]{3,2,1,0:T(8,128)S(1)}) custom-call(s32[8]{0:T(128)S(1)} %copy-done.1, s32[8]{0:T(128)S(1)} %copy-done.2, bf16[528,128]{1,0:T(8,128)(2,1)S(1)} %collective-permute-done.2.rest_4_.rest_0_, bf16[1040,128]{1,0:T(8,128)(2,1)S(1)} %collective-permute-done.3.rest_5_.direct_b.rest_1_, ...), custom_call_target="tpu_custom_call" | custom-call | flops 536870912 | bytes 1048576 | tf_op jit(solution)/shard_map/far/pallas_call | solution.py:268
  22.7 1.6 %collective-permute-start.6 = (bf16[2,2,128,128]{3,2,1,0:T(8,128)(2,1)S(1)}, bf16[2,2,128,128]{3,2,1,0:T(8,128)(2,1)S(1)}, u32[]{:S(2)}, u32[]{:S(2)}) collective-permute-start(bf16[2,2,128,128]{3,2,1,0:T(8,128)(2,1)S(1)} %get-tuple-element.20), channel_id=1, source_target_pairs={{0,2},{1,3},{2,0},{3,1},{4,6},{5,7},{6,4},{7,5},{8,10},{9,11},{10,... | collective-permute-start | bytes 393224 | tf_op jit(solution)/shard_map/ppermute | solution.py:221
  24.3 4.0 %collective-permute-done.6 = bf16[2,2,128,128]{3,2,1,0:T(8,128)(2,1)S(1)} collective-permute-done((bf16[2,2,128,128]{3,2,1,0:T(8,128)(2,1)S(1)}, bf16[2,2,128,128]{3,2,1,0:T(8,128)(2,1)S(1)}, u32[]{:S(2)}, u32[]{:S(2)}) %collective-permute-start.6) | collective-permute-done | bytes 131104 | tf_op jit(solution)/shard_map/ppermute | solution.py:221
  28.3 0.7 %add_convert_fusion = bf16[2,2,128,128]{3,2,1,0:T(8,128)(2,1)} fusion(bf16[2,2,128,128]{3,2,1,0:T(8,128)(2,1)S(1)} %collective-permute-done.6, f32[2,2,128,128]{3,2,1,0:T(8,128)S(1)} %near.1.rest_6_, f32[2,2,128,128]{3,2,1,0:T(8,128)S(1)} %get-tuple-element.19, pred[]{:T(512)S(6)} %eq.3), kind=kLoop, calls=%fused_computation | loop fusion | flops 262144 | bytes 786433 | tf_op jit(solution)/shard_map/convert_element_type | solution.py:297
  (2 shorter events, 0.0 us)
Async XLA Ops:
  0.0 18.6 %copy-start = (bf16[2,8,128,128]{3,2,1,0:T(8,128)(2,1)S(1)}, bf16[2,8,128,128]{3,2,1,0:T(8,128)(2,1)}, u32[]{:S(2)}) copy-start(bf16[2,8,128,128]{3,2,1,0:T(8,128)(2,1)} %rest_0_.1) | copy-start | bytes 1572868
  2.1 16.5 %collective-permute-start.1 = (bf16[1552,128]{1,0:T(8,128)(2,1)S(1)}, bf16[1552,128]{1,0:T(8,128)(2,1)S(1)}, u32[]{:S(2)}, u32[]{:S(2)}) collective-permute-start(bf16[1552,128]{1,0:T(8,128)(2,1)S(1)} %get-tuple-element.15.rest_2_.rest_4_), channel_id=1, source_target_pairs={{0,1},{1,0},{2,3},{3,2},{4,5},{5,4},{6,7},{7,6},{8,9},{9,8},{10,11... | collective-permute-start | bytes 1191944 | tf_op jit(solution)/shard_map/ppermute | solution.py:221
  2.7 14.8 %collective-permute-start.3 = (bf16[1040,128]{1,0:T(8,128)(2,1)S(1)}, bf16[1040,128]{1,0:T(8,128)(2,1)S(1)}, u32[]{:S(2)}, u32[]{:S(2)}) collective-permute-start(bf16[1040,128]{1,0:T(8,128)(2,1)S(1)} %get-tuple-element.16), channel_id=1, source_target_pairs={{0,4},{1,8},{2,6},{3,10},{4,13},{5,1},{6,15},{7,3},{8,12},{9,0},{1... | collective-permute-start | bytes 798728 | tf_op jit(solution)/shard_map/ppermute | solution.py:229
  5.3 11.0 %collective-permute-start.2 = (bf16[528,128]{1,0:T(8,128)(2,1)S(1)}, bf16[528,128]{1,0:T(8,128)(2,1)S(1)}, u32[]{:S(2)}, u32[]{:S(2)}) collective-permute-start(bf16[528,128]{1,0:T(8,128)(2,1)S(1)} %get-tuple-element.14.rest_1_), channel_id=1, source_target_pairs={{0,8},{1,4},{2,10},{3,6},{4,1},{5,13},{6,3},{7,15},{8,0},{9,12},{1... | collective-permute-start | bytes 405512 | tf_op jit(solution)/shard_map/ppermute | solution.py:229
  7.9 10.7 %copy-start.1 = (s32[8]{0:T(128)S(1)}, s32[8]{0:T(128)}, u32[]{:S(2)}) copy-start(s32[8]{0:T(128)} %lsize_ref.5) | copy-start | bytes 100
  7.9 10.7 %copy-start.2 = (s32[8]{0:T(128)S(1)}, s32[8]{0:T(128)}, u32[]{:S(2)}) copy-start(s32[8]{0:T(128)} %rsize_ref.5) | copy-start | bytes 100
  7.9 11.9 %collective-permute-start = (bf16[512,128]{1,0:T(8,128)(2,1)S(1)}, bf16[512,128]{1,0:T(8,128)(2,1)S(1)}, u32[]{:S(2)}, u32[]{:S(2)}) collective-permute-start(bf16[512,128]{1,0:T(8,128)(2,1)S(1)} %get-tuple-element.13), channel_id=1, source_target_pairs={{0,0},{1,12},{2,2},{3,14},{4,9},{5,5},{6,11},{7,7},{8,8},{9,4},{10... | collective-permute-start | bytes 393224 | tf_op jit(solution)/shard_map/ppermute | solution.py:237
  16.4 4.1 %collective-permute-start.4 = (bf16[528,128]{1,0:T(8,128)(2,1)S(1)}, bf16[528,128]{1,0:T(8,128)(2,1)S(1)}, u32[]{:S(2)}, u32[]{:S(2)}) collective-permute-start(bf16[528,128]{1,0:T(8,128)(2,1)S(1)} %collective-permute-done.2.rest_4_.rest_0_), channel_id=1, source_target_pairs={{0,4},{1,0},{2,6},{3,2},{4,5},{5,1},{6,7},{7,3},{8,12},{9,8},{10,1... | collective-permute-start | bytes 405512 | tf_op jit(solution)/shard_map/ppermute | solution.py:229
  17.5 4.0 %collective-permute-start.5 = (bf16[528,128]{1,0:T(8,128)(2,1)S(1)}, bf16[528,128]{1,0:T(8,128)(2,1)S(1)}, u32[]{:S(2)}, u32[]{:S(2)}) collective-permute-start(bf16[528,128]{1,0:T(8,128)(2,1)S(1)} %slice.4), channel_id=1, source_target_pairs={{0,4},{1,0},{2,6},{3,2},{4,5},{5,1},{6,7},{7,3},{8,12},{9,8},{10,1... | collective-permute-start | bytes 405512 | tf_op jit(solution)/shard_map/ppermute | solution.py:229
  22.7 5.6 %collective-permute-start.6 = (bf16[2,2,128,128]{3,2,1,0:T(8,128)(2,1)S(1)}, bf16[2,2,128,128]{3,2,1,0:T(8,128)(2,1)S(1)}, u32[]{:S(2)}, u32[]{:S(2)}) collective-permute-start(bf16[2,2,128,128]{3,2,1,0:T(8,128)(2,1)S(1)} %get-tuple-element.20), channel_id=1, source_target_pairs={{0,2},{1,3},{2,0},{3,1},{4,6},{5,7},{6,4},{7,5},{8,10},{9,11},{10,... | collective-permute-start | bytes 393224 | tf_op jit(solution)/shard_map/ppermute | solution.py:221

commit v7 on v6

--- a/solution.py
+++ b/solution.py
@@ -36,7 +36,7 @@
 
 
 def pack_kernel(blocks_ref, psi_ref, left_ref, right_ref, *rest):
-    left_out, both_out, swap_out, far_out, sem = rest
+    a_out, b_out, swap_out, far_out, sem = rest
     z, _, _ = place()
     sectors, tile = psi_ref.shape[0], psi_ref.shape[-1]
     count = 2 * sectors
@@ -55,18 +55,18 @@
         for slot, term in enumerate(acting_terms(blocks_ref, z * sectors + local)):
             spot = 2 * local + slot
             ids = jnp.where(row == spot, term.astype(jnp.float32), ids)
-            for out, first in ((left_out, 0), (both_out, 0), (swap_out, begin)):
+            for out, first in ((a_out, 0), (b_out, 0), (swap_out, begin)):
                 bring(left_ref.at[term, local], out, first + spot * tile, tile)
-    beside = jnp.bitwise_xor(z, jnp.where(is_home(), 1, 2)) * sectors
     far = jnp.bitwise_xor(z, 3) * sectors
-    for a in range(sectors):
+    for a, out in enumerate((a_out, b_out)):
+        steps = (2, 1) if a == 0 else (1, 2)
+        beside = jnp.bitwise_xor(z, jnp.where(is_home(), *steps)) * sectors
         for b in range(sectors):
-            spot = (sectors * a + b) * tile
-            bring(psi_ref.at[a, beside + b], both_out, count * tile + ID_ROWS + spot, tile)
-            bring(psi_ref.at[a, far + b], far_out, spot, tile)
+            bring(psi_ref.at[a, beside + b], out, count * tile + ID_ROWS + b * tile, tile)
+            bring(psi_ref.at[a, far + b], far_out, (sectors * a + b) * tile, tile)
     for copy in copies:
         copy.start()
-    for out, first in ((left_out, 0), (both_out, 0), (swap_out, begin)):
+    for out, first in ((a_out, 0), (b_out, 0), (swap_out, begin)):
         out[pl.ds(first + count * tile, ID_ROWS)] = ids.astype(jnp.bfloat16)
     for copy in copies:
         copy.wait()
@@ -136,11 +136,12 @@
 
 
 def near_kernel(lsize_ref, rsize_ref, *rest):
-    psi_ref, left_own, swap_own, swapped, direct_a, direct_b, out_ref = rest
+    psi_ref, swap_own, swapped, direct_a, direct_b, out_ref = rest
     z, _, _ = place()
     sectors, tile = out_ref.shape[0], out_ref.shape[-1]
     sizes, columns = (lsize_ref, rsize_ref), range(sectors)
-    begin = swap_own.shape[0] - left_own.shape[0]
+    rows = 2 * sectors * tile + ID_ROWS
+    begin = swap_own.shape[0] - rows
 
     def store(b, a, total):
         out_ref[b, a] = total
@@ -150,7 +151,7 @@
         @pl.when(is_home() == at_home)
         def _(at_home=at_home):
             if at_home:
-                pair = [(left_own, 0, sectors, swap_own), (swapped, begin, sectors, swapped)]
+                pair = [(swap_own, begin, sectors, swap_own), (swapped, begin, sectors, swapped)]
             else:
                 pair = [(direct_b, 0, sectors, swap_own), (direct_a, 0, sectors, swapped)]
 
@@ -158,7 +159,7 @@
                 if at_home:
                     blocks = [psi_ref[a, z * sectors + b] for b in columns]
                 else:
-                    blocks = psi_rows(direct_b, left_own.shape[0], a, sectors)
+                    blocks = psi_rows((direct_a, direct_b)[a], rows, 0, sectors)
                 return wide_psi(z, 0 if at_home else 1, sizes, a, columns, blocks)
 
             lefts, rights = zip(*[message(*one) for one in pair])
@@ -166,18 +167,21 @@
             partial_sums(z, distance, sizes, columns, psi, lefts, rights, store)
 
 
-def mask_kernel(lsize_ref, rsize_ref, direct_b, psi_far, wide_ref):
+def mask_kernel(lsize_ref, rsize_ref, direct_a, direct_b, psi_far, wide_ref):
     z, _, _ = place()
     sectors = wide_ref.shape[0]
     columns = range(sectors)
     sizes = (lsize_ref, rsize_ref)
-    first = direct_b.shape[0] - psi_far.shape[0]
-    for at_home, distance, ref, begin in ((True, 2, direct_b, first), (False, 3, psi_far, 0)):
+    first = 2 * sectors * wide_ref.shape[1] + ID_ROWS
+    for at_home, distance in ((True, 2), (False, 3)):
 
         @pl.when(is_home() == at_home)
-        def _(distance=distance, ref=ref, begin=begin):
+        def _(at_home=at_home, distance=distance):
             for a in columns:
-                blocks = psi_rows(ref, begin, a, sectors)
+                if at_home:
+                    blocks = psi_rows((direct_a, direct_b)[a], first, 0, sectors)
+                else:
+                    blocks = psi_rows(psi_far, 0, a, sectors)
                 wide_ref[a] = wide_psi(z, distance, sizes, a, columns, blocks)
 
 
@@ -243,11 +247,11 @@
     ]
     rows, right_rows = 2 * sectors * tile + ID_ROWS, rights.shape[0]
     psi_count = sectors * sectors
-    left_sent, both_sent, swap_sent, far_sent = pl.pallas_call(
+    sent_a, sent_b, swap_sent, far_sent = pl.pallas_call(
         pack_kernel,
         out_shape=[
-            block((rows, tile)),
-            block((rows + psi_count * tile, tile)),
+            block((rows + sectors * tile, tile)),
+            block((rows + sectors * tile, tile)),
             block((right_rows + rows, tile)),
             block((psi_count * tile, tile)),
         ],
@@ -257,11 +261,11 @@
         compiler_params=PARAMS,
         name="pack",
     )(*inputs)
-    direct_a = over_z(left_sent, 2, 1)
-    direct_b = over_z(both_sent, 1, 2)
+    direct_a = over_z(sent_a, 2, 1)
+    direct_b = over_z(sent_b, 1, 2)
     psi_far = to_third(far_sent)
     swapped = over_op(swap_sent, 1)
-    passed_a = over_z(direct_a, 1, 0)
+    passed_a = over_z(direct_a[:rows], 1, 0)
     passed_b = over_z(direct_b[:rows], 1, 0)
 
     def apply(kernel, name, outs, scalars, operands):
@@ -281,12 +285,12 @@
     total = jax.ShapeDtypeStruct(out_shape, jnp.float32)
     (near,) = apply(
         near_kernel, "near", [total], sizes,
-        [psi, left_sent, swap_sent, swapped, direct_a, direct_b],
+        [psi, swap_sent, swapped, direct_a, direct_b],
     )
     psi_turn, near = lax.optimization_barrier((psi_far, near))
     (wide,) = apply(
         mask_kernel, "mask", [block((sectors, tile, sectors * tile))], sizes,
-        [direct_b, psi_turn],
+        [direct_a, direct_b, psi_turn],
     )
     sent, far = apply(
         far_kernel, "far", [block(out_shape), total], sizes,

time: 29.1 us -> 29.2 us (level)
  starting transfers between devices: 10.4 us -> 9.05 us
  waiting for transfers between devices: 12.7 us -> 14 us
    ppermute x4, starting transfers between devices: 7.44 us -> 6.45 us  [over_z(): return lax.ppermute(array, ('blk', 'op'), pairs)]
    ppermute x4, waiting for transfers between devices: 8.69 us -> 9.45 us  [over_z(): return lax.ppermute(array, ('blk', 'op'), pairs)]
    ppermute x2, waiting for transfers between devices: 4 us -> 4.59 us  [over_op(): return lax.ppermute(array, 'op', [(o, o ^ step) for o in range(n)])]
  transfers between devices with their start and end apart: 7 -> 7, of which waited for: 3 -> 4; matrix products, arithmetic and copies ran while one was open for 0% -> 0% of each run, Pallas kernels for 6% -> 6%
where the time goes in v7:
time: 29.2 us; the launch traced here: 29.1 us
  waiting for transfers between devices  14 us (48%)
  starting transfers between devices  9.05 us (31%)
  Pallas kernels  5.13 us (18%)
  other arithmetic  0.69 us (2%)
    ppermute x4, waiting for transfers between devices, over_z(): return lax.ppermute(array, ('blk', 'op'), pairs)  9.45 us
    ppermute x4, starting transfers between devices, over_z(): return lax.ppermute(array, ('blk', 'op'), pairs)  6.45 us
    ppermute x2, waiting for transfers between devices, over_op(): return lax.ppermute(array, 'op', [(o, o ^ step) for o in range(n)])  4.59 us
    pallas_call x3, Pallas kernels, apply(): pl.pallas_call(kernel, out_shape=outs, in_specs=[SMEM] * len(scalars) + [...  3.02 us
    pallas_call x1, Pallas kernels, shards(): pl.pallas_call(pack_kernel, out_shape=[block((rows + sectors * tile, tile...  2.12 us
    ppermute x2, starting transfers between devices, over_op(): return lax.ppermute(array, 'op', [(o, o ^ step) for o in range(n)])  1.94 us
    convert_element_type x1, other arithmetic, shards(): return (kept + arrived.astype(jnp.float32)).astype(jnp.bfloat16)  0.69 us
    ppermute x1, starting transfers between devices, to_third(): return lax.ppermute(array, ('blk', 'op'), pairs)  0.66 us
  transfers between devices with their start and end apart: 7, of which 4 were waited for; matrix products, arithmetic and copies ran while one was open for 0% of the time, Pallas kernels for 6%

profile of v7, /device:TPU:0, one launch (start us, length us, event | category | flops | bytes accessed | tf_op | source)
XLA Modules:
  0.0 29.1 jit_solution(10946824438464861775)
XLA Ops:
  0.0 2.1 %pack.1 = (bf16[784,128]{1,0:T(8,128)(2,1)S(1)}, bf16[784,128]{1,0:T(8,128)(2,1)S(1)}, bf16[1552,128]{1,0:T(8,128)(2,1)S(1)}, bf16[512,128]{1,0:T(8,128)(2,1)S(1)}) custom-call(s32[4,8]{1,0:T(4,128)} %blocks_ref.1, bf16[2,8,128,128]{3,2,1,0:T(8,128)(2,1)} %rest_0_.1, bf16[4,2,128,128]{3,2,1,0:T(8,128)(2,1)} %left_ref.1, bf16[1024,128]{1,0:T(8,128)(2,1)} %bitcast.1), custom_call_target="tpu_custom_call" | custom-call | tf_op jit(solution)/shard_map/pack/pallas_call | solution.py:250
  2.1 0.0 copy-start
  2.1 0.4 %collective-permute-start.1 = (bf16[1552,128]{1,0:T(8,128)(2,1)S(1)}, bf16[1552,128]{1,0:T(8,128)(2,1)S(1)}, u32[]{:S(2)}, u32[]{:S(2)}) collective-permute-start(bf16[1552,128]{1,0:T(8,128)(2,1)S(1)} %get-tuple-element.14.rest_1_.rest_4_), channel_id=1, source_target_pairs={{0,1},{1,0},{2,3},{3,2},{4,5},{5,4},{6,7},{7,6},{8,9},{9,8},{10,11... | collective-permute-start | bytes 1191944 | tf_op jit(solution)/shard_map/ppermute | solution.py:225
  2.6 3.7 %collective-permute-start.2 = (bf16[784,128]{1,0:T(8,128)(2,1)S(1)}, bf16[784,128]{1,0:T(8,128)(2,1)S(1)}, u32[]{:S(2)}, u32[]{:S(2)}) collective-permute-start(bf16[784,128]{1,0:T(8,128)(2,1)S(1)} %get-tuple-element.15), channel_id=1, source_target_pairs={{0,8},{1,4},{2,10},{3,6},{4,1},{5,13},{6,3},{7,15},{8,0},{9,12},{1... | collective-permute-start | bytes 602120 | tf_op jit(solution)/shard_map/ppermute | solution.py:233
  6.2 0.0 collective-permute-start.3
  6.2 0.7 %collective-permute-start = (bf16[512,128]{1,0:T(8,128)(2,1)S(1)}, bf16[512,128]{1,0:T(8,128)(2,1)S(1)}, u32[]{:S(2)}, u32[]{:S(2)}) collective-permute-start(bf16[512,128]{1,0:T(8,128)(2,1)S(1)} %get-tuple-element.13), channel_id=1, source_target_pairs={{0,0},{1,12},{2,2},{3,14},{4,9},{5,5},{6,11},{7,7},{8,8},{9,4},{10... | collective-permute-start | bytes 393224 | tf_op jit(solution)/shard_map/ppermute | solution.py:241
  6.9 6.1 %collective-permute-done.2.rest_3_.direct_a.rest_0_ = bf16[784,128]{1,0:T(8,128)(2,1)S(1)} collective-permute-done((bf16[784,128]{1,0:T(8,128)(2,1)S(1)}, bf16[784,128]{1,0:T(8,128)(2,1)S(1)}, u32[]{:S(2)}, u32[]{:S(2)}) %collective-permute-start.2) | collective-permute-done | bytes 200736 | tf_op jit(solution)/shard_map/ppermute | solution.py:233
  13.0 0.0 copy-start.1
  13.1 0.0 copy-start.2
  13.1 0.1 collective-permute-start.4
  13.1 2.6 %collective-permute-done.3.rest_4_.direct_b.rest_1_ = bf16[784,128]{1,0:T(8,128)(2,1)S(1)} collective-permute-done((bf16[784,128]{1,0:T(8,128)(2,1)S(1)}, bf16[784,128]{1,0:T(8,128)(2,1)S(1)}, u32[]{:S(2)}, u32[]{:S(2)}) %collective-permute-start.3) | collective-permute-done | bytes 200736 | tf_op jit(solution)/shard_map/ppermute | solution.py:233
  15.8 2.7 %collective-permute-start.5 = (bf16[528,128]{1,0:T(8,128)(2,1)S(1)}, bf16[528,128]{1,0:T(8,128)(2,1)S(1)}, u32[]{:S(2)}, u32[]{:S(2)}) collective-permute-start(bf16[528,128]{1,0:T(8,128)(2,1)S(1)} %slice.9), channel_id=1, source_target_pairs={{0,4},{1,0},{2,6},{3,2},{4,5},{5,1},{6,7},{7,3},{8,12},{9,8},{10,1... | collective-permute-start | bytes 405512 | tf_op jit(solution)/shard_map/ppermute | solution.py:233
  18.5 0.0 collective-permute-done.1.rest_2_.rest_5_
  18.5 0.0 copy-done.1
  18.5 0.0 copy-done.2
  18.5 1.2 %near.1.rest_6_ = f32[2,2,128,128]{3,2,1,0:T(8,128)S(1)} custom-call(s32[8]{0:T(128)S(1)} %copy-done.1, s32[8]{0:T(128)S(1)} %copy-done.2, bf16[2,8,128,128]{3,2,1,0:T(8,128)(2,1)S(1)} %copy-done, bf16[1552,128]{1,0:T(8,128)(2,1)S(1)} %get-tuple-element.14.rest_1_.rest_4_, bf16[1552,128]{1,0:T(8,128)(2,1)S(1)} %collective-permute-done.1.rest_2_.rest_5_, ...), custom_call_target="tpu_custom_call" | custom-call | flops 536870912 | bytes 1048576 | tf_op jit(solution)/shard_map/near/pallas_call | solution.py:272
  19.7 0.0 collective-permute-done.psi_far
  19.7 0.6 %mask.1.rest_7_ = bf16[2,128,256]{2,1,0:T(8,128)(2,1)S(1)} custom-call(s32[8]{0:T(128)S(1)} %copy-done.1, s32[8]{0:T(128)S(1)} %copy-done.2, bf16[784,128]{1,0:T(8,128)(2,1)S(1)} %collective-permute-done.2.rest_3_.direct_a.rest_0_, bf16[784,128]{1,0:T(8,128)(2,1)S(1)} %collective-permute-done.3.rest_4_.direct_b.rest_1_, ...), custom_call_target="tpu_custom_call" | custom-call | flops 536870912 | bytes 1048576 | tf_op jit(solution)/shard_map/mask/pallas_call | solution.py:272
  20.3 0.0 collective-permute-done.4.rest_2_
  20.3 0.7 %collective-permute-done.5.rest_3_ = bf16[528,128]{1,0:T(8,128)(2,1)S(1)} collective-permute-done((bf16[528,128]{1,0:T(8,128)(2,1)S(1)}, bf16[528,128]{1,0:T(8,128)(2,1)S(1)}, u32[]{:S(2)}, u32[]{:S(2)}) %collective-permute-start.5) | collective-permute-done | bytes 135200 | tf_op jit(solution)/shard_map/ppermute | solution.py:233
  21.0 1.2 %far.1 = (bf16[2,2,128,128]{3,2,1,0:T(8,128)(2,1)S(1)}, f32[2,2,128,128]{3,2,1,0:T(8,128)S(1)}) custom-call(s32[8]{0:T(128)S(1)} %copy-done.1, s32[8]{0:T(128)S(1)} %copy-done.2, bf16[784,128]{1,0:T(8,128)(2,1)S(1)} %collective-permute-done.2.rest_3_.direct_a.rest_0_, bf16[784,128]{1,0:T(8,128)(2,1)S(1)} %collective-permute-done.3.rest_4_.direct_b.rest_1_, ...), custom_call_target="tpu_custom_call" | custom-call | flops 536870912 | bytes 1048576 | tf_op jit(solution)/shard_map/far/pallas_call | solution.py:272
  22.3 1.5 %collective-permute-start.6 = (bf16[2,2,128,128]{3,2,1,0:T(8,128)(2,1)S(1)}, bf16[2,2,128,128]{3,2,1,0:T(8,128)(2,1)S(1)}, u32[]{:S(2)}, u32[]{:S(2)}) collective-permute-start(bf16[2,2,128,128]{3,2,1,0:T(8,128)(2,1)S(1)} %get-tuple-element.20), channel_id=1, source_target_pairs={{0,2},{1,3},{2,0},{3,1},{4,6},{5,7},{6,4},{7,5},{8,10},{9,11},{10,... | collective-permute-start | bytes 393224 | tf_op jit(solution)/shard_map/ppermute | solution.py:225
  23.8 4.6 %collective-permute-done.6 = bf16[2,2,128,128]{3,2,1,0:T(8,128)(2,1)S(1)} collective-permute-done((bf16[2,2,128,128]{3,2,1,0:T(8,128)(2,1)S(1)}, bf16[2,2,128,128]{3,2,1,0:T(8,128)(2,1)S(1)}, u32[]{:S(2)}, u32[]{:S(2)}) %collective-permute-start.6) | collective-permute-done | bytes 131104 | tf_op jit(solution)/shard_map/ppermute | solution.py:225
  28.4 0.7 %add_convert_fusion = bf16[2,2,128,128]{3,2,1,0:T(8,128)(2,1)} fusion(bf16[2,2,128,128]{3,2,1,0:T(8,128)(2,1)S(1)} %collective-permute-done.6, f32[2,2,128,128]{3,2,1,0:T(8,128)S(1)} %near.1.rest_6_, f32[2,2,128,128]{3,2,1,0:T(8,128)S(1)} %get-tuple-element.19, pred[]{:T(512)S(6)} %eq.3), kind=kLoop, calls=%fused_computation | loop fusion | flops 262144 | bytes 786433 | tf_op jit(solution)/shard_map/convert_element_type | solution.py:301
  (3 shorter events, 0.0 us)
Async XLA Ops:
  2.1 16.4 %copy-start = (bf16[2,8,128,128]{3,2,1,0:T(8,128)(2,1)S(1)}, bf16[2,8,128,128]{3,2,1,0:T(8,128)(2,1)}, u32[]{:S(2)}) copy-start(bf16[2,8,128,128]{3,2,1,0:T(8,128)(2,1)} %rest_0_.1) | copy-start | bytes 1572868
  2.1 16.3 %collective-permute-start.1 = (bf16[1552,128]{1,0:T(8,128)(2,1)S(1)}, bf16[1552,128]{1,0:T(8,128)(2,1)S(1)}, u32[]{:S(2)}, u32[]{:S(2)}) collective-permute-start(bf16[1552,128]{1,0:T(8,128)(2,1)S(1)} %get-tuple-element.14.rest_1_.rest_4_), channel_id=1, source_target_pairs={{0,1},{1,0},{2,3},{3,2},{4,5},{5,4},{6,7},{7,6},{8,9},{9,8},{10,11... | collective-permute-start | bytes 1191944 | tf_op jit(solution)/shard_map/ppermute | solution.py:225
  2.6 10.5 %collective-permute-start.2 = (bf16[784,128]{1,0:T(8,128)(2,1)S(1)}, bf16[784,128]{1,0:T(8,128)(2,1)S(1)}, u32[]{:S(2)}, u32[]{:S(2)}) collective-permute-start(bf16[784,128]{1,0:T(8,128)(2,1)S(1)} %get-tuple-element.15), channel_id=1, source_target_pairs={{0,8},{1,4},{2,10},{3,6},{4,1},{5,13},{6,3},{7,15},{8,0},{9,12},{1... | collective-permute-start | bytes 602120 | tf_op jit(solution)/shard_map/ppermute | solution.py:233
  6.2 9.5 %collective-permute-start.3 = (bf16[784,128]{1,0:T(8,128)(2,1)S(1)}, bf16[784,128]{1,0:T(8,128)(2,1)S(1)}, u32[]{:S(2)}, u32[]{:S(2)}) collective-permute-start(bf16[784,128]{1,0:T(8,128)(2,1)S(1)} %get-tuple-element.16), channel_id=1, source_target_pairs={{0,4},{1,8},{2,6},{3,10},{4,13},{5,1},{6,15},{7,3},{8,12},{9,0},{1... | collective-permute-start | bytes 602120 | tf_op jit(solution)/shard_map/ppermute | solution.py:233
  6.2 13.5 %collective-permute-start = (bf16[512,128]{1,0:T(8,128)(2,1)S(1)}, bf16[512,128]{1,0:T(8,128)(2,1)S(1)}, u32[]{:S(2)}, u32[]{:S(2)}) collective-permute-start(bf16[512,128]{1,0:T(8,128)(2,1)S(1)} %get-tuple-element.13), channel_id=1, source_target_pairs={{0,0},{1,12},{2,2},{3,14},{4,9},{5,5},{6,11},{7,7},{8,8},{9,4},{10... | collective-permute-start | bytes 393224 | tf_op jit(solution)/shard_map/ppermute | solution.py:241
  13.0 5.4 %copy-start.1 = (s32[8]{0:T(128)S(1)}, s32[8]{0:T(128)}, u32[]{:S(2)}) copy-start(s32[8]{0:T(128)} %lsize_ref.5) | copy-start | bytes 100
  13.1 5.4 %copy-start.2 = (s32[8]{0:T(128)S(1)}, s32[8]{0:T(128)}, u32[]{:S(2)}) copy-start(s32[8]{0:T(128)} %rsize_ref.5) | copy-start | bytes 100
  13.1 7.3 %collective-permute-start.4 = (bf16[528,128]{1,0:T(8,128)(2,1)S(1)}, bf16[528,128]{1,0:T(8,128)(2,1)S(1)}, u32[]{:S(2)}, u32[]{:S(2)}) collective-permute-start(bf16[528,128]{1,0:T(8,128)(2,1)S(1)} %slice.8), channel_id=1, source_target_pairs={{0,4},{1,0},{2,6},{3,2},{4,5},{5,1},{6,7},{7,3},{8,12},{9,8},{10,1... | collective-permute-start | bytes 405512 | tf_op jit(solution)/shard_map/ppermute | solution.py:233
  15.8 5.3 %collective-permute-start.5 = (bf16[528,128]{1,0:T(8,128)(2,1)S(1)}, bf16[528,128]{1,0:T(8,128)(2,1)S(1)}, u32[]{:S(2)}, u32[]{:S(2)}) collective-permute-start(bf16[528,128]{1,0:T(8,128)(2,1)S(1)} %slice.9), channel_id=1, source_target_pairs={{0,4},{1,0},{2,6},{3,2},{4,5},{5,1},{6,7},{7,3},{8,12},{9,8},{10,1... | collective-permute-start | bytes 405512 | tf_op jit(solution)/shard_map/ppermute | solution.py:233
  22.3 6.1 %collective-permute-start.6 = (bf16[2,2,128,128]{3,2,1,0:T(8,128)(2,1)S(1)}, bf16[2,2,128,128]{3,2,1,0:T(8,128)(2,1)S(1)}, u32[]{:S(2)}, u32[]{:S(2)}) collective-permute-start(bf16[2,2,128,128]{3,2,1,0:T(8,128)(2,1)S(1)} %get-tuple-element.20), channel_id=1, source_target_pairs={{0,2},{1,3},{2,0},{3,1},{4,6},{5,7},{6,4},{7,5},{8,10},{9,11},{10,... | collective-permute-start | bytes 393224 | tf_op jit(solution)/shard_map/ppermute | solution.py:225

commit v8 on v3

--- a/solution.py
+++ b/solution.py
@@ -12,6 +12,7 @@
 VMEM = pl.BlockSpec(memory_space=pltpu.VMEM)
 PARAMS = pltpu.CompilerParams(vmem_limit_bytes=32 * 1024 * 1024)
 ID_ROWS = 16
+FAR_PAD = 32
 
 
 def acting_terms(blocks_ref, sector):
@@ -55,10 +56,11 @@
             for spot, source in enumerate(sources)
         ]
 
-    far = pl.ds(jnp.bitwise_xor(z, jnp.where(is_home(), 2, 3)) * sectors, sectors)
+    far = jnp.bitwise_xor(z, jnp.where(is_home(), 2, 3)) * sectors
     plain = copies(picked, left_out, 0)
-    plain.append(pltpu.make_async_copy(psi_ref.at[:, far], far_out, sem.at[2 * count]))
-    plain.append(pltpu.make_async_copy(right_ref, right_out, sem.at[2 * count + 1]))
+    plain.append(pltpu.make_async_copy(right_ref, right_out, sem.at[2 * count]))
+    wanted = [psi_ref.at[a, far + b] for a in range(sectors) for b in range(sectors)]
+    plain += copies(wanted, far_out, 2 * count + 1)
     for copy in plain:
         copy.start()
     for at_home, sources in ((True, asked), (False, picked)):
@@ -70,6 +72,7 @@
 
     for out in (left_out, side_out):
         out[pl.ds(count * tile, ID_ROWS)] = ids.astype(jnp.bfloat16)
+    far_out[pl.ds(count * tile, FAR_PAD)] = jnp.zeros((FAR_PAD, tile), jnp.bfloat16)
     for copy in plain + copies(picked, side_out, count):
         copy.wait()
 
@@ -131,15 +134,6 @@
     return left, right
 
 
-def mask_kernel(lsize_ref, rsize_ref, psi_ref, wide_ref):
-    z, _, _ = place()
-    far = jnp.where(is_home(), 2, 3)
-    columns = range(psi_ref.shape[1])
-    for a in range(psi_ref.shape[0]):
-        blocks = [psi_ref[a, b] for b in columns]
-        wide_ref[a] = wide_psi(z, far, (lsize_ref, rsize_ref), a, columns, blocks)
-
-
 def near_kernel(lsize_ref, rsize_ref, blocks_ref, *rest):
     psi_ref, left_ref, side, direct_a, direct_b, right_own, right_other, out_ref = rest
     z, _, _ = place()
@@ -176,9 +170,10 @@
 
 def far_kernel(lsize_ref, rsize_ref, *rest):
     direct_a, direct_b, passed_a, passed_b, right_own, right_other = rest[:6]
-    near_ref, wide_ref, sent_ref, out_ref = rest[6:]
+    near_ref, psi_ref, sent_ref, out_ref = rest[6:]
     z, x, _ = place()
-    columns = range(out_ref.shape[0])
+    sectors, tile = out_ref.shape[0], out_ref.shape[-1]
+    columns = range(sectors)
     far_leaves = lax.shift_right_logical(z, 1) == x
 
     def store_sent(b, a, total):
@@ -198,9 +193,12 @@
             def _(store=store, distance=distance, first=first, second=second):
                 lefts, rights = zip(message(first, right_own), message(second, right_other))
                 sizes = (lsize_ref, rsize_ref)
-                partial_sums(
-                    z, distance, sizes, columns, lambda a: wide_ref[a], lefts, rights, store
-                )
+
+                def psi(a):
+                    blocks = [psi_ref[pl.ds((sectors * a + b) * tile, tile)] for b in columns]
+                    return wide_psi(z, distance, sizes, a, columns, blocks)
+
+                partial_sums(z, distance, sizes, columns, psi, lefts, rights, store)
 
 
 def shards(psi, left_ops, right_ops, term_blocks, left_sizes, right_sizes):
@@ -230,12 +228,12 @@
         out_shape=[
             block(message_shape),
             block(message_shape),
-            block(out_shape),
+            block((sectors * sectors * tile + FAR_PAD, tile)),
             block(right_ops.shape),
         ],
         in_specs=[SMEM, ANY, ANY, ANY],
         out_specs=[VMEM] * 4,
-        scratch_shapes=[pltpu.SemaphoreType.DMA((4 * sectors + 2,))],
+        scratch_shapes=[pltpu.SemaphoreType.DMA((4 * sectors + 1 + sectors**2,))],
         compiler_params=PARAMS,
         name="pack",
     )(blocks_hbm, psi_hbm, left_hbm, right_hbm)
@@ -267,14 +265,9 @@
         near_kernel, "near", [total], sizes + (term_blocks,),
         [psi, left_ops, side, direct_a, direct_b] + rights,
     )
-    psi_turn, near = lax.optimization_barrier((psi_far, near))
-    (wide,) = apply(
-        mask_kernel, "mask", [block((sectors, tile, sectors * tile))], sizes,
-        [psi_turn],
-    )
     sent, far = apply(
         far_kernel, "far", [block(out_shape), total], sizes,
-        [direct_a, direct_b, passed_a, passed_b] + rights + [near, wide],
+        [direct_a, direct_b, passed_a, passed_b] + rights + [near, psi_far],
     )
     arrived = over_op(sent, 2)
     kept = jnp.where(lax.axis_index("blk") // 2 == lax.axis_index("op") // 2, near, far)

time: 27.7 us -> 27.9 us (level)
  waiting for transfers between devices: 8.38 us -> 9.09 us
  Pallas kernels: 5.07 us -> 4.44 us
    pallas_call x3 -> x2, Pallas kernels: 3.04 us -> 2.44 us  [apply(): pl.pallas_call(kernel, out_shape=outs, in_specs=[SMEM] * len(scalars) + [...]
    ppermute x2, waiting for transfers between devices: 4.1 us -> 4.56 us  [over_op(): return lax.ppermute(array, 'op', [(o, o ^ step) for o in range(n)])]
  transfers between devices with their start and end apart: 8 -> 8, of which waited for: 4 -> 4; matrix products, arithmetic and copies ran while one was open for 0% -> 0% of each run, Pallas kernels for 7% -> 4%
where the time goes in v8:
time: 27.9 us; the launch traced here: 27.7 us
  starting transfers between devices  13.4 us (48%)
  waiting for transfers between devices  9.09 us (33%)
  Pallas kernels  4.44 us (16%)
  other arithmetic  0.69 us (2%)
    ppermute x6, starting transfers between devices, over_z(): return lax.ppermute(array, ('blk', 'op'), pairs)  11.3 us
    ppermute x2, waiting for transfers between devices, over_op(): return lax.ppermute(array, 'op', [(o, o ^ step) for o in range(n)])  4.56 us
    ppermute x6, waiting for transfers between devices, over_z(): return lax.ppermute(array, ('blk', 'op'), pairs)  4.53 us
    pallas_call x2, Pallas kernels, apply(): pl.pallas_call(kernel, out_shape=outs, in_specs=[SMEM] * len(scalars) + [...  2.44 us
    ppermute x2, starting transfers between devices, over_op(): return lax.ppermute(array, 'op', [(o, o ^ step) for o in range(n)])  2.09 us
    pallas_call x1, Pallas kernels, shards(): pl.pallas_call(pack_kernel, out_shape=[block(message_shape), block(messag...  2 us
    convert_element_type x1, other arithmetic, shards(): return (kept + arrived.astype(jnp.float32)).astype(jnp.bfloat16)  0.69 us
  transfers between devices with their start and end apart: 8, of which 4 were waited for; matrix products, arithmetic and copies ran while one was open for 0% of the time, Pallas kernels for 4%

profile of v8, /device:TPU:0, one launch (start us, length us, event | category | flops | bytes accessed | tf_op | source)
XLA Modules:
  0.0 27.7 jit_solution(16681622889263330265)
XLA Ops:
  0.0 2.0 %pack.1 = (bf16[528,128]{1,0:T(8,128)(2,1)S(1)}, bf16[528,128]{1,0:T(8,128)(2,1)S(1)}, bf16[544,128]{1,0:T(8,128)(2,1)S(1)}, bf16[4,2,128,128]{3,2,1,0:T(8,128)(2,1)S(1)}) custom-call(s32[4,8]{1,0:T(4,128)} %blocks_ref.3, bf16[2,8,128,128]{3,2,1,0:T(8,128)(2,1)} %rest_0_.1, bf16[4,2,128,128]{3,2,1,0:T(8,128)(2,1)} %rest_1_.1, bf16[4,2,128,128]{3,2,1,0:T(8,128)(2,1)} %right_ref.1), custom_call_target="tpu_custom_call" | custom-call | tf_op jit(solution)/shard_map/pack/pallas_call | solution.py:226
  2.0 0.5 %collective-permute-start.3 = (bf16[4,2,128,128]{3,2,1,0:T(8,128)(2,1)S(1)}, bf16[4,2,128,128]{3,2,1,0:T(8,128)(2,1)S(1)}, u32[]{:S(2)}, u32[]{:S(2)}) collective-permute-start(bf16[4,2,128,128]{3,2,1,0:T(8,128)(2,1)S(1)} %get-tuple-element.13.rest_5_.rest_4_), channel_id=1, source_target_pairs={{0,1},{1,0},{2,3},{3,2},{4,5},{5,4},{6,7},{7,6},{8,9},{9,8},{10,11... | collective-permute-start | bytes 786440 | tf_op jit(solution)/shard_map/ppermute | solution.py:212
  2.5 3.7 %collective-permute-start.1 = (bf16[528,128]{1,0:T(8,128)(2,1)S(1)}, bf16[528,128]{1,0:T(8,128)(2,1)S(1)}, u32[]{:S(2)}, u32[]{:S(2)}) collective-permute-start(bf16[528,128]{1,0:T(8,128)(2,1)S(1)} %get-tuple-element.12), channel_id=1, source_target_pairs={{0,8},{1,4},{2,10},{3,6},{4,1},{5,13},{6,3},{7,15},{8,0},{9,12},{1... | collective-permute-start | bytes 405512 | tf_op jit(solution)/shard_map/ppermute | solution.py:220
  6.2 0.0 collective-permute-start.2
  6.2 1.7 %collective-permute-start = (bf16[528,128]{1,0:T(8,128)(2,1)S(1)}, bf16[528,128]{1,0:T(8,128)(2,1)S(1)}, u32[]{:S(2)}, u32[]{:S(2)}) collective-permute-start(bf16[528,128]{1,0:T(8,128)(2,1)S(1)} %get-tuple-element.11), channel_id=1, source_target_pairs={{0,4},{1,0},{2,6},{3,2},{4,5},{5,1},{6,7},{7,3},{8,12},{9,8},{10,1... | collective-permute-start | bytes 405512 | tf_op jit(solution)/shard_map/ppermute | solution.py:220
  7.9 2.6 %collective-permute-start.6 = (bf16[544,128]{1,0:T(8,128)(2,1)S(1)}, bf16[544,128]{1,0:T(8,128)(2,1)S(1)}, u32[]{:S(2)}, u32[]{:S(2)}) collective-permute-start(bf16[544,128]{1,0:T(8,128)(2,1)S(1)} %get-tuple-element.14), channel_id=1, source_target_pairs={{0,8},{1,12},{2,10},{3,14},{4,9},{5,13},{6,11},{7,15},{8,0},{9,4},... | collective-permute-start | bytes 417800 | tf_op jit(solution)/shard_map/ppermute | solution.py:220
  10.5 0.3 %collective-permute-done.1.rest_3_.rest_0_ = bf16[528,128]{1,0:T(8,128)(2,1)S(1)} collective-permute-done((bf16[528,128]{1,0:T(8,128)(2,1)S(1)}, bf16[528,128]{1,0:T(8,128)(2,1)S(1)}, u32[]{:S(2)}, u32[]{:S(2)}) %collective-permute-start.1) | collective-permute-done | bytes 135200 | tf_op jit(solution)/shard_map/ppermute | solution.py:220
  10.8 0.0 collective-permute-start.4
  10.8 1.8 %collective-permute-done.2.rest_4_.rest_1_ = bf16[528,128]{1,0:T(8,128)(2,1)S(1)} collective-permute-done((bf16[528,128]{1,0:T(8,128)(2,1)S(1)}, bf16[528,128]{1,0:T(8,128)(2,1)S(1)}, u32[]{:S(2)}, u32[]{:S(2)}) %collective-permute-start.2) | collective-permute-done | bytes 135200 | tf_op jit(solution)/shard_map/ppermute | solution.py:220
  12.6 3.4 %collective-permute-start.5 = (bf16[528,128]{1,0:T(8,128)(2,1)S(1)}, bf16[528,128]{1,0:T(8,128)(2,1)S(1)}, u32[]{:S(2)}, u32[]{:S(2)}) collective-permute-start(bf16[528,128]{1,0:T(8,128)(2,1)S(1)} %collective-permute-done.2.rest_4_.rest_1_), channel_id=1, source_target_pairs={{0,4},{1,0},{2,6},{3,2},{4,5},{5,1},{6,7},{7,3},{8,12},{9,8},{10,1... | collective-permute-start | bytes 405512 | tf_op jit(solution)/shard_map/ppermute | solution.py:220
  16.0 0.0 collective-permute-done.rest_2_
  16.0 0.0 collective-permute-done.3.rest_6_.rest_5_
  16.0 0.0 copy-done.1
  16.0 0.0 copy-done.2
  16.0 0.0 copy-done.3
  16.0 0.0 copy-done.4
  16.0 1.2 %near.1.rest_6_ = f32[2,2,128,128]{3,2,1,0:T(8,128)S(1)} custom-call(s32[8]{0:T(128)S(1)} %copy-done.3, s32[8]{0:T(128)S(1)} %copy-done.4, s32[4,8]{1,0:T(4,128)S(1)} %copy-done.2, bf16[2,8,128,128]{3,2,1,0:T(8,128)(2,1)S(1)} %copy-done, bf16[4,2,128,128]{3,2,1,0:T(8,128)(2,1)S(1)} %copy-done.1, bf16[528,128]{1,0:T(8,128)(2,1)S(1)} %collective-permute-done.rest_2_, ...), custom_call_target="tpu_custom_call" | custom-call | flops 536870912 | bytes 1048576 | tf_op jit(solution)/shard_map/near/pallas_call | solution.py:249
  17.3 2.4 %collective-permute-done.6.rest_7_ = bf16[544,128]{1,0:T(8,128)(2,1)S(1)} collective-permute-done((bf16[544,128]{1,0:T(8,128)(2,1)S(1)}, bf16[544,128]{1,0:T(8,128)(2,1)S(1)}, u32[]{:S(2)}, u32[]{:S(2)}) %collective-permute-start.6) | collective-permute-done | bytes 139296 | tf_op jit(solution)/shard_map/ppermute | solution.py:220
  19.7 0.0 collective-permute-done.4.rest_2_
  19.7 0.0 collective-permute-done.5.rest_3_
  19.7 1.2 %far.1 = (bf16[2,2,128,128]{3,2,1,0:T(8,128)(2,1)S(1)}, f32[2,2,128,128]{3,2,1,0:T(8,128)S(1)}) custom-call(s32[8]{0:T(128)S(1)} %copy-done.3, s32[8]{0:T(128)S(1)} %copy-done.4, bf16[528,128]{1,0:T(8,128)(2,1)S(1)} %collective-permute-done.1.rest_3_.rest_0_, bf16[528,128]{1,0:T(8,128)(2,1)S(1)} %collective-permute-done.2.rest_4_.rest_1_, ...), custom_call_target="tpu_custom_call" | custom-call | flops 536870912 | bytes 1048576 | tf_op jit(solution)/shard_map/far/pallas_call | solution.py:249
  20.9 1.6 %collective-permute-start.7 = (bf16[2,2,128,128]{3,2,1,0:T(8,128)(2,1)S(1)}, bf16[2,2,128,128]{3,2,1,0:T(8,128)(2,1)S(1)}, u32[]{:S(2)}, u32[]{:S(2)}) collective-permute-start(bf16[2,2,128,128]{3,2,1,0:T(8,128)(2,1)S(1)} %get-tuple-element.16), channel_id=1, source_target_pairs={{0,2},{1,3},{2,0},{3,1},{4,6},{5,7},{6,4},{7,5},{8,10},{9,11},{10,... | collective-permute-start | bytes 393224 | tf_op jit(solution)/shard_map/ppermute | solution.py:212
  22.5 4.6 %collective-permute-done.7 = bf16[2,2,128,128]{3,2,1,0:T(8,128)(2,1)S(1)} collective-permute-done((bf16[2,2,128,128]{3,2,1,0:T(8,128)(2,1)S(1)}, bf16[2,2,128,128]{3,2,1,0:T(8,128)(2,1)S(1)}, u32[]{:S(2)}, u32[]{:S(2)}) %collective-permute-start.7) | collective-permute-done | bytes 131104 | tf_op jit(solution)/shard_map/ppermute | solution.py:212
  27.0 0.7 %add_convert_fusion = bf16[2,2,128,128]{3,2,1,0:T(8,128)(2,1)} fusion(bf16[2,2,128,128]{3,2,1,0:T(8,128)(2,1)S(1)} %collective-permute-done.7, f32[2,2,128,128]{3,2,1,0:T(8,128)S(1)} %near.1.rest_6_, f32[2,2,128,128]{3,2,1,0:T(8,128)S(1)} %get-tuple-element.15, pred[]{:T(512)S(6)} %eq.3), kind=kLoop, calls=%fused_computation | loop fusion | flops 262144 | bytes 786433 | tf_op jit(solution)/shard_map/convert_element_type | solution.py:274
  (6 shorter events, 0.0 us)
Async XLA Ops:
  0.0 16.0 %copy-start = (bf16[2,8,128,128]{3,2,1,0:T(8,128)(2,1)S(1)}, bf16[2,8,128,128]{3,2,1,0:T(8,128)(2,1)}, u32[]{:S(2)}) copy-start(bf16[2,8,128,128]{3,2,1,0:T(8,128)(2,1)} %rest_0_.1) | copy-start | bytes 1572868
  0.0 16.0 %copy-start.1 = (bf16[4,2,128,128]{3,2,1,0:T(8,128)(2,1)S(1)}, bf16[4,2,128,128]{3,2,1,0:T(8,128)(2,1)}, u32[]{:S(2)}) copy-start(bf16[4,2,128,128]{3,2,1,0:T(8,128)(2,1)} %rest_1_.1) | copy-start | bytes 786436
  2.0 14.0 %collective-permute-start.3 = (bf16[4,2,128,128]{3,2,1,0:T(8,128)(2,1)S(1)}, bf16[4,2,128,128]{3,2,1,0:T(8,128)(2,1)S(1)}, u32[]{:S(2)}, u32[]{:S(2)}) collective-permute-start(bf16[4,2,128,128]{3,2,1,0:T(8,128)(2,1)S(1)} %get-tuple-element.13.rest_5_.rest_4_), channel_id=1, source_target_pairs={{0,1},{1,0},{2,3},{3,2},{4,5},{5,4},{6,7},{7,6},{8,9},{9,8},{10,11... | collective-permute-start | bytes 786440 | tf_op jit(solution)/shard_map/ppermute | solution.py:212
  2.5 13.5 %copy-start.2 = (s32[4,8]{1,0:T(4,128)S(1)}, s32[4,8]{1,0:T(4,128)}, u32[]{:S(2)}) copy-start(s32[4,8]{1,0:T(4,128)} %blocks_ref.3) | copy-start | bytes 388
  2.5 8.2 %collective-permute-start.1 = (bf16[528,128]{1,0:T(8,128)(2,1)S(1)}, bf16[528,128]{1,0:T(8,128)(2,1)S(1)}, u32[]{:S(2)}, u32[]{:S(2)}) collective-permute-start(bf16[528,128]{1,0:T(8,128)(2,1)S(1)} %get-tuple-element.12), channel_id=1, source_target_pairs={{0,8},{1,4},{2,10},{3,6},{4,1},{5,13},{6,3},{7,15},{8,0},{9,12},{1... | collective-permute-start | bytes 405512 | tf_op jit(solution)/shard_map/ppermute | solution.py:220
  6.2 6.4 %collective-permute-start.2 = (bf16[528,128]{1,0:T(8,128)(2,1)S(1)}, bf16[528,128]{1,0:T(8,128)(2,1)S(1)}, u32[]{:S(2)}, u32[]{:S(2)}) collective-permute-start(bf16[528,128]{1,0:T(8,128)(2,1)S(1)} %get-tuple-element.12), channel_id=1, source_target_pairs={{0,4},{1,8},{2,6},{3,10},{4,13},{5,1},{6,15},{7,3},{8,12},{9,0},{1... | collective-permute-start | bytes 405512 | tf_op jit(solution)/shard_map/ppermute | solution.py:220
  6.2 9.8 %copy-start.3 = (s32[8]{0:T(128)S(1)}, s32[8]{0:T(128)}, u32[]{:S(2)}) copy-start(s32[8]{0:T(128)} %lsize_ref.3) | copy-start | bytes 100
  6.2 9.8 %copy-start.4 = (s32[8]{0:T(128)S(1)}, s32[8]{0:T(128)}, u32[]{:S(2)}) copy-start(s32[8]{0:T(128)} %rsize_ref.3) | copy-start | bytes 100
  6.2 9.8 %collective-permute-start = (bf16[528,128]{1,0:T(8,128)(2,1)S(1)}, bf16[528,128]{1,0:T(8,128)(2,1)S(1)}, u32[]{:S(2)}, u32[]{:S(2)}) collective-permute-start(bf16[528,128]{1,0:T(8,128)(2,1)S(1)} %get-tuple-element.11), channel_id=1, source_target_pairs={{0,4},{1,0},{2,6},{3,2},{4,5},{5,1},{6,7},{7,3},{8,12},{9,8},{10,1... | collective-permute-start | bytes 405512 | tf_op jit(solution)/shard_map/ppermute | solution.py:220
  7.9 11.8 %collective-permute-start.6 = (bf16[544,128]{1,0:T(8,128)(2,1)S(1)}, bf16[544,128]{1,0:T(8,128)(2,1)S(1)}, u32[]{:S(2)}, u32[]{:S(2)}) collective-permute-start(bf16[544,128]{1,0:T(8,128)(2,1)S(1)} %get-tuple-element.14), channel_id=1, source_target_pairs={{0,8},{1,12},{2,10},{3,14},{4,9},{5,13},{6,11},{7,15},{8,0},{9,4},... | collective-permute-start | bytes 417800 | tf_op jit(solution)/shard_map/ppermute | solution.py:220
  10.8 8.9 %collective-permute-start.4 = (bf16[528,128]{1,0:T(8,128)(2,1)S(1)}, bf16[528,128]{1,0:T(8,128)(2,1)S(1)}, u32[]{:S(2)}, u32[]{:S(2)}) collective-permute-start(bf16[528,128]{1,0:T(8,128)(2,1)S(1)} %collective-permute-done.1.rest_3_.rest_0_), channel_id=1, source_target_pairs={{0,4},{1,0},{2,6},{3,2},{4,5},{5,1},{6,7},{7,3},{8,12},{9,8},{10,1... | collective-permute-start | bytes 405512 | tf_op jit(solution)/shard_map/ppermute | solution.py:220
  12.6 7.1 %collective-permute-start.5 = (bf16[528,128]{1,0:T(8,128)(2,1)S(1)}, bf16[528,128]{1,0:T(8,128)(2,1)S(1)}, u32[]{:S(2)}, u32[]{:S(2)}) collective-permute-start(bf16[528,128]{1,0:T(8,128)(2,1)S(1)} %collective-permute-done.2.rest_4_.rest_1_), channel_id=1, source_target_pairs={{0,4},{1,0},{2,6},{3,2},{4,5},{5,1},{6,7},{7,3},{8,12},{9,8},{10,1... | collective-permute-start | bytes 405512 | tf_op jit(solution)/shard_map/ppermute | solution.py:220
  20.9 6.1 %collective-permute-start.7 = (bf16[2,2,128,128]{3,2,1,0:T(8,128)(2,1)S(1)}, bf16[2,2,128,128]{3,2,1,0:T(8,128)(2,1)S(1)}, u32[]{:S(2)}, u32[]{:S(2)}) collective-permute-start(bf16[2,2,128,128]{3,2,1,0:T(8,128)(2,1)S(1)} %get-tuple-element.16), channel_id=1, source_target_pairs={{0,2},{1,3},{2,0},{3,1},{4,6},{5,7},{6,4},{7,5},{8,10},{9,11},{10,... | collective-permute-start | bytes 393224 | tf_op jit(solution)/shard_map/ppermute | solution.py:212

commit v9 on v8

--- a/solution.py
+++ b/solution.py
@@ -170,18 +170,19 @@
 
 def far_kernel(lsize_ref, rsize_ref, *rest):
     direct_a, direct_b, passed_a, passed_b, right_own, right_other = rest[:6]
-    near_ref, psi_ref, sent_ref, out_ref = rest[6:]
+    near_ref, psi_ref, out_ref = rest[6:9]
+    sent_refs = rest[9:]
     z, x, _ = place()
     sectors, tile = out_ref.shape[0], out_ref.shape[-1]
     columns = range(sectors)
     far_leaves = lax.shift_right_logical(z, 1) == x
 
     def store_sent(b, a, total):
-        sent_ref[b, a] = total.astype(sent_ref.dtype)
+        sent_refs[b][a] = total.astype(sent_refs[b].dtype)
 
     def store_kept(b, a, total):
         out_ref[b, a] = total
-        sent_ref[b, a] = near_ref[b, a].astype(sent_ref.dtype)
+        sent_refs[b][a] = near_ref[b, a].astype(sent_refs[b].dtype)
 
     for leaves, store in ((True, store_sent), (False, store_kept)):
         for at_home, distance, first, second in (
@@ -265,11 +266,13 @@
         near_kernel, "near", [total], sizes + (term_blocks,),
         [psi, left_ops, side, direct_a, direct_b] + rights,
     )
-    sent, far = apply(
-        far_kernel, "far", [block(out_shape), total], sizes,
+    far, *sent = apply(
+        far_kernel, "far", [total] + [block((sectors, tile, tile))] * sectors, sizes,
         [direct_a, direct_b, passed_a, passed_b] + rights + [near, psi_far],
     )
-    arrived = over_op(sent, 2)
+    first, second = [over_op(part, 2)[None] for part in sent]
+    places = lax.broadcasted_iota(jnp.int32, out_shape, 0)
+    arrived = jnp.where(places == 0, first, second)
     kept = jnp.where(lax.axis_index("blk") // 2 == lax.axis_index("op") // 2, near, far)
     return (kept + arrived.astype(jnp.float32)).astype(jnp.bfloat16)
 

time: 27.9 us -> 28 us (level)
  waiting for transfers between devices: 9.09 us -> 7.93 us
  local copies, waits for them, and re-layouts: 0.02 us -> 0.66 us
  starting transfers between devices: 13.4 us -> 13.9 us
    ppermute x6, waiting for transfers between devices: 4.53 us -> 3.88 us  [over_z(): return lax.ppermute(array, ('blk', 'op'), pairs)]
    unnamed x10, local copies, waits for them, and re-layouts: 0.02 us -> 0.66 us
    ppermute x2 -> x3, starting transfers between devices: 2.09 us -> 2.61 us  [over_op(): return lax.ppermute(array, 'op', [(o, o ^ step) for o in range(n)])]
    ppermute x2 -> x3, waiting for transfers between devices: 4.56 us -> 4.05 us  [over_op(): return lax.ppermute(array, 'op', [(o, o ^ step) for o in range(n)])]
  transfers between devices with their start and end apart: 8 -> 9, of which waited for: 4 -> 5; matrix products, arithmetic and copies ran while one was open for 0% -> 0% of each run, Pallas kernels for 4% -> 4%
where the time goes in v9:
time: 28 us; the launch traced here: 27.8 us
  starting transfers between devices  13.9 us (50%)
  waiting for transfers between devices  7.93 us (28%)
  Pallas kernels  4.43 us (16%)
  other arithmetic  0.78 us (3%)
  local copies, waits for them, and re-layouts  0.66 us (2%)
    ppermute x6, starting transfers between devices, over_z(): return lax.ppermute(array, ('blk', 'op'), pairs)  11.3 us
    ppermute x3, waiting for transfers between devices, over_op(): return lax.ppermute(array, 'op', [(o, o ^ step) for o in range(n)])  4.05 us
    ppermute x6, waiting for transfers between devices, over_z(): return lax.ppermute(array, ('blk', 'op'), pairs)  3.88 us
    ppermute x3, starting transfers between devices, over_op(): return lax.ppermute(array, 'op', [(o, o ^ step) for o in range(n)])  2.61 us
    pallas_call x2, Pallas kernels, apply(): pl.pallas_call(kernel, out_shape=outs, in_specs=[SMEM] * len(scalars) + [...  2.44 us
    pallas_call x1, Pallas kernels, shards(): pl.pallas_call(pack_kernel, out_shape=[block(message_shape), block(messag...  2 us
    convert_element_type x1, other arithmetic, shards(): return (kept + arrived.astype(jnp.float32)).astype(jnp.bfloat16)  0.77 us
    unnamed x10, local copies, waits for them, and re-layouts  0.66 us
  transfers between devices with their start and end apart: 9, of which 5 were waited for; matrix products, arithmetic and copies ran while one was open for 0% of the time, Pallas kernels for 4%

profile of v9, /device:TPU:0, one launch (start us, length us, event | category | flops | bytes accessed | tf_op | source)
XLA Modules:
  0.0 27.8 jit_solution(1758540013535633987)
XLA Ops:
  0.0 2.0 %pack.1 = (bf16[528,128]{1,0:T(8,128)(2,1)S(1)}, bf16[528,128]{1,0:T(8,128)(2,1)S(1)}, bf16[544,128]{1,0:T(8,128)(2,1)S(1)}, bf16[4,2,128,128]{3,2,1,0:T(8,128)(2,1)S(1)}) custom-call(s32[4,8]{1,0:T(4,128)} %blocks_ref.3, bf16[2,8,128,128]{3,2,1,0:T(8,128)(2,1)} %rest_0_.1, bf16[4,2,128,128]{3,2,1,0:T(8,128)(2,1)} %rest_1_.1, bf16[4,2,128,128]{3,2,1,0:T(8,128)(2,1)} %right_ref.1), custom_call_target="tpu_custom_call" | custom-call | tf_op jit(solution)/shard_map/pack/pallas_call | solution.py:227
  2.0 0.5 %collective-permute-start.3 = (bf16[4,2,128,128]{3,2,1,0:T(8,128)(2,1)S(1)}, bf16[4,2,128,128]{3,2,1,0:T(8,128)(2,1)S(1)}, u32[]{:S(2)}, u32[]{:S(2)}) collective-permute-start(bf16[4,2,128,128]{3,2,1,0:T(8,128)(2,1)S(1)} %get-tuple-element.14.rest_5_.rest_4_), channel_id=1, source_target_pairs={{0,1},{1,0},{2,3},{3,2},{4,5},{5,4},{6,7},{7,6},{8,9},{9,8},{10,11... | collective-permute-start | bytes 786440 | tf_op jit(solution)/shard_map/ppermute | solution.py:213
  2.5 3.7 %collective-permute-start.1 = (bf16[528,128]{1,0:T(8,128)(2,1)S(1)}, bf16[528,128]{1,0:T(8,128)(2,1)S(1)}, u32[]{:S(2)}, u32[]{:S(2)}) collective-permute-start(bf16[528,128]{1,0:T(8,128)(2,1)S(1)} %get-tuple-element.13), channel_id=1, source_target_pairs={{0,8},{1,4},{2,10},{3,6},{4,1},{5,13},{6,3},{7,15},{8,0},{9,12},{1... | collective-permute-start | bytes 405512 | tf_op jit(solution)/shard_map/ppermute | solution.py:221
  6.2 0.0 collective-permute-start.2
  6.2 1.7 %collective-permute-start = (bf16[528,128]{1,0:T(8,128)(2,1)S(1)}, bf16[528,128]{1,0:T(8,128)(2,1)S(1)}, u32[]{:S(2)}, u32[]{:S(2)}) collective-permute-start(bf16[528,128]{1,0:T(8,128)(2,1)S(1)} %get-tuple-element.12), channel_id=1, source_target_pairs={{0,4},{1,0},{2,6},{3,2},{4,5},{5,1},{6,7},{7,3},{8,12},{9,8},{10,1... | collective-permute-start | bytes 405512 | tf_op jit(solution)/shard_map/ppermute | solution.py:221
  7.9 2.6 %collective-permute-start.6 = (bf16[544,128]{1,0:T(8,128)(2,1)S(1)}, bf16[544,128]{1,0:T(8,128)(2,1)S(1)}, u32[]{:S(2)}, u32[]{:S(2)}) collective-permute-start(bf16[544,128]{1,0:T(8,128)(2,1)S(1)} %get-tuple-element.15), channel_id=1, source_target_pairs={{0,8},{1,12},{2,10},{3,14},{4,9},{5,13},{6,11},{7,15},{8,0},{9,4},... | collective-permute-start | bytes 417800 | tf_op jit(solution)/shard_map/ppermute | solution.py:221
  10.4 0.3 collective-permute-done.1.rest_3_.rest_0_
  10.7 0.0 collective-permute-start.4
  10.7 1.9 %collective-permute-done.2.rest_4_.rest_1_ = bf16[528,128]{1,0:T(8,128)(2,1)S(1)} collective-permute-done((bf16[528,128]{1,0:T(8,128)(2,1)S(1)}, bf16[528,128]{1,0:T(8,128)(2,1)S(1)}, u32[]{:S(2)}, u32[]{:S(2)}) %collective-permute-start.2) | collective-permute-done | bytes 135200 | tf_op jit(solution)/shard_map/ppermute | solution.py:221
  12.6 3.4 %collective-permute-start.5 = (bf16[528,128]{1,0:T(8,128)(2,1)S(1)}, bf16[528,128]{1,0:T(8,128)(2,1)S(1)}, u32[]{:S(2)}, u32[]{:S(2)}) collective-permute-start(bf16[528,128]{1,0:T(8,128)(2,1)S(1)} %collective-permute-done.2.rest_4_.rest_1_), channel_id=1, source_target_pairs={{0,4},{1,0},{2,6},{3,2},{4,5},{5,1},{6,7},{7,3},{8,12},{9,8},{10,1... | collective-permute-start | bytes 405512 | tf_op jit(solution)/shard_map/ppermute | solution.py:221
  16.0 0.0 collective-permute-done.rest_2_
  16.0 0.0 collective-permute-done.3.rest_6_.rest_5_
  16.0 0.6 %copy-done.2 = s32[4,8]{1,0:T(4,128)S(1)} copy-done((s32[4,8]{1,0:T(4,128)S(1)}, s32[4,8]{1,0:T(4,128)}, u32[]{:S(2)}) %copy-start.2) | copy-done | bytes 152
  16.7 0.0 copy-done.4
  16.7 1.2 %near.1.rest_6_ = f32[2,2,128,128]{3,2,1,0:T(8,128)S(1)} custom-call(s32[8]{0:T(128)S(1)} %copy-done.3, s32[8]{0:T(128)S(1)} %copy-done.4, s32[4,8]{1,0:T(4,128)S(1)} %copy-done.2, bf16[2,8,128,128]{3,2,1,0:T(8,128)(2,1)S(1)} %copy-done, bf16[4,2,128,128]{3,2,1,0:T(8,128)(2,1)S(1)} %copy-done.1, bf16[528,128]{1,0:T(8,128)(2,1)S(1)} %collective-permute-done.rest_2_, ...), custom_call_target="tpu_custom_call" | custom-call | flops 536870912 | bytes 1048576 | tf_op jit(solution)/shard_map/near/pallas_call | solution.py:250
  17.9 1.7 %collective-permute-done.6.rest_7_ = bf16[544,128]{1,0:T(8,128)(2,1)S(1)} collective-permute-done((bf16[544,128]{1,0:T(8,128)(2,1)S(1)}, bf16[544,128]{1,0:T(8,128)(2,1)S(1)}, u32[]{:S(2)}, u32[]{:S(2)}) %collective-permute-start.6) | collective-permute-done | bytes 139296 | tf_op jit(solution)/shard_map/ppermute | solution.py:221
  19.6 0.0 collective-permute-done.4.rest_2_
  19.6 0.0 collective-permute-done.5.rest_3_
  19.7 1.2 %far.1 = (f32[2,2,128,128]{3,2,1,0:T(8,128)S(1)}, bf16[2,128,128]{2,1,0:T(8,128)(2,1)S(1)}, bf16[2,128,128]{2,1,0:T(8,128)(2,1)S(1)}) custom-call(s32[8]{0:T(128)S(1)} %copy-done.3, s32[8]{0:T(128)S(1)} %copy-done.4, bf16[528,128]{1,0:T(8,128)(2,1)S(1)} %collective-permute-done.1.rest_3_.rest_0_, ...), custom_call_target="tpu_custom_call" | custom-call | flops 536870912 | bytes 1048576 | tf_op jit(solution)/shard_map/far/pallas_call | solution.py:250
  20.9 1.6 %collective-permute-start.8 = (bf16[2,128,128]{2,1,0:T(8,128)(2,1)S(1)}, bf16[2,128,128]{2,1,0:T(8,128)(2,1)S(1)}, u32[]{:S(2)}, u32[]{:S(2)}) collective-permute-start(bf16[2,128,128]{2,1,0:T(8,128)(2,1)S(1)} %get-tuple-element.18), channel_id=1, source_target_pairs={{0,2},{1,3},{2,0},{3,1},{4,6},{5,7},{6,4},{7,5},{8,10},{9,11},{10,... | collective-permute-start | bytes 196616 | tf_op jit(solution)/shard_map/ppermute | solution.py:213
  22.5 0.5 %collective-permute-start.7 = (bf16[2,128,128]{2,1,0:T(8,128)(2,1)S(1)}, bf16[2,128,128]{2,1,0:T(8,128)(2,1)S(1)}, u32[]{:S(2)}, u32[]{:S(2)}) collective-permute-start(bf16[2,128,128]{2,1,0:T(8,128)(2,1)S(1)} %get-tuple-element.17), channel_id=1, source_target_pairs={{0,2},{1,3},{2,0},{3,1},{4,6},{5,7},{6,4},{7,5},{8,10},{9,11},{10,... | collective-permute-start | bytes 196616 | tf_op jit(solution)/shard_map/ppermute | solution.py:213
  23.0 2.8 %collective-permute-done.8 = bf16[2,128,128]{2,1,0:T(8,128)(2,1)S(1)} collective-permute-done((bf16[2,128,128]{2,1,0:T(8,128)(2,1)S(1)}, bf16[2,128,128]{2,1,0:T(8,128)(2,1)S(1)}, u32[]{:S(2)}, u32[]{:S(2)}) %collective-permute-start.8) | collective-permute-done | bytes 65568 | tf_op jit(solution)/shard_map/ppermute | solution.py:213
  25.8 1.2 %collective-permute-done.7 = bf16[2,128,128]{2,1,0:T(8,128)(2,1)S(1)} collective-permute-done((bf16[2,128,128]{2,1,0:T(8,128)(2,1)S(1)}, bf16[2,128,128]{2,1,0:T(8,128)(2,1)S(1)}, u32[]{:S(2)}, u32[]{:S(2)}) %collective-permute-start.7) | collective-permute-done | bytes 65568 | tf_op jit(solution)/shard_map/ppermute | solution.py:213
  27.0 0.8 %add_convert_fusion = bf16[2,2,128,128]{3,2,1,0:T(8,128)(2,1)} fusion(f32[2,2,128,128]{3,2,1,0:T(8,128)S(1)} %near.1.rest_6_, f32[2,2,128,128]{3,2,1,0:T(8,128)S(1)} %get-tuple-element.16, pred[2]{0:T(512)(128)(4,1)S(1)} %iota_compare_fusion, pred[]{:T(512)S(6)} %eq.10, bf16[2,128,128]{2,1,0:T(8,128)(2,1)S(1)} %collective-permute-done.8, ...), kind=kLoop, calls=%fused_computation | loop fusion | flops 327680 | bytes 786435 | tf_op jit(solution)/shard_map/convert_element_type | solution.py:277
  (9 shorter events, 0.0 us)
Async XLA Ops:
  0.0 16.0 %copy-start = (bf16[2,8,128,128]{3,2,1,0:T(8,128)(2,1)S(1)}, bf16[2,8,128,128]{3,2,1,0:T(8,128)(2,1)}, u32[]{:S(2)}) copy-start(bf16[2,8,128,128]{3,2,1,0:T(8,128)(2,1)} %rest_0_.1) | copy-start | bytes 1572868
  0.0 16.0 %copy-start.1 = (bf16[4,2,128,128]{3,2,1,0:T(8,128)(2,1)S(1)}, bf16[4,2,128,128]{3,2,1,0:T(8,128)(2,1)}, u32[]{:S(2)}) copy-start(bf16[4,2,128,128]{3,2,1,0:T(8,128)(2,1)} %rest_1_.1) | copy-start | bytes 786436
  2.0 14.0 %collective-permute-start.3 = (bf16[4,2,128,128]{3,2,1,0:T(8,128)(2,1)S(1)}, bf16[4,2,128,128]{3,2,1,0:T(8,128)(2,1)S(1)}, u32[]{:S(2)}, u32[]{:S(2)}) collective-permute-start(bf16[4,2,128,128]{3,2,1,0:T(8,128)(2,1)S(1)} %get-tuple-element.14.rest_5_.rest_4_), channel_id=1, source_target_pairs={{0,1},{1,0},{2,3},{3,2},{4,5},{5,4},{6,7},{7,6},{8,9},{9,8},{10,11... | collective-permute-start | bytes 786440 | tf_op jit(solution)/shard_map/ppermute | solution.py:213
  2.5 8.2 %collective-permute-start.1 = (bf16[528,128]{1,0:T(8,128)(2,1)S(1)}, bf16[528,128]{1,0:T(8,128)(2,1)S(1)}, u32[]{:S(2)}, u32[]{:S(2)}) collective-permute-start(bf16[528,128]{1,0:T(8,128)(2,1)S(1)} %get-tuple-element.13), channel_id=1, source_target_pairs={{0,8},{1,4},{2,10},{3,6},{4,1},{5,13},{6,3},{7,15},{8,0},{9,12},{1... | collective-permute-start | bytes 405512 | tf_op jit(solution)/shard_map/ppermute | solution.py:221
  6.2 6.4 %collective-permute-start.2 = (bf16[528,128]{1,0:T(8,128)(2,1)S(1)}, bf16[528,128]{1,0:T(8,128)(2,1)S(1)}, u32[]{:S(2)}, u32[]{:S(2)}) collective-permute-start(bf16[528,128]{1,0:T(8,128)(2,1)S(1)} %get-tuple-element.13), channel_id=1, source_target_pairs={{0,4},{1,8},{2,6},{3,10},{4,13},{5,1},{6,15},{7,3},{8,12},{9,0},{1... | collective-permute-start | bytes 405512 | tf_op jit(solution)/shard_map/ppermute | solution.py:221
  6.2 9.8 %collective-permute-start = (bf16[528,128]{1,0:T(8,128)(2,1)S(1)}, bf16[528,128]{1,0:T(8,128)(2,1)S(1)}, u32[]{:S(2)}, u32[]{:S(2)}) collective-permute-start(bf16[528,128]{1,0:T(8,128)(2,1)S(1)} %get-tuple-element.12), channel_id=1, source_target_pairs={{0,4},{1,0},{2,6},{3,2},{4,5},{5,1},{6,7},{7,3},{8,12},{9,8},{10,1... | collective-permute-start | bytes 405512 | tf_op jit(solution)/shard_map/ppermute | solution.py:221
  7.9 11.8 %collective-permute-start.6 = (bf16[544,128]{1,0:T(8,128)(2,1)S(1)}, bf16[544,128]{1,0:T(8,128)(2,1)S(1)}, u32[]{:S(2)}, u32[]{:S(2)}) collective-permute-start(bf16[544,128]{1,0:T(8,128)(2,1)S(1)} %get-tuple-element.15), channel_id=1, source_target_pairs={{0,8},{1,12},{2,10},{3,14},{4,9},{5,13},{6,11},{7,15},{8,0},{9,4},... | collective-permute-start | bytes 417800 | tf_op jit(solution)/shard_map/ppermute | solution.py:221
  10.7 8.9 %collective-permute-start.4 = (bf16[528,128]{1,0:T(8,128)(2,1)S(1)}, bf16[528,128]{1,0:T(8,128)(2,1)S(1)}, u32[]{:S(2)}, u32[]{:S(2)}) collective-permute-start(bf16[528,128]{1,0:T(8,128)(2,1)S(1)} %collective-permute-done.1.rest_3_.rest_0_), channel_id=1, source_target_pairs={{0,4},{1,0},{2,6},{3,2},{4,5},{5,1},{6,7},{7,3},{8,12},{9,8},{10,1... | collective-permute-start | bytes 405512 | tf_op jit(solution)/shard_map/ppermute | solution.py:221
  12.6 7.1 %collective-permute-start.5 = (bf16[528,128]{1,0:T(8,128)(2,1)S(1)}, bf16[528,128]{1,0:T(8,128)(2,1)S(1)}, u32[]{:S(2)}, u32[]{:S(2)}) collective-permute-start(bf16[528,128]{1,0:T(8,128)(2,1)S(1)} %collective-permute-done.2.rest_4_.rest_1_), channel_id=1, source_target_pairs={{0,4},{1,0},{2,6},{3,2},{4,5},{5,1},{6,7},{7,3},{8,12},{9,8},{10,1... | collective-permute-start | bytes 405512 | tf_op jit(solution)/shard_map/ppermute | solution.py:221
  16.0 0.7 %copy-start.2 = (s32[4,8]{1,0:T(4,128)S(1)}, s32[4,8]{1,0:T(4,128)}, u32[]{:S(2)}) copy-start(s32[4,8]{1,0:T(4,128)} %blocks_ref.3) | copy-start | bytes 388
  16.0 0.7 %copy-start.3 = (s32[8]{0:T(128)S(1)}, s32[8]{0:T(128)}, u32[]{:S(2)}) copy-start(s32[8]{0:T(128)} %lsize_ref.3) | copy-start | bytes 100
  16.0 0.7 %copy-start.4 = (s32[8]{0:T(128)S(1)}, s32[8]{0:T(128)}, u32[]{:S(2)}) copy-start(s32[8]{0:T(128)} %rsize_ref.3) | copy-start | bytes 100
  20.9 4.9 %collective-permute-start.8 = (bf16[2,128,128]{2,1,0:T(8,128)(2,1)S(1)}, bf16[2,128,128]{2,1,0:T(8,128)(2,1)S(1)}, u32[]{:S(2)}, u32[]{:S(2)}) collective-permute-start(bf16[2,128,128]{2,1,0:T(8,128)(2,1)S(1)} %get-tuple-element.18), channel_id=1, source_target_pairs={{0,2},{1,3},{2,0},{3,1},{4,6},{5,7},{6,4},{7,5},{8,10},{9,11},{10,... | collective-permute-start | bytes 196616 | tf_op jit(solution)/shard_map/ppermute | solution.py:213
  22.5 4.5 %collective-permute-start.7 = (bf16[2,128,128]{2,1,0:T(8,128)(2,1)S(1)}, bf16[2,128,128]{2,1,0:T(8,128)(2,1)S(1)}, u32[]{:S(2)}, u32[]{:S(2)}) collective-permute-start(bf16[2,128,128]{2,1,0:T(8,128)(2,1)S(1)} %get-tuple-element.17), channel_id=1, source_target_pairs={{0,2},{1,3},{2,0},{3,1},{4,6},{5,7},{6,4},{7,5},{8,10},{9,11},{10,... | collective-permute-start | bytes 196616 | tf_op jit(solution)/shard_map/ppermute | solution.py:213

commit v10 on v8

--- a/solution.py
+++ b/solution.py
@@ -35,45 +35,64 @@
     return c == jnp.bitwise_and(z, 1)
 
 
-def pack_kernel(blocks_ref, psi_ref, left_ref, right_ref, *rest):
-    left_out, side_out, far_out, right_out, sem = rest
+def pack_kernel(blocks_hbm, psi_ref, left_ref, right_ref, *rest):
+    left_out, side_out, far_out, right_out, blocks_ref, left_all, sem = rest
     z, _, _ = place()
     sectors, tile = psi_ref.shape[0], psi_ref.shape[-1]
     count = 2 * sectors
+    near = jnp.bitwise_xor(z, 1) * sectors
+    far = jnp.bitwise_xor(z, jnp.where(is_home(), 2, 3)) * sectors
+
+    def psi_copies(column, out, first):
+        return [
+            pltpu.make_async_copy(
+                psi_ref.at[a, column + b],
+                out.at[pl.ds((sectors * a + b) * tile, tile)],
+                sem.at[first + sectors * a + b],
+            )
+            for a in range(sectors)
+            for b in range(sectors)
+        ]
+
+    table = pltpu.make_async_copy(blocks_hbm, blocks_ref, sem.at[0])
+    lefts = pltpu.make_async_copy(left_ref, left_all, sem.at[1])
+    others = [pltpu.make_async_copy(right_ref, right_out, sem.at[2])]
+    others += psi_copies(far, far_out, 3)
+    sides = psi_copies(near, side_out, 3 + sectors * sectors)
+    for copy in [table, lefts] + others:
+        copy.start()
+
+    @pl.when(is_home())
+    def _():
+        for copy in sides:
+            copy.start()
+
+    far_out[pl.ds(count * tile, FAR_PAD)] = jnp.zeros((FAR_PAD, tile), jnp.bfloat16)
+    table.wait()
     row = lax.broadcasted_iota(jnp.int32, (ID_ROWS, tile), 0)
     ids = jnp.zeros((ID_ROWS, tile), jnp.float32)
     picked = []
     for local in range(sectors):
         for term in acting_terms(blocks_ref, z * sectors + local):
             ids = jnp.where(row == len(picked), term.astype(jnp.float32), ids)
-            picked.append(left_ref.at[term, local])
-    near = jnp.bitwise_xor(z, 1) * sectors
-    asked = [psi_ref.at[a, near + b] for a in range(sectors) for b in range(sectors)]
-
-    def copies(sources, out, first):
-        return [
-            pltpu.make_async_copy(source, out.at[pl.ds(spot * tile, tile)], sem.at[first + spot])
-            for spot, source in enumerate(sources)
-        ]
-
-    far = jnp.bitwise_xor(z, jnp.where(is_home(), 2, 3)) * sectors
-    plain = copies(picked, left_out, 0)
-    plain.append(pltpu.make_async_copy(right_ref, right_out, sem.at[2 * count]))
-    wanted = [psi_ref.at[a, far + b] for a in range(sectors) for b in range(sectors)]
-    plain += copies(wanted, far_out, 2 * count + 1)
-    for copy in plain:
-        copy.start()
-    for at_home, sources in ((True, asked), (False, picked)):
-
-        @pl.when(is_home() == at_home)
-        def _(sources=sources):
-            for copy in copies(sources, side_out, count):
-                copy.start()
-
+            picked.append((term, local))
     for out in (left_out, side_out):
         out[pl.ds(count * tile, ID_ROWS)] = ids.astype(jnp.bfloat16)
-    far_out[pl.ds(count * tile, FAR_PAD)] = jnp.zeros((FAR_PAD, tile), jnp.bfloat16)
-    for copy in plain + copies(picked, side_out, count):
+    lefts.wait()
+    for spot, (term, local) in enumerate(picked):
+        left_out[pl.ds(spot * tile, tile)] = left_all[term, local]
+
+    @pl.when(is_home())
+    def _():
+        for copy in sides:
+            copy.wait()
+
+    @pl.when(jnp.logical_not(is_home()))
+    def _():
+        for spot, (term, local) in enumerate(picked):
+            side_out[pl.ds(spot * tile, tile)] = left_all[term, local]
+
+    for copy in others:
         copy.wait()
 
 
@@ -85,35 +104,31 @@
     return (rows < height) & (lanes < rsize_ref[z * sectors + b])
 
 
-def wide_psi(z, distance, sizes, a, columns, blocks):
-    tile = blocks[0].shape[-1]
+def wide_psi(keep, a, blocks):
     cut = []
-    for b, block in zip(columns, blocks):
-        keep = keep_mask(z, distance, sizes, a, b, len(blocks), tile)
-        cut.append(jnp.where(keep, block.astype(jnp.float32), 0.0).astype(jnp.bfloat16))
+    for b, block in enumerate(blocks):
+        cut.append(jnp.where(keep(a, b), block.astype(jnp.float32), 0.0).astype(jnp.bfloat16))
     return jnp.concatenate(cut, axis=1)
 
 
-def partial_sums(z, distance, sizes, columns, psi, lefts, rights, store):
-    sectors = len(columns)
+def partial_sums(sectors, keep, psi, lefts, rights, store):
     for a in range(sectors):
-        wide = psi(a)
+        wide = wide_psi(keep, a, psi(a))
         tile = wide.shape[0]
         applied = []
         for left in lefts:
             both = jnp.dot(left(a), wide, preferred_element_type=jnp.float32).astype(jnp.bfloat16)
             applied += [both[:tile], both[tile:]]
-        for side, b in enumerate(columns):
+        for b in range(sectors):
             picked = [right(a, slot, b) for right in rights for slot in range(2)]
-            column = [part[:, side * tile : (side + 1) * tile] for part in applied]
+            column = [part[:, b * tile : (b + 1) * tile] for part in applied]
             total = lax.dot_general(
                 jnp.concatenate(column, axis=1),
                 jnp.concatenate(picked, axis=1),
                 (((1,), (1,)), ((), ())),
                 preferred_element_type=jnp.float32,
             )
-            keep = keep_mask(z, distance, sizes, a, b, sectors, tile)
-            store(b, a, jnp.where(keep, total, 0.0))
+            store(b, a, jnp.where(keep(a, b), total, 0.0))
 
 
 def message(ref, right_ref):
@@ -135,24 +150,30 @@
 
 
 def near_kernel(lsize_ref, rsize_ref, blocks_ref, *rest):
-    psi_ref, left_ref, side, direct_a, direct_b, right_own, right_other, out_ref = rest
+    psi_ref, left_ref, side, direct_a, direct_b, right_own, right_other = rest[:7]
+    out_ref, mask_ref = rest[7:]
     z, _, _ = place()
     sectors, tile = out_ref.shape[0], out_ref.shape[-1]
-    sizes, columns = (lsize_ref, rsize_ref), range(sectors)
+    columns = range(sectors)
+
+    def masks(distance):
+        return lambda a, b: keep_mask(z, distance, (lsize_ref, rsize_ref), a, b, sectors, tile)
+
+    far = masks(jnp.where(is_home(), 2, 3))
+    for a in columns:
+        for b in columns:
+            mask_ref[a, b] = jnp.where(far(a, b), 1.0, 0.0).astype(mask_ref.dtype)
 
     def store(b, a, total):
         out_ref[b, a] = total
-
-    def masked(distance, a, blocks):
-        return wide_psi(z, distance, sizes, a, columns, blocks)
 
     @pl.when(is_home())
     def _():
         terms = [acting_terms(blocks_ref, z * sectors + a) for a in columns]
         left, right = message(side, right_other)
         partial_sums(
-            z, 0, sizes, columns,
-            lambda a: masked(0, a, [psi_ref[a, z * sectors + b] for b in columns]),
+            sectors, masks(0),
+            lambda a: [psi_ref[a, z * sectors + b] for b in columns],
             [lambda a: jnp.concatenate([left_ref[term, a] for term in terms[a]], axis=0), left],
             [lambda a, slot, b: right_own[terms[a][slot], b], right],
             store,
@@ -163,17 +184,16 @@
         lefts, rights = zip(message(direct_b, right_own), message(direct_a, right_other))
 
         def psi(a):
-            return masked(1, a, [side[pl.ds((sectors * a + b) * tile, tile)] for b in columns])
-
-        partial_sums(z, 1, sizes, columns, psi, lefts, rights, store)
-
-
-def far_kernel(lsize_ref, rsize_ref, *rest):
-    direct_a, direct_b, passed_a, passed_b, right_own, right_other = rest[:6]
-    near_ref, psi_ref, sent_ref, out_ref = rest[6:]
+            return [side[pl.ds((sectors * a + b) * tile, tile)] for b in columns]
+
+        partial_sums(sectors, masks(1), psi, lefts, rights, store)
+
+
+def far_kernel(*refs):
+    direct_a, direct_b, passed_a, passed_b, right_own, right_other = refs[:6]
+    near_ref, mask_ref, psi_ref, sent_ref, out_ref = refs[6:]
     z, x, _ = place()
     sectors, tile = out_ref.shape[0], out_ref.shape[-1]
-    columns = range(sectors)
     far_leaves = lax.shift_right_logical(z, 1) == x
 
     def store_sent(b, a, total):
@@ -183,22 +203,22 @@
         out_ref[b, a] = total
         sent_ref[b, a] = near_ref[b, a].astype(sent_ref.dtype)
 
+    def keep(a, b):
+        return mask_ref[a, b].astype(jnp.float32) > 0
+
+    def psi(a):
+        return [psi_ref[pl.ds((sectors * a + b) * tile, tile)] for b in range(sectors)]
+
     for leaves, store in ((True, store_sent), (False, store_kept)):
-        for at_home, distance, first, second in (
-            (True, 2, direct_a, direct_b),
-            (False, 3, passed_a, passed_b),
+        for at_home, first, second in (
+            (True, direct_a, direct_b),
+            (False, passed_a, passed_b),
         ):
 
             @pl.when((is_home() == at_home) & (far_leaves == leaves))
-            def _(store=store, distance=distance, first=first, second=second):
+            def _(store=store, first=first, second=second):
                 lefts, rights = zip(message(first, right_own), message(second, right_other))
-                sizes = (lsize_ref, rsize_ref)
-
-                def psi(a):
-                    blocks = [psi_ref[pl.ds((sectors * a + b) * tile, tile)] for b in columns]
-                    return wide_psi(z, distance, sizes, a, columns, blocks)
-
-                partial_sums(z, distance, sizes, columns, psi, lefts, rights, store)
+                partial_sums(sectors, keep, psi, lefts, rights, store)
 
 
 def shards(psi, left_ops, right_ops, term_blocks, left_sizes, right_sizes):
@@ -231,9 +251,13 @@
             block((sectors * sectors * tile + FAR_PAD, tile)),
             block(right_ops.shape),
         ],
-        in_specs=[SMEM, ANY, ANY, ANY],
+        in_specs=[ANY] * 4,
         out_specs=[VMEM] * 4,
-        scratch_shapes=[pltpu.SemaphoreType.DMA((4 * sectors + 1 + sectors**2,))],
+        scratch_shapes=[
+            pltpu.SMEM(term_blocks.shape, jnp.int32),
+            pltpu.VMEM(left_ops.shape, jnp.bfloat16),
+            pltpu.SemaphoreType.DMA((3 + 2 * sectors**2,)),
+        ],
         compiler_params=PARAMS,
         name="pack",
     )(blocks_hbm, psi_hbm, left_hbm, right_hbm)
@@ -261,13 +285,13 @@
     sizes = (left_sizes, right_sizes)
     rights = [right_own, right_other]
     total = jax.ShapeDtypeStruct(out_shape, jnp.float32)
-    (near,) = apply(
-        near_kernel, "near", [total], sizes + (term_blocks,),
+    near, far_mask = apply(
+        near_kernel, "near", [total, block(out_shape)], sizes + (term_blocks,),
         [psi, left_ops, side, direct_a, direct_b] + rights,
     )
     sent, far = apply(
-        far_kernel, "far", [block(out_shape), total], sizes,
-        [direct_a, direct_b, passed_a, passed_b] + rights + [near, psi_far],
+        far_kernel, "far", [block(out_shape), total], (),
+        [direct_a, direct_b, passed_a, passed_b] + rights + [near, far_mask, psi_far],
     )
     arrived = over_op(sent, 2)
     kept = jnp.where(lax.axis_index("blk") // 2 == lax.axis_index("op") // 2, near, far)

time: 27.9 us -> 26.5 us (0.950)
  Pallas kernels: 4.44 us -> 3.13 us
    pallas_call x1, Pallas kernels: 2 us -> 1.21 us  [shards(): pl.pallas_call(pack_kernel, out_shape=[block(message_shape), block(messag...]
    pallas_call x2, Pallas kernels: 2.44 us -> 1.93 us  [apply(): pl.pallas_call(kernel, out_shape=outs, in_specs=[SMEM] * len(scalars) + [...]
  transfers between devices with their start and end apart: 8 -> 8, of which waited for: 4 -> 4; matrix products, arithmetic and copies ran while one was open for 0% -> 0% of each run, Pallas kernels for 4% -> 5%
where the time goes in v10:
time: 26.5 us; the launch traced here: 26.4 us
  starting transfers between devices  13.4 us (51%)
  waiting for transfers between devices  9.07 us (34%)
  Pallas kernels  3.13 us (12%)
  other arithmetic  0.69 us (3%)
    ppermute x6, starting transfers between devices, over_z(): return lax.ppermute(array, ('blk', 'op'), pairs)  11.3 us
    ppermute x2, waiting for transfers between devices, over_op(): return lax.ppermute(array, 'op', [(o, o ^ step) for o in range(n)])  4.58 us
    ppermute x6, waiting for transfers between devices, over_z(): return lax.ppermute(array, ('blk', 'op'), pairs)  4.5 us
    ppermute x2, starting transfers between devices, over_op(): return lax.ppermute(array, 'op', [(o, o ^ step) for o in range(n)])  2.08 us
    pallas_call x2, Pallas kernels, apply(): pl.pallas_call(kernel, out_shape=outs, in_specs=[SMEM] * len(scalars) + [...  1.93 us
    pallas_call x1, Pallas kernels, shards(): pl.pallas_call(pack_kernel, out_shape=[block(message_shape), block(messag...  1.21 us
    convert_element_type x1, other arithmetic, shards(): return (kept + arrived.astype(jnp.float32)).astype(jnp.bfloat16)  0.69 us
  transfers between devices with their start and end apart: 8, of which 4 were waited for; matrix products, arithmetic and copies ran while one was open for 0% of the time, Pallas kernels for 5%

profile of v10, /device:TPU:0, one launch (start us, length us, event | category | flops | bytes accessed | tf_op | source)
XLA Modules:
  0.0 26.4 jit_solution(16295533806178067751)
XLA Ops:
  0.0 1.2 %pack.1 = (bf16[528,128]{1,0:T(8,128)(2,1)S(1)}, bf16[528,128]{1,0:T(8,128)(2,1)S(1)}, bf16[544,128]{1,0:T(8,128)(2,1)S(1)}, bf16[4,2,128,128]{3,2,1,0:T(8,128)(2,1)S(1)}) custom-call(s32[4,8]{1,0:T(4,128)} %blocks_ref.1, bf16[2,8,128,128]{3,2,1,0:T(8,128)(2,1)} %rest_0_.1, bf16[4,2,128,128]{3,2,1,0:T(8,128)(2,1)} %rest_1_.1, bf16[4,2,128,128]{3,2,1,0:T(8,128)(2,1)} %right_ref.1), custom_call_target="tpu_custom_call" | custom-call | tf_op jit(solution)/shard_map/pack/pallas_call | solution.py:246
  1.2 0.5 %collective-permute-start.3 = (bf16[4,2,128,128]{3,2,1,0:T(8,128)(2,1)S(1)}, bf16[4,2,128,128]{3,2,1,0:T(8,128)(2,1)S(1)}, u32[]{:S(2)}, u32[]{:S(2)}) collective-permute-start(bf16[4,2,128,128]{3,2,1,0:T(8,128)(2,1)S(1)} %get-tuple-element.15.rest_5_.refs_4_), channel_id=1, source_target_pairs={{0,1},{1,0},{2,3},{3,2},{4,5},{5,4},{6,7},{7,6},{8,9},{9,8},{10,11... | collective-permute-start | bytes 786440 | tf_op jit(solution)/shard_map/ppermute | solution.py:232
  1.7 3.7 %collective-permute-start.1 = (bf16[528,128]{1,0:T(8,128)(2,1)S(1)}, bf16[528,128]{1,0:T(8,128)(2,1)S(1)}, u32[]{:S(2)}, u32[]{:S(2)}) collective-permute-start(bf16[528,128]{1,0:T(8,128)(2,1)S(1)} %get-tuple-element.14), channel_id=1, source_target_pairs={{0,8},{1,4},{2,10},{3,6},{4,1},{5,13},{6,3},{7,15},{8,0},{9,12},{1... | collective-permute-start | bytes 405512 | tf_op jit(solution)/shard_map/ppermute | solution.py:240
  5.4 0.0 collective-permute-start.2
  5.4 1.7 %collective-permute-start = (bf16[528,128]{1,0:T(8,128)(2,1)S(1)}, bf16[528,128]{1,0:T(8,128)(2,1)S(1)}, u32[]{:S(2)}, u32[]{:S(2)}) collective-permute-start(bf16[528,128]{1,0:T(8,128)(2,1)S(1)} %get-tuple-element.13), channel_id=1, source_target_pairs={{0,4},{1,0},{2,6},{3,2},{4,5},{5,1},{6,7},{7,3},{8,12},{9,8},{10,1... | collective-permute-start | bytes 405512 | tf_op jit(solution)/shard_map/ppermute | solution.py:240
  7.1 2.6 %collective-permute-start.6 = (bf16[544,128]{1,0:T(8,128)(2,1)S(1)}, bf16[544,128]{1,0:T(8,128)(2,1)S(1)}, u32[]{:S(2)}, u32[]{:S(2)}) collective-permute-start(bf16[544,128]{1,0:T(8,128)(2,1)S(1)} %get-tuple-element.18), channel_id=1, source_target_pairs={{0,8},{1,12},{2,10},{3,14},{4,9},{5,13},{6,11},{7,15},{8,0},{9,4},... | collective-permute-start | bytes 417800 | tf_op jit(solution)/shard_map/ppermute | solution.py:240
  9.7 0.3 %collective-permute-done.1.rest_3_.refs_0_ = bf16[528,128]{1,0:T(8,128)(2,1)S(1)} collective-permute-done((bf16[528,128]{1,0:T(8,128)(2,1)S(1)}, bf16[528,128]{1,0:T(8,128)(2,1)S(1)}, u32[]{:S(2)}, u32[]{:S(2)}) %collective-permute-start.1) | collective-permute-done | bytes 135200 | tf_op jit(solution)/shard_map/ppermute | solution.py:240
  10.0 0.0 collective-permute-start.4
  10.0 1.8 %collective-permute-done.2.rest_4_.refs_1_ = bf16[528,128]{1,0:T(8,128)(2,1)S(1)} collective-permute-done((bf16[528,128]{1,0:T(8,128)(2,1)S(1)}, bf16[528,128]{1,0:T(8,128)(2,1)S(1)}, u32[]{:S(2)}, u32[]{:S(2)}) %collective-permute-start.2) | collective-permute-done | bytes 135200 | tf_op jit(solution)/shard_map/ppermute | solution.py:240
  11.8 3.4 %collective-permute-start.5 = (bf16[528,128]{1,0:T(8,128)(2,1)S(1)}, bf16[528,128]{1,0:T(8,128)(2,1)S(1)}, u32[]{:S(2)}, u32[]{:S(2)}) collective-permute-start(bf16[528,128]{1,0:T(8,128)(2,1)S(1)} %collective-permute-done.2.rest_4_.refs_1_), channel_id=1, source_target_pairs={{0,4},{1,0},{2,6},{3,2},{4,5},{5,1},{6,7},{7,3},{8,12},{9,8},{10,1... | collective-permute-start | bytes 405512 | tf_op jit(solution)/shard_map/ppermute | solution.py:240
  15.2 0.0 collective-permute-done.rest_2_
  15.2 0.0 collective-permute-done.3.rest_6_.refs_5_
  15.2 0.0 copy-done
  15.2 0.0 copy-done.1
  15.2 0.0 copy-done.2
  15.2 0.0 copy-done.3
  15.2 1.3 %near.1 = (f32[2,2,128,128]{3,2,1,0:T(8,128)S(1)}, bf16[2,2,128,128]{3,2,1,0:T(8,128)(2,1)S(1)}) custom-call(s32[8]{0:T(128)S(1)} %copy-done.3, s32[8]{0:T(128)S(1)} %copy-done.4, s32[4,8]{1,0:T(4,128)S(1)} %copy-done.2, bf16[2,8,128,128]{3,2,1,0:T(8,128)(2,1)S(1)} %copy-done, bf16[4,2,128,128]{3,2,1,0:T(8,128)(2,1)S(1)} %copy-done.1, ...), custom_call_target="tpu_custom_call" | custom-call | flops 536870912 | bytes 1048576 | tf_op jit(solution)/shard_map/near/pallas_call | solution.py:273
  16.5 2.4 %collective-permute-done.6.refs_8_ = bf16[544,128]{1,0:T(8,128)(2,1)S(1)} collective-permute-done((bf16[544,128]{1,0:T(8,128)(2,1)S(1)}, bf16[544,128]{1,0:T(8,128)(2,1)S(1)}, u32[]{:S(2)}, u32[]{:S(2)}) %collective-permute-start.6) | collective-permute-done | bytes 139296 | tf_op jit(solution)/shard_map/ppermute | solution.py:240
  18.9 0.0 collective-permute-done.4.refs_2_
  18.9 0.0 collective-permute-done.5.refs_3_
  18.9 0.7 %far.1 = (bf16[2,2,128,128]{3,2,1,0:T(8,128)(2,1)S(1)}, f32[2,2,128,128]{3,2,1,0:T(8,128)S(1)}) custom-call(bf16[528,128]{1,0:T(8,128)(2,1)S(1)} %collective-permute-done.1.rest_3_.refs_0_, bf16[528,128]{1,0:T(8,128)(2,1)S(1)} %collective-permute-done.2.rest_4_.refs_1_, bf16[528,128]{1,0:T(8,128)(2,1)S(1)} %collective-permute-done.4.refs_2_, ...), custom_call_target="tpu_custom_call" | custom-call | flops 536870912 | bytes 1048576 | tf_op jit(solution)/shard_map/far/pallas_call | solution.py:273
  19.5 1.6 %collective-permute-start.7 = (bf16[2,2,128,128]{3,2,1,0:T(8,128)(2,1)S(1)}, bf16[2,2,128,128]{3,2,1,0:T(8,128)(2,1)S(1)}, u32[]{:S(2)}, u32[]{:S(2)}) collective-permute-start(bf16[2,2,128,128]{3,2,1,0:T(8,128)(2,1)S(1)} %get-tuple-element.20), channel_id=1, source_target_pairs={{0,2},{1,3},{2,0},{3,1},{4,6},{5,7},{6,4},{7,5},{8,10},{9,11},{10,... | collective-permute-start | bytes 393224 | tf_op jit(solution)/shard_map/ppermute | solution.py:232
  21.1 4.6 %collective-permute-done.7 = bf16[2,2,128,128]{3,2,1,0:T(8,128)(2,1)S(1)} collective-permute-done((bf16[2,2,128,128]{3,2,1,0:T(8,128)(2,1)S(1)}, bf16[2,2,128,128]{3,2,1,0:T(8,128)(2,1)S(1)}, u32[]{:S(2)}, u32[]{:S(2)}) %collective-permute-start.7) | collective-permute-done | bytes 131104 | tf_op jit(solution)/shard_map/ppermute | solution.py:232
  25.7 0.7 %add_convert_fusion = bf16[2,2,128,128]{3,2,1,0:T(8,128)(2,1)} fusion(bf16[2,2,128,128]{3,2,1,0:T(8,128)(2,1)S(1)} %collective-permute-done.7, f32[2,2,128,128]{3,2,1,0:T(8,128)S(1)} %get-tuple-element.16.refs_6_, f32[2,2,128,128]{3,2,1,0:T(8,128)S(1)} %get-tuple-element.19, pred[]{:T(512)S(6)} %eq.3), kind=kLoop, calls=%fused_computation | loop fusion | flops 262144 | bytes 786433 | tf_op jit(solution)/shard_map/convert_element_type | solution.py:298
  (6 shorter events, 0.0 us)
Async XLA Ops:
  0.0 15.2 %copy-start = (bf16[2,8,128,128]{3,2,1,0:T(8,128)(2,1)S(1)}, bf16[2,8,128,128]{3,2,1,0:T(8,128)(2,1)}, u32[]{:S(2)}) copy-start(bf16[2,8,128,128]{3,2,1,0:T(8,128)(2,1)} %rest_0_.1) | copy-start | bytes 1572868
  0.0 15.2 %copy-start.1 = (bf16[4,2,128,128]{3,2,1,0:T(8,128)(2,1)S(1)}, bf16[4,2,128,128]{3,2,1,0:T(8,128)(2,1)}, u32[]{:S(2)}) copy-start(bf16[4,2,128,128]{3,2,1,0:T(8,128)(2,1)} %rest_1_.1) | copy-start | bytes 786436
  1.2 14.0 %collective-permute-start.3 = (bf16[4,2,128,128]{3,2,1,0:T(8,128)(2,1)S(1)}, bf16[4,2,128,128]{3,2,1,0:T(8,128)(2,1)S(1)}, u32[]{:S(2)}, u32[]{:S(2)}) collective-permute-start(bf16[4,2,128,128]{3,2,1,0:T(8,128)(2,1)S(1)} %get-tuple-element.15.rest_5_.refs_4_), channel_id=1, source_target_pairs={{0,1},{1,0},{2,3},{3,2},{4,5},{5,4},{6,7},{7,6},{8,9},{9,8},{10,11... | collective-permute-start | bytes 786440 | tf_op jit(solution)/shard_map/ppermute | solution.py:232
  1.7 13.5 %copy-start.2 = (s32[4,8]{1,0:T(4,128)S(1)}, s32[4,8]{1,0:T(4,128)}, u32[]{:S(2)}) copy-start(s32[4,8]{1,0:T(4,128)} %blocks_ref.1) | copy-start | bytes 388
  1.7 8.2 %collective-permute-start.1 = (bf16[528,128]{1,0:T(8,128)(2,1)S(1)}, bf16[528,128]{1,0:T(8,128)(2,1)S(1)}, u32[]{:S(2)}, u32[]{:S(2)}) collective-permute-start(bf16[528,128]{1,0:T(8,128)(2,1)S(1)} %get-tuple-element.14), channel_id=1, source_target_pairs={{0,8},{1,4},{2,10},{3,6},{4,1},{5,13},{6,3},{7,15},{8,0},{9,12},{1... | collective-permute-start | bytes 405512 | tf_op jit(solution)/shard_map/ppermute | solution.py:240
  5.4 6.4 %collective-permute-start.2 = (bf16[528,128]{1,0:T(8,128)(2,1)S(1)}, bf16[528,128]{1,0:T(8,128)(2,1)S(1)}, u32[]{:S(2)}, u32[]{:S(2)}) collective-permute-start(bf16[528,128]{1,0:T(8,128)(2,1)S(1)} %get-tuple-element.14), channel_id=1, source_target_pairs={{0,4},{1,8},{2,6},{3,10},{4,13},{5,1},{6,15},{7,3},{8,12},{9,0},{1... | collective-permute-start | bytes 405512 | tf_op jit(solution)/shard_map/ppermute | solution.py:240
  5.4 9.8 %copy-start.3 = (s32[8]{0:T(128)S(1)}, s32[8]{0:T(128)}, u32[]{:S(2)}) copy-start(s32[8]{0:T(128)} %lsize_ref.1) | copy-start | bytes 100
  5.4 9.8 %copy-start.4 = (s32[8]{0:T(128)S(1)}, s32[8]{0:T(128)}, u32[]{:S(2)}) copy-start(s32[8]{0:T(128)} %rsize_ref.1) | copy-start | bytes 100
  5.4 9.8 %collective-permute-start = (bf16[528,128]{1,0:T(8,128)(2,1)S(1)}, bf16[528,128]{1,0:T(8,128)(2,1)S(1)}, u32[]{:S(2)}, u32[]{:S(2)}) collective-permute-start(bf16[528,128]{1,0:T(8,128)(2,1)S(1)} %get-tuple-element.13), channel_id=1, source_target_pairs={{0,4},{1,0},{2,6},{3,2},{4,5},{5,1},{6,7},{7,3},{8,12},{9,8},{10,1... | collective-permute-start | bytes 405512 | tf_op jit(solution)/shard_map/ppermute | solution.py:240
  7.1 11.8 %collective-permute-start.6 = (bf16[544,128]{1,0:T(8,128)(2,1)S(1)}, bf16[544,128]{1,0:T(8,128)(2,1)S(1)}, u32[]{:S(2)}, u32[]{:S(2)}) collective-permute-start(bf16[544,128]{1,0:T(8,128)(2,1)S(1)} %get-tuple-element.18), channel_id=1, source_target_pairs={{0,8},{1,12},{2,10},{3,14},{4,9},{5,13},{6,11},{7,15},{8,0},{9,4},... | collective-permute-start | bytes 417800 | tf_op jit(solution)/shard_map/ppermute | solution.py:240
  10.0 8.9 %collective-permute-start.4 = (bf16[528,128]{1,0:T(8,128)(2,1)S(1)}, bf16[528,128]{1,0:T(8,128)(2,1)S(1)}, u32[]{:S(2)}, u32[]{:S(2)}) collective-permute-start(bf16[528,128]{1,0:T(8,128)(2,1)S(1)} %collective-permute-done.1.rest_3_.refs_0_), channel_id=1, source_target_pairs={{0,4},{1,0},{2,6},{3,2},{4,5},{5,1},{6,7},{7,3},{8,12},{9,8},{10,1... | collective-permute-start | bytes 405512 | tf_op jit(solution)/shard_map/ppermute | solution.py:240
  11.8 7.1 %collective-permute-start.5 = (bf16[528,128]{1,0:T(8,128)(2,1)S(1)}, bf16[528,128]{1,0:T(8,128)(2,1)S(1)}, u32[]{:S(2)}, u32[]{:S(2)}) collective-permute-start(bf16[528,128]{1,0:T(8,128)(2,1)S(1)} %collective-permute-done.2.rest_4_.refs_1_), channel_id=1, source_target_pairs={{0,4},{1,0},{2,6},{3,2},{4,5},{5,1},{6,7},{7,3},{8,12},{9,8},{10,1... | collective-permute-start | bytes 405512 | tf_op jit(solution)/shard_map/ppermute | solution.py:240
  19.5 6.1 %collective-permute-start.7 = (bf16[2,2,128,128]{3,2,1,0:T(8,128)(2,1)S(1)}, bf16[2,2,128,128]{3,2,1,0:T(8,128)(2,1)S(1)}, u32[]{:S(2)}, u32[]{:S(2)}) collective-permute-start(bf16[2,2,128,128]{3,2,1,0:T(8,128)(2,1)S(1)} %get-tuple-element.20), channel_id=1, source_target_pairs={{0,2},{1,3},{2,0},{3,1},{4,6},{5,7},{6,4},{7,5},{8,10},{9,11},{10,... | collective-permute-start | bytes 393224 | tf_op jit(solution)/shard_map/ppermute | solution.py:232

commit v11 on v10

--- a/solution.py
+++ b/solution.py
@@ -269,7 +269,7 @@
     passed_b = over_z(direct_b, 1, 0)
     right_other = over_op(right_own, 1)
 
-    def apply(kernel, name, outs, scalars, operands):
+    def apply(kernel, name, outs, scalars, operands, cost):
         return pl.pallas_call(
             kernel,
             out_shape=outs,
@@ -277,7 +277,7 @@
             out_specs=[VMEM] * len(outs),
             compiler_params=PARAMS,
             cost_estimate=pl.CostEstimate(
-                flops=64 * tile**3 * sectors**2, bytes_accessed=2**20, transcendentals=0
+                flops=64 * cost**3, bytes_accessed=16 * cost**2, transcendentals=0
             ),
             name=name,
         )(*scalars, *operands)
@@ -287,11 +287,11 @@
     total = jax.ShapeDtypeStruct(out_shape, jnp.float32)
     near, far_mask = apply(
         near_kernel, "near", [total, block(out_shape)], sizes + (term_blocks,),
-        [psi, left_ops, side, direct_a, direct_b] + rights,
+        [psi, left_ops, side, direct_a, direct_b] + rights, 1,
     )
     sent, far = apply(
         far_kernel, "far", [block(out_shape), total], (),
-        [direct_a, direct_b, passed_a, passed_b] + rights + [near, far_mask, psi_far],
+        [direct_a, direct_b, passed_a, passed_b] + rights + [near, far_mask, psi_far], 2 * tile,
     )
     arrived = over_op(sent, 2)
     kept = jnp.where(lax.axis_index("blk") // 2 == lax.axis_index("op") // 2, near, far)

time: 26.5 us -> 26.3 us (level)
  starting transfers between devices: 13.4 us -> 8.94 us
  waiting for transfers between devices: 9.07 us -> 13.3 us
    ppermute x6, waiting for transfers between devices: 4.5 us -> 9.36 us  [over_z(): return lax.ppermute(array, ('blk', 'op'), pairs)]
    ppermute x6, starting transfers between devices: 11.3 us -> 7.2 us  [over_z(): return lax.ppermute(array, ('blk', 'op'), pairs)]
    ppermute x2, waiting for transfers between devices: 4.58 us -> 3.96 us  [over_op(): return lax.ppermute(array, 'op', [(o, o ^ step) for o in range(n)])]
    ppermute x2, starting transfers between devices: 2.08 us -> 1.74 us  [over_op(): return lax.ppermute(array, 'op', [(o, o ^ step) for o in range(n)])]
where the time goes in v11:
time: 26.3 us; the launch traced here: 26.2 us
  waiting for transfers between devices  13.3 us (51%)
  starting transfers between devices  8.94 us (34%)
  Pallas kernels  3.12 us (12%)
  other arithmetic  0.69 us (3%)
    ppermute x6, waiting for transfers between devices, over_z(): return lax.ppermute(array, ('blk', 'op'), pairs)  9.36 us
    ppermute x6, starting transfers between devices, over_z(): return lax.ppermute(array, ('blk', 'op'), pairs)  7.2 us
    ppermute x2, waiting for transfers between devices, over_op(): return lax.ppermute(array, 'op', [(o, o ^ step) for o in range(n)])  3.96 us
    pallas_call x2, Pallas kernels, apply(): pl.pallas_call(kernel, out_shape=outs, in_specs=[SMEM] * len(scalars) + [...  1.91 us
    ppermute x2, starting transfers between devices, over_op(): return lax.ppermute(array, 'op', [(o, o ^ step) for o in range(n)])  1.74 us
    pallas_call x1, Pallas kernels, shards(): pl.pallas_call(pack_kernel, out_shape=[block(message_shape), block(messag...  1.21 us
    convert_element_type x1, other arithmetic, shards(): return (kept + arrived.astype(jnp.float32)).astype(jnp.bfloat16)  0.69 us
  transfers between devices with their start and end apart: 8, of which 4 were waited for; matrix products, arithmetic and copies ran while one was open for 0% of the time, Pallas kernels for 5%

profile of v11, /device:TPU:0, one launch (start us, length us, event | category | flops | bytes accessed | tf_op | source)
XLA Modules:
  0.0 26.2 jit_solution(17762273596627543960)
XLA Ops:
  0.0 1.2 %pack.1 = (bf16[528,128]{1,0:T(8,128)(2,1)S(1)}, bf16[528,128]{1,0:T(8,128)(2,1)S(1)}, bf16[544,128]{1,0:T(8,128)(2,1)S(1)}, bf16[4,2,128,128]{3,2,1,0:T(8,128)(2,1)S(1)}) custom-call(s32[4,8]{1,0:T(4,128)} %blocks_ref.1, bf16[2,8,128,128]{3,2,1,0:T(8,128)(2,1)} %rest_0_.1, bf16[4,2,128,128]{3,2,1,0:T(8,128)(2,1)} %rest_1_.1, bf16[4,2,128,128]{3,2,1,0:T(8,128)(2,1)} %right_ref.1), custom_call_target="tpu_custom_call" | custom-call | tf_op jit(solution)/shard_map/pack/pallas_call | solution.py:246
  1.2 4.1 %collective-permute-start.1 = (bf16[528,128]{1,0:T(8,128)(2,1)S(1)}, bf16[528,128]{1,0:T(8,128)(2,1)S(1)}, u32[]{:S(2)}, u32[]{:S(2)}) collective-permute-start(bf16[528,128]{1,0:T(8,128)(2,1)S(1)} %get-tuple-element.14), channel_id=1, source_target_pairs={{0,8},{1,4},{2,10},{3,6},{4,1},{5,13},{6,3},{7,15},{8,0},{9,12},{1... | collective-permute-start | bytes 405512 | tf_op jit(solution)/shard_map/ppermute | solution.py:240
  5.3 0.0 collective-permute-start.2
  5.3 0.2 collective-permute-start.3
  5.5 2.8 %collective-permute-start.6 = (bf16[544,128]{1,0:T(8,128)(2,1)S(1)}, bf16[544,128]{1,0:T(8,128)(2,1)S(1)}, u32[]{:S(2)}, u32[]{:S(2)}) collective-permute-start(bf16[544,128]{1,0:T(8,128)(2,1)S(1)} %get-tuple-element.18), channel_id=1, source_target_pairs={{0,8},{1,12},{2,10},{3,14},{4,9},{5,13},{6,11},{7,15},{8,0},{9,4},... | collective-permute-start | bytes 417800 | tf_op jit(solution)/shard_map/ppermute | solution.py:240
  8.4 0.2 collective-permute-start
  8.6 1.7 %collective-permute-done.1.rest_3_.refs_0_ = bf16[528,128]{1,0:T(8,128)(2,1)S(1)} collective-permute-done((bf16[528,128]{1,0:T(8,128)(2,1)S(1)}, bf16[528,128]{1,0:T(8,128)(2,1)S(1)}, u32[]{:S(2)}, u32[]{:S(2)}) %collective-permute-start.1) | collective-permute-done | bytes 135200 | tf_op jit(solution)/shard_map/ppermute | solution.py:240
  10.3 0.0 collective-permute-start.4
  10.3 6.4 %collective-permute-done.2.rest_4_.refs_1_ = bf16[528,128]{1,0:T(8,128)(2,1)S(1)} collective-permute-done((bf16[528,128]{1,0:T(8,128)(2,1)S(1)}, bf16[528,128]{1,0:T(8,128)(2,1)S(1)}, u32[]{:S(2)}, u32[]{:S(2)}) %collective-permute-start.2) | collective-permute-done | bytes 135200 | tf_op jit(solution)/shard_map/ppermute | solution.py:240
  16.7 0.0 collective-permute-start.5
  16.8 0.0 collective-permute-done.rest_2_
  16.8 0.0 collective-permute-done.3.rest_6_.refs_5_
  16.8 0.0 copy-done
  16.8 0.0 copy-done.1
  16.8 0.0 copy-done.2
  16.8 0.0 copy-done.3
  16.8 1.3 %near.1 = (f32[2,2,128,128]{3,2,1,0:T(8,128)S(1)}, bf16[2,2,128,128]{3,2,1,0:T(8,128)(2,1)S(1)}) custom-call(s32[8]{0:T(128)S(1)} %copy-done.3, s32[8]{0:T(128)S(1)} %copy-done.4, s32[4,8]{1,0:T(4,128)S(1)} %copy-done.2, bf16[2,8,128,128]{3,2,1,0:T(8,128)(2,1)S(1)} %copy-done, bf16[4,2,128,128]{3,2,1,0:T(8,128)(2,1)S(1)} %copy-done.1, ...), custom_call_target="tpu_custom_call" | custom-call | flops 64 | bytes 16 | tf_op jit(solution)/shard_map/near/pallas_call | solution.py:273
  18.1 0.0 collective-permute-done.6.refs_8_
  18.1 0.0 collective-permute-done.4.refs_2_
  18.1 1.2 %collective-permute-done.5.refs_3_ = bf16[528,128]{1,0:T(8,128)(2,1)S(1)} collective-permute-done((bf16[528,128]{1,0:T(8,128)(2,1)S(1)}, bf16[528,128]{1,0:T(8,128)(2,1)S(1)}, u32[]{:S(2)}, u32[]{:S(2)}) %collective-permute-start.5) | collective-permute-done | bytes 135200 | tf_op jit(solution)/shard_map/ppermute | solution.py:240
  19.3 0.7 %far.1 = (bf16[2,2,128,128]{3,2,1,0:T(8,128)(2,1)S(1)}, f32[2,2,128,128]{3,2,1,0:T(8,128)S(1)}) custom-call(bf16[528,128]{1,0:T(8,128)(2,1)S(1)} %collective-permute-done.1.rest_3_.refs_0_, bf16[528,128]{1,0:T(8,128)(2,1)S(1)} %collective-permute-done.2.rest_4_.refs_1_, bf16[528,128]{1,0:T(8,128)(2,1)S(1)} %collective-permute-done.4.refs_2_, ...), custom_call_target="tpu_custom_call" | custom-call | flops 1073741824 | bytes 1048576 | tf_op jit(solution)/shard_map/far/pallas_call | solution.py:273
  20.0 1.6 %collective-permute-start.7 = (bf16[2,2,128,128]{3,2,1,0:T(8,128)(2,1)S(1)}, bf16[2,2,128,128]{3,2,1,0:T(8,128)(2,1)S(1)}, u32[]{:S(2)}, u32[]{:S(2)}) collective-permute-start(bf16[2,2,128,128]{3,2,1,0:T(8,128)(2,1)S(1)} %get-tuple-element.20), channel_id=1, source_target_pairs={{0,2},{1,3},{2,0},{3,1},{4,6},{5,7},{6,4},{7,5},{8,10},{9,11},{10,... | collective-permute-start | bytes 393224 | tf_op jit(solution)/shard_map/ppermute | solution.py:232
  21.5 4.0 %collective-permute-done.7 = bf16[2,2,128,128]{3,2,1,0:T(8,128)(2,1)S(1)} collective-permute-done((bf16[2,2,128,128]{3,2,1,0:T(8,128)(2,1)S(1)}, bf16[2,2,128,128]{3,2,1,0:T(8,128)(2,1)S(1)}, u32[]{:S(2)}, u32[]{:S(2)}) %collective-permute-start.7) | collective-permute-done | bytes 131104 | tf_op jit(solution)/shard_map/ppermute | solution.py:232
  25.5 0.7 %add_convert_fusion = bf16[2,2,128,128]{3,2,1,0:T(8,128)(2,1)} fusion(bf16[2,2,128,128]{3,2,1,0:T(8,128)(2,1)S(1)} %collective-permute-done.7, f32[2,2,128,128]{3,2,1,0:T(8,128)S(1)} %get-tuple-element.16.refs_6_, f32[2,2,128,128]{3,2,1,0:T(8,128)S(1)} %get-tuple-element.19, pred[]{:T(512)S(6)} %eq.3), kind=kLoop, calls=%fused_computation | loop fusion | flops 262144 | bytes 786433 | tf_op jit(solution)/shard_map/convert_element_type | solution.py:298
  (6 shorter events, 0.0 us)
Async XLA Ops:
  0.0 16.8 %copy-start = (bf16[2,8,128,128]{3,2,1,0:T(8,128)(2,1)S(1)}, bf16[2,8,128,128]{3,2,1,0:T(8,128)(2,1)}, u32[]{:S(2)}) copy-start(bf16[2,8,128,128]{3,2,1,0:T(8,128)(2,1)} %rest_0_.1) | copy-start | bytes 1572868
  0.0 16.8 %copy-start.1 = (bf16[4,2,128,128]{3,2,1,0:T(8,128)(2,1)S(1)}, bf16[4,2,128,128]{3,2,1,0:T(8,128)(2,1)}, u32[]{:S(2)}) copy-start(bf16[4,2,128,128]{3,2,1,0:T(8,128)(2,1)} %rest_1_.1) | copy-start | bytes 786436
  1.2 9.1 %collective-permute-start.1 = (bf16[528,128]{1,0:T(8,128)(2,1)S(1)}, bf16[528,128]{1,0:T(8,128)(2,1)S(1)}, u32[]{:S(2)}, u32[]{:S(2)}) collective-permute-start(bf16[528,128]{1,0:T(8,128)(2,1)S(1)} %get-tuple-element.14), channel_id=1, source_target_pairs={{0,8},{1,4},{2,10},{3,6},{4,1},{5,13},{6,3},{7,15},{8,0},{9,12},{1... | collective-permute-start | bytes 405512 | tf_op jit(solution)/shard_map/ppermute | solution.py:240
  5.3 11.4 %collective-permute-start.2 = (bf16[528,128]{1,0:T(8,128)(2,1)S(1)}, bf16[528,128]{1,0:T(8,128)(2,1)S(1)}, u32[]{:S(2)}, u32[]{:S(2)}) collective-permute-start(bf16[528,128]{1,0:T(8,128)(2,1)S(1)} %get-tuple-element.14), channel_id=1, source_target_pairs={{0,4},{1,8},{2,6},{3,10},{4,13},{5,1},{6,15},{7,3},{8,12},{9,0},{1... | collective-permute-start | bytes 405512 | tf_op jit(solution)/shard_map/ppermute | solution.py:240
  5.3 11.5 %copy-start.2 = (s32[4,8]{1,0:T(4,128)S(1)}, s32[4,8]{1,0:T(4,128)}, u32[]{:S(2)}) copy-start(s32[4,8]{1,0:T(4,128)} %blocks_ref.1) | copy-start | bytes 388
  5.3 11.4 %collective-permute-start.3 = (bf16[4,2,128,128]{3,2,1,0:T(8,128)(2,1)S(1)}, bf16[4,2,128,128]{3,2,1,0:T(8,128)(2,1)S(1)}, u32[]{:S(2)}, u32[]{:S(2)}) collective-permute-start(bf16[4,2,128,128]{3,2,1,0:T(8,128)(2,1)S(1)} %get-tuple-element.15.rest_5_.refs_4_), channel_id=1, source_target_pairs={{0,1},{1,0},{2,3},{3,2},{4,5},{5,4},{6,7},{7,6},{8,9},{9,8},{10,11... | collective-permute-start | bytes 786440 | tf_op jit(solution)/shard_map/ppermute | solution.py:232
  5.5 11.3 %copy-start.3 = (s32[8]{0:T(128)S(1)}, s32[8]{0:T(128)}, u32[]{:S(2)}) copy-start(s32[8]{0:T(128)} %lsize_ref.1) | copy-start | bytes 100
  5.5 11.3 %copy-start.4 = (s32[8]{0:T(128)S(1)}, s32[8]{0:T(128)}, u32[]{:S(2)}) copy-start(s32[8]{0:T(128)} %rsize_ref.1) | copy-start | bytes 100
  5.5 12.6 %collective-permute-start.6 = (bf16[544,128]{1,0:T(8,128)(2,1)S(1)}, bf16[544,128]{1,0:T(8,128)(2,1)S(1)}, u32[]{:S(2)}, u32[]{:S(2)}) collective-permute-start(bf16[544,128]{1,0:T(8,128)(2,1)S(1)} %get-tuple-element.18), channel_id=1, source_target_pairs={{0,8},{1,12},{2,10},{3,14},{4,9},{5,13},{6,11},{7,15},{8,0},{9,4},... | collective-permute-start | bytes 417800 | tf_op jit(solution)/shard_map/ppermute | solution.py:240
  8.4 8.4 %collective-permute-start = (bf16[528,128]{1,0:T(8,128)(2,1)S(1)}, bf16[528,128]{1,0:T(8,128)(2,1)S(1)}, u32[]{:S(2)}, u32[]{:S(2)}) collective-permute-start(bf16[528,128]{1,0:T(8,128)(2,1)S(1)} %get-tuple-element.13), channel_id=1, source_target_pairs={{0,4},{1,0},{2,6},{3,2},{4,5},{5,1},{6,7},{7,3},{8,12},{9,8},{10,1... | collective-permute-start | bytes 405512 | tf_op jit(solution)/shard_map/ppermute | solution.py:240
  10.3 7.7 %collective-permute-start.4 = (bf16[528,128]{1,0:T(8,128)(2,1)S(1)}, bf16[528,128]{1,0:T(8,128)(2,1)S(1)}, u32[]{:S(2)}, u32[]{:S(2)}) collective-permute-start(bf16[528,128]{1,0:T(8,128)(2,1)S(1)} %collective-permute-done.1.rest_3_.refs_0_), channel_id=1, source_target_pairs={{0,4},{1,0},{2,6},{3,2},{4,5},{5,1},{6,7},{7,3},{8,12},{9,8},{10,1... | collective-permute-start | bytes 405512 | tf_op jit(solution)/shard_map/ppermute | solution.py:240
  16.7 2.6 %collective-permute-start.5 = (bf16[528,128]{1,0:T(8,128)(2,1)S(1)}, bf16[528,128]{1,0:T(8,128)(2,1)S(1)}, u32[]{:S(2)}, u32[]{:S(2)}) collective-permute-start(bf16[528,128]{1,0:T(8,128)(2,1)S(1)} %collective-permute-done.2.rest_4_.refs_1_), channel_id=1, source_target_pairs={{0,4},{1,0},{2,6},{3,2},{4,5},{5,1},{6,7},{7,3},{8,12},{9,8},{10,1... | collective-permute-start | bytes 405512 | tf_op jit(solution)/shard_map/ppermute | solution.py:240
  20.0 5.5 %collective-permute-start.7 = (bf16[2,2,128,128]{3,2,1,0:T(8,128)(2,1)S(1)}, bf16[2,2,128,128]{3,2,1,0:T(8,128)(2,1)S(1)}, u32[]{:S(2)}, u32[]{:S(2)}) collective-permute-start(bf16[2,2,128,128]{3,2,1,0:T(8,128)(2,1)S(1)} %get-tuple-element.20), channel_id=1, source_target_pairs={{0,2},{1,3},{2,0},{3,1},{4,6},{5,7},{6,4},{7,5},{8,10},{9,11},{10,... | collective-permute-start | bytes 393224 | tf_op jit(solution)/shard_map/ppermute | solution.py:232

commit v12 on v11

--- a/solution.py
+++ b/solution.py
@@ -295,6 +295,7 @@
     )
     arrived = over_op(sent, 2)
     kept = jnp.where(lax.axis_index("blk") // 2 == lax.axis_index("op") // 2, near, far)
+    kept = lax.optimization_barrier(kept)
     return (kept + arrived.astype(jnp.float32)).astype(jnp.bfloat16)
 
 

time: 26.3 us -> 26.4 us (level)
  local copies, waits for them, and re-layouts: 0.02 us -> 0.64 us
  waiting for transfers between devices: 13.3 us -> 12.8 us
    unnamed x10, local copies, waits for them, and re-layouts: 0.02 us -> 0.64 us
    ppermute x6, waiting for transfers between devices: 9.36 us -> 8.8 us  [over_z(): return lax.ppermute(array, ('blk', 'op'), pairs)]
where the time goes in v12:
time: 26.4 us; the launch traced here: 26.2 us
  waiting for transfers between devices  12.8 us (48%)
  starting transfers between devices  8.86 us (34%)
  Pallas kernels  3.11 us (12%)
  other arithmetic  0.72 us (3%)
  local copies, waits for them, and re-layouts  0.64 us (2%)
    ppermute x6, waiting for transfers between devices, over_z(): return lax.ppermute(array, ('blk', 'op'), pairs)  8.8 us
    ppermute x6, starting transfers between devices, over_z(): return lax.ppermute(array, ('blk', 'op'), pairs)  7.13 us
    ppermute x2, waiting for transfers between devices, over_op(): return lax.ppermute(array, 'op', [(o, o ^ step) for o in range(n)])  3.97 us
    pallas_call x2, Pallas kernels, apply(): pl.pallas_call(kernel, out_shape=outs, in_specs=[SMEM] * len(scalars) + [...  1.9 us
    ppermute x2, starting transfers between devices, over_op(): return lax.ppermute(array, 'op', [(o, o ^ step) for o in range(n)])  1.73 us
    pallas_call x1, Pallas kernels, shards(): pl.pallas_call(pack_kernel, out_shape=[block(message_shape), block(messag...  1.21 us
    convert_element_type x1, other arithmetic, shards(): return (kept + arrived.astype(jnp.float32)).astype(jnp.bfloat16)  0.69 us
    unnamed x10, local copies, waits for them, and re-layouts  0.64 us
  transfers between devices with their start and end apart: 8, of which 4 were waited for; matrix products, arithmetic and copies ran while one was open for 0% of the time, Pallas kernels for 5%

profile of v12, /device:TPU:0, one launch (start us, length us, event | category | flops | bytes accessed | tf_op | source)
XLA Modules:
  0.0 26.2 jit_solution(11970206714776638519)
XLA Ops:
  0.0 1.2 %pack.1 = (bf16[528,128]{1,0:T(8,128)(2,1)S(1)}, bf16[528,128]{1,0:T(8,128)(2,1)S(1)}, bf16[544,128]{1,0:T(8,128)(2,1)S(1)}, bf16[4,2,128,128]{3,2,1,0:T(8,128)(2,1)S(1)}) custom-call(s32[4,8]{1,0:T(4,128)} %blocks_ref.1, bf16[2,8,128,128]{3,2,1,0:T(8,128)(2,1)} %rest_0_.1, bf16[4,2,128,128]{3,2,1,0:T(8,128)(2,1)} %rest_1_.1, bf16[4,2,128,128]{3,2,1,0:T(8,128)(2,1)} %right_ref.1), custom_call_target="tpu_custom_call" | custom-call | tf_op jit(solution)/shard_map/pack/pallas_call | solution.py:246
  1.2 4.1 %collective-permute-start.1 = (bf16[528,128]{1,0:T(8,128)(2,1)S(1)}, bf16[528,128]{1,0:T(8,128)(2,1)S(1)}, u32[]{:S(2)}, u32[]{:S(2)}) collective-permute-start(bf16[528,128]{1,0:T(8,128)(2,1)S(1)} %get-tuple-element.14), channel_id=1, source_target_pairs={{0,8},{1,4},{2,10},{3,6},{4,1},{5,13},{6,3},{7,15},{8,0},{9,12},{1... | collective-permute-start | bytes 405512 | tf_op jit(solution)/shard_map/ppermute | solution.py:240
  5.3 0.0 collective-permute-start.2
  5.3 0.2 collective-permute-start.3
  5.5 2.8 %collective-permute-start.6 = (bf16[544,128]{1,0:T(8,128)(2,1)S(1)}, bf16[544,128]{1,0:T(8,128)(2,1)S(1)}, u32[]{:S(2)}, u32[]{:S(2)}) collective-permute-start(bf16[544,128]{1,0:T(8,128)(2,1)S(1)} %get-tuple-element.18), channel_id=1, source_target_pairs={{0,8},{1,12},{2,10},{3,14},{4,9},{5,13},{6,11},{7,15},{8,0},{9,4},... | collective-permute-start | bytes 417800 | tf_op jit(solution)/shard_map/ppermute | solution.py:240
  8.4 0.2 collective-permute-start
  8.5 1.8 %collective-permute-done.1.rest_3_.refs_0_ = bf16[528,128]{1,0:T(8,128)(2,1)S(1)} collective-permute-done((bf16[528,128]{1,0:T(8,128)(2,1)S(1)}, bf16[528,128]{1,0:T(8,128)(2,1)S(1)}, u32[]{:S(2)}, u32[]{:S(2)}) %collective-permute-start.1) | collective-permute-done | bytes 135200 | tf_op jit(solution)/shard_map/ppermute | solution.py:240
  10.3 0.0 collective-permute-start.4
  10.3 6.4 %collective-permute-done.2.rest_4_.refs_1_ = bf16[528,128]{1,0:T(8,128)(2,1)S(1)} collective-permute-done((bf16[528,128]{1,0:T(8,128)(2,1)S(1)}, bf16[528,128]{1,0:T(8,128)(2,1)S(1)}, u32[]{:S(2)}, u32[]{:S(2)}) %collective-permute-start.2) | collective-permute-done | bytes 135200 | tf_op jit(solution)/shard_map/ppermute | solution.py:240
  16.7 0.0 collective-permute-start.5
  16.8 0.0 collective-permute-done.rest_2_
  16.8 0.0 collective-permute-done.3.rest_6_.refs_5_
  16.8 0.0 copy-done
  16.8 0.0 copy-done.1
  16.8 0.6 %copy-done.2 = s32[4,8]{1,0:T(4,128)S(1)} copy-done((s32[4,8]{1,0:T(4,128)S(1)}, s32[4,8]{1,0:T(4,128)}, u32[]{:S(2)}) %copy-start.2) | copy-done | bytes 152
  17.4 0.0 copy-done.3
  17.4 1.3 %near.1 = (f32[2,2,128,128]{3,2,1,0:T(8,128)S(1)}, bf16[2,2,128,128]{3,2,1,0:T(8,128)(2,1)S(1)}) custom-call(s32[8]{0:T(128)S(1)} %copy-done.3, s32[8]{0:T(128)S(1)} %copy-done.4, s32[4,8]{1,0:T(4,128)S(1)} %copy-done.2, bf16[2,8,128,128]{3,2,1,0:T(8,128)(2,1)S(1)} %copy-done, bf16[4,2,128,128]{3,2,1,0:T(8,128)(2,1)S(1)} %copy-done.1, ...), custom_call_target="tpu_custom_call" | custom-call | flops 64 | bytes 16 | tf_op jit(solution)/shard_map/near/pallas_call | solution.py:273
  18.7 0.0 collective-permute-done.6.refs_8_
  18.7 0.0 collective-permute-done.4.refs_2_
  18.7 0.6 %collective-permute-done.5.refs_3_ = bf16[528,128]{1,0:T(8,128)(2,1)S(1)} collective-permute-done((bf16[528,128]{1,0:T(8,128)(2,1)S(1)}, bf16[528,128]{1,0:T(8,128)(2,1)S(1)}, u32[]{:S(2)}, u32[]{:S(2)}) %collective-permute-start.5) | collective-permute-done | bytes 135200 | tf_op jit(solution)/shard_map/ppermute | solution.py:240
  19.3 0.7 %far.1 = (bf16[2,2,128,128]{3,2,1,0:T(8,128)(2,1)S(1)}, f32[2,2,128,128]{3,2,1,0:T(8,128)S(1)}) custom-call(bf16[528,128]{1,0:T(8,128)(2,1)S(1)} %collective-permute-done.1.rest_3_.refs_0_, bf16[528,128]{1,0:T(8,128)(2,1)S(1)} %collective-permute-done.2.rest_4_.refs_1_, bf16[528,128]{1,0:T(8,128)(2,1)S(1)} %collective-permute-done.4.refs_2_, ...), custom_call_target="tpu_custom_call" | custom-call | flops 1073741824 | bytes 1048576 | tf_op jit(solution)/shard_map/far/pallas_call | solution.py:273
  20.0 1.5 %collective-permute-start.7 = (bf16[2,2,128,128]{3,2,1,0:T(8,128)(2,1)S(1)}, bf16[2,2,128,128]{3,2,1,0:T(8,128)(2,1)S(1)}, u32[]{:S(2)}, u32[]{:S(2)}) collective-permute-start(bf16[2,2,128,128]{3,2,1,0:T(8,128)(2,1)S(1)} %get-tuple-element.20), channel_id=1, source_target_pairs={{0,2},{1,3},{2,0},{3,1},{4,6},{5,7},{6,4},{7,5},{8,10},{9,11},{10,... | collective-permute-start | bytes 393224 | tf_op jit(solution)/shard_map/ppermute | solution.py:232
  21.5 4.0 %collective-permute-done.7 = bf16[2,2,128,128]{3,2,1,0:T(8,128)(2,1)S(1)} collective-permute-done((bf16[2,2,128,128]{3,2,1,0:T(8,128)(2,1)S(1)}, bf16[2,2,128,128]{3,2,1,0:T(8,128)(2,1)S(1)}, u32[]{:S(2)}, u32[]{:S(2)}) %collective-permute-start.7) | collective-permute-done | bytes 131104 | tf_op jit(solution)/shard_map/ppermute | solution.py:232
  25.5 0.7 %add_convert_fusion = bf16[2,2,128,128]{3,2,1,0:T(8,128)(2,1)} fusion(f32[2,2,128,128]{3,2,1,0:T(8,128)S(1)} %broadcast_select_fusion, bf16[2,2,128,128]{3,2,1,0:T(8,128)(2,1)S(1)} %collective-permute-done.7), kind=kLoop, calls=%fused_computation | loop fusion | flops 196608 | bytes 524288 | tf_op jit(solution)/shard_map/convert_element_type | solution.py:299
  (7 shorter events, 0.0 us)
Async XLA Ops:
  0.0 16.8 %copy-start = (bf16[2,8,128,128]{3,2,1,0:T(8,128)(2,1)S(1)}, bf16[2,8,128,128]{3,2,1,0:T(8,128)(2,1)}, u32[]{:S(2)}) copy-start(bf16[2,8,128,128]{3,2,1,0:T(8,128)(2,1)} %rest_0_.1) | copy-start | bytes 1572868
  0.0 16.8 %copy-start.1 = (bf16[4,2,128,128]{3,2,1,0:T(8,128)(2,1)S(1)}, bf16[4,2,128,128]{3,2,1,0:T(8,128)(2,1)}, u32[]{:S(2)}) copy-start(bf16[4,2,128,128]{3,2,1,0:T(8,128)(2,1)} %rest_1_.1) | copy-start | bytes 786436
  1.2 9.1 %collective-permute-start.1 = (bf16[528,128]{1,0:T(8,128)(2,1)S(1)}, bf16[528,128]{1,0:T(8,128)(2,1)S(1)}, u32[]{:S(2)}, u32[]{:S(2)}) collective-permute-start(bf16[528,128]{1,0:T(8,128)(2,1)S(1)} %get-tuple-element.14), channel_id=1, source_target_pairs={{0,8},{1,4},{2,10},{3,6},{4,1},{5,13},{6,3},{7,15},{8,0},{9,12},{1... | collective-permute-start | bytes 405512 | tf_op jit(solution)/shard_map/ppermute | solution.py:240
  5.3 11.4 %collective-permute-start.2 = (bf16[528,128]{1,0:T(8,128)(2,1)S(1)}, bf16[528,128]{1,0:T(8,128)(2,1)S(1)}, u32[]{:S(2)}, u32[]{:S(2)}) collective-permute-start(bf16[528,128]{1,0:T(8,128)(2,1)S(1)} %get-tuple-element.14), channel_id=1, source_target_pairs={{0,4},{1,8},{2,6},{3,10},{4,13},{5,1},{6,15},{7,3},{8,12},{9,0},{1... | collective-permute-start | bytes 405512 | tf_op jit(solution)/shard_map/ppermute | solution.py:240
  5.3 11.5 %collective-permute-start.3 = (bf16[4,2,128,128]{3,2,1,0:T(8,128)(2,1)S(1)}, bf16[4,2,128,128]{3,2,1,0:T(8,128)(2,1)S(1)}, u32[]{:S(2)}, u32[]{:S(2)}) collective-permute-start(bf16[4,2,128,128]{3,2,1,0:T(8,128)(2,1)S(1)} %get-tuple-element.15.rest_5_.refs_4_), channel_id=1, source_target_pairs={{0,1},{1,0},{2,3},{3,2},{4,5},{5,4},{6,7},{7,6},{8,9},{9,8},{10,11... | collective-permute-start | bytes 786440 | tf_op jit(solution)/shard_map/ppermute | solution.py:232
  5.5 13.2 %collective-permute-start.6 = (bf16[544,128]{1,0:T(8,128)(2,1)S(1)}, bf16[544,128]{1,0:T(8,128)(2,1)S(1)}, u32[]{:S(2)}, u32[]{:S(2)}) collective-permute-start(bf16[544,128]{1,0:T(8,128)(2,1)S(1)} %get-tuple-element.18), channel_id=1, source_target_pairs={{0,8},{1,12},{2,10},{3,14},{4,9},{5,13},{6,11},{7,15},{8,0},{9,4},... | collective-permute-start | bytes 417800 | tf_op jit(solution)/shard_map/ppermute | solution.py:240
  8.4 8.4 %collective-permute-start = (bf16[528,128]{1,0:T(8,128)(2,1)S(1)}, bf16[528,128]{1,0:T(8,128)(2,1)S(1)}, u32[]{:S(2)}, u32[]{:S(2)}) collective-permute-start(bf16[528,128]{1,0:T(8,128)(2,1)S(1)} %get-tuple-element.13), channel_id=1, source_target_pairs={{0,4},{1,0},{2,6},{3,2},{4,5},{5,1},{6,7},{7,3},{8,12},{9,8},{10,1... | collective-permute-start | bytes 405512 | tf_op jit(solution)/shard_map/ppermute | solution.py:240
  10.3 8.4 %collective-permute-start.4 = (bf16[528,128]{1,0:T(8,128)(2,1)S(1)}, bf16[528,128]{1,0:T(8,128)(2,1)S(1)}, u32[]{:S(2)}, u32[]{:S(2)}) collective-permute-start(bf16[528,128]{1,0:T(8,128)(2,1)S(1)} %collective-permute-done.1.rest_3_.refs_0_), channel_id=1, source_target_pairs={{0,4},{1,0},{2,6},{3,2},{4,5},{5,1},{6,7},{7,3},{8,12},{9,8},{10,1... | collective-permute-start | bytes 405512 | tf_op jit(solution)/shard_map/ppermute | solution.py:240
  16.7 2.6 %collective-permute-start.5 = (bf16[528,128]{1,0:T(8,128)(2,1)S(1)}, bf16[528,128]{1,0:T(8,128)(2,1)S(1)}, u32[]{:S(2)}, u32[]{:S(2)}) collective-permute-start(bf16[528,128]{1,0:T(8,128)(2,1)S(1)} %collective-permute-done.2.rest_4_.refs_1_), channel_id=1, source_target_pairs={{0,4},{1,0},{2,6},{3,2},{4,5},{5,1},{6,7},{7,3},{8,12},{9,8},{10,1... | collective-permute-start | bytes 405512 | tf_op jit(solution)/shard_map/ppermute | solution.py:240
  16.7 0.7 %copy-start.2 = (s32[4,8]{1,0:T(4,128)S(1)}, s32[4,8]{1,0:T(4,128)}, u32[]{:S(2)}) copy-start(s32[4,8]{1,0:T(4,128)} %blocks_ref.1) | copy-start | bytes 388
  16.8 0.7 %copy-start.3 = (s32[8]{0:T(128)S(1)}, s32[8]{0:T(128)}, u32[]{:S(2)}) copy-start(s32[8]{0:T(128)} %lsize_ref.1) | copy-start | bytes 100
  16.8 0.7 %copy-start.4 = (s32[8]{0:T(128)S(1)}, s32[8]{0:T(128)}, u32[]{:S(2)}) copy-start(s32[8]{0:T(128)} %rsize_ref.1) | copy-start | bytes 100
  20.0 5.5 %collective-permute-start.7 = (bf16[2,2,128,128]{3,2,1,0:T(8,128)(2,1)S(1)}, bf16[2,2,128,128]{3,2,1,0:T(8,128)(2,1)S(1)}, u32[]{:S(2)}, u32[]{:S(2)}) collective-permute-start(bf16[2,2,128,128]{3,2,1,0:T(8,128)(2,1)S(1)} %get-tuple-element.20), channel_id=1, source_target_pairs={{0,2},{1,3},{2,0},{3,1},{4,6},{5,7},{6,4},{7,5},{8,10},{9,11},{10,... | collective-permute-start | bytes 393224 | tf_op jit(solution)/shard_map/ppermute | solution.py:232

commit v13 on v10

--- a/solution.py
+++ b/solution.py
@@ -295,6 +295,7 @@
     )
     arrived = over_op(sent, 2)
     kept = jnp.where(lax.axis_index("blk") // 2 == lax.axis_index("op") // 2, near, far)
+    kept = lax.optimization_barrier(kept)
     return (kept + arrived.astype(jnp.float32)).astype(jnp.bfloat16)
 
 

time: 26.5 us -> 26.5 us (level)
  waiting for transfers between devices: 9.07 us -> 8.4 us
  local copies, waits for them, and re-layouts: 0.02 us -> 0.66 us
    unnamed x10, local copies, waits for them, and re-layouts: 0.02 us -> 0.66 us
    ppermute x6, waiting for transfers between devices: 4.5 us -> 3.87 us  [over_z(): return lax.ppermute(array, ('blk', 'op'), pairs)]
where the time goes in v13:
time: 26.5 us; the launch traced here: 26.4 us
  starting transfers between devices  13.4 us (51%)
  waiting for transfers between devices  8.4 us (32%)
  Pallas kernels  3.11 us (12%)
  other arithmetic  0.71 us (3%)
  local copies, waits for them, and re-layouts  0.66 us (2%)
    ppermute x6, starting transfers between devices, over_z(): return lax.ppermute(array, ('blk', 'op'), pairs)  11.3 us
    ppermute x2, waiting for transfers between devices, over_op(): return lax.ppermute(array, 'op', [(o, o ^ step) for o in range(n)])  4.53 us
    ppermute x6, waiting for transfers between devices, over_z(): return lax.ppermute(array, ('blk', 'op'), pairs)  3.87 us
    ppermute x2, starting transfers between devices, over_op(): return lax.ppermute(array, 'op', [(o, o ^ step) for o in range(n)])  2.1 us
    pallas_call x2, Pallas kernels, apply(): pl.pallas_call(kernel, out_shape=outs, in_specs=[SMEM] * len(scalars) + [...  1.9 us
    pallas_call x1, Pallas kernels, shards(): pl.pallas_call(pack_kernel, out_shape=[block(message_shape), block(messag...  1.21 us
    convert_element_type x1, other arithmetic, shards(): return (kept + arrived.astype(jnp.float32)).astype(jnp.bfloat16)  0.68 us
    unnamed x10, local copies, waits for them, and re-layouts  0.66 us
  transfers between devices with their start and end apart: 8, of which 4 were waited for; matrix products, arithmetic and copies ran while one was open for 0% of the time, Pallas kernels for 5%

profile of v13, /device:TPU:0, one launch (start us, length us, event | category | flops | bytes accessed | tf_op | source)
XLA Modules:
  0.0 26.4 jit_solution(4096999600959786700)
XLA Ops:
  0.0 1.2 %pack.1 = (bf16[528,128]{1,0:T(8,128)(2,1)S(1)}, bf16[528,128]{1,0:T(8,128)(2,1)S(1)}, bf16[544,128]{1,0:T(8,128)(2,1)S(1)}, bf16[4,2,128,128]{3,2,1,0:T(8,128)(2,1)S(1)}) custom-call(s32[4,8]{1,0:T(4,128)} %blocks_ref.1, bf16[2,8,128,128]{3,2,1,0:T(8,128)(2,1)} %rest_0_.1, bf16[4,2,128,128]{3,2,1,0:T(8,128)(2,1)} %rest_1_.1, bf16[4,2,128,128]{3,2,1,0:T(8,128)(2,1)} %right_ref.1), custom_call_target="tpu_custom_call" | custom-call | tf_op jit(solution)/shard_map/pack/pallas_call | solution.py:246
  1.2 0.5 %collective-permute-start.3 = (bf16[4,2,128,128]{3,2,1,0:T(8,128)(2,1)S(1)}, bf16[4,2,128,128]{3,2,1,0:T(8,128)(2,1)S(1)}, u32[]{:S(2)}, u32[]{:S(2)}) collective-permute-start(bf16[4,2,128,128]{3,2,1,0:T(8,128)(2,1)S(1)} %get-tuple-element.15.rest_5_.refs_4_), channel_id=1, source_target_pairs={{0,1},{1,0},{2,3},{3,2},{4,5},{5,4},{6,7},{7,6},{8,9},{9,8},{10,11... | collective-permute-start | bytes 786440 | tf_op jit(solution)/shard_map/ppermute | solution.py:232
  1.7 3.7 %collective-permute-start.1 = (bf16[528,128]{1,0:T(8,128)(2,1)S(1)}, bf16[528,128]{1,0:T(8,128)(2,1)S(1)}, u32[]{:S(2)}, u32[]{:S(2)}) collective-permute-start(bf16[528,128]{1,0:T(8,128)(2,1)S(1)} %get-tuple-element.14), channel_id=1, source_target_pairs={{0,8},{1,4},{2,10},{3,6},{4,1},{5,13},{6,3},{7,15},{8,0},{9,12},{1... | collective-permute-start | bytes 405512 | tf_op jit(solution)/shard_map/ppermute | solution.py:240
  5.4 0.0 collective-permute-start.2
  5.4 1.7 %collective-permute-start = (bf16[528,128]{1,0:T(8,128)(2,1)S(1)}, bf16[528,128]{1,0:T(8,128)(2,1)S(1)}, u32[]{:S(2)}, u32[]{:S(2)}) collective-permute-start(bf16[528,128]{1,0:T(8,128)(2,1)S(1)} %get-tuple-element.13), channel_id=1, source_target_pairs={{0,4},{1,0},{2,6},{3,2},{4,5},{5,1},{6,7},{7,3},{8,12},{9,8},{10,1... | collective-permute-start | bytes 405512 | tf_op jit(solution)/shard_map/ppermute | solution.py:240
  7.1 2.6 %collective-permute-start.6 = (bf16[544,128]{1,0:T(8,128)(2,1)S(1)}, bf16[544,128]{1,0:T(8,128)(2,1)S(1)}, u32[]{:S(2)}, u32[]{:S(2)}) collective-permute-start(bf16[544,128]{1,0:T(8,128)(2,1)S(1)} %get-tuple-element.18), channel_id=1, source_target_pairs={{0,8},{1,12},{2,10},{3,14},{4,9},{5,13},{6,11},{7,15},{8,0},{9,4},... | collective-permute-start | bytes 417800 | tf_op jit(solution)/shard_map/ppermute | solution.py:240
  9.7 0.3 %collective-permute-done.1.rest_3_.refs_0_ = bf16[528,128]{1,0:T(8,128)(2,1)S(1)} collective-permute-done((bf16[528,128]{1,0:T(8,128)(2,1)S(1)}, bf16[528,128]{1,0:T(8,128)(2,1)S(1)}, u32[]{:S(2)}, u32[]{:S(2)}) %collective-permute-start.1) | collective-permute-done | bytes 135200 | tf_op jit(solution)/shard_map/ppermute | solution.py:240
  9.9 0.0 collective-permute-start.4
  9.9 1.9 %collective-permute-done.2.rest_4_.refs_1_ = bf16[528,128]{1,0:T(8,128)(2,1)S(1)} collective-permute-done((bf16[528,128]{1,0:T(8,128)(2,1)S(1)}, bf16[528,128]{1,0:T(8,128)(2,1)S(1)}, u32[]{:S(2)}, u32[]{:S(2)}) %collective-permute-start.2) | collective-permute-done | bytes 135200 | tf_op jit(solution)/shard_map/ppermute | solution.py:240
  11.8 3.4 %collective-permute-start.5 = (bf16[528,128]{1,0:T(8,128)(2,1)S(1)}, bf16[528,128]{1,0:T(8,128)(2,1)S(1)}, u32[]{:S(2)}, u32[]{:S(2)}) collective-permute-start(bf16[528,128]{1,0:T(8,128)(2,1)S(1)} %collective-permute-done.2.rest_4_.refs_1_), channel_id=1, source_target_pairs={{0,4},{1,0},{2,6},{3,2},{4,5},{5,1},{6,7},{7,3},{8,12},{9,8},{10,1... | collective-permute-start | bytes 405512 | tf_op jit(solution)/shard_map/ppermute | solution.py:240
  15.2 0.0 collective-permute-done.rest_2_
  15.2 0.0 collective-permute-done.3.rest_6_.refs_5_
  15.2 0.0 copy-done
  15.2 0.0 copy-done.1
  15.2 0.6 %copy-done.2 = s32[4,8]{1,0:T(4,128)S(1)} copy-done((s32[4,8]{1,0:T(4,128)S(1)}, s32[4,8]{1,0:T(4,128)}, u32[]{:S(2)}) %copy-start.2) | copy-done | bytes 152
  15.9 0.0 copy-done.4
  15.9 1.3 %near.1 = (f32[2,2,128,128]{3,2,1,0:T(8,128)S(1)}, bf16[2,2,128,128]{3,2,1,0:T(8,128)(2,1)S(1)}) custom-call(s32[8]{0:T(128)S(1)} %copy-done.3, s32[8]{0:T(128)S(1)} %copy-done.4, s32[4,8]{1,0:T(4,128)S(1)} %copy-done.2, bf16[2,8,128,128]{3,2,1,0:T(8,128)(2,1)S(1)} %copy-done, bf16[4,2,128,128]{3,2,1,0:T(8,128)(2,1)S(1)} %copy-done.1, ...), custom_call_target="tpu_custom_call" | custom-call | flops 536870912 | bytes 1048576 | tf_op jit(solution)/shard_map/near/pallas_call | solution.py:273
  17.1 1.7 %collective-permute-done.6.refs_8_ = bf16[544,128]{1,0:T(8,128)(2,1)S(1)} collective-permute-done((bf16[544,128]{1,0:T(8,128)(2,1)S(1)}, bf16[544,128]{1,0:T(8,128)(2,1)S(1)}, u32[]{:S(2)}, u32[]{:S(2)}) %collective-permute-start.6) | collective-permute-done | bytes 139296 | tf_op jit(solution)/shard_map/ppermute | solution.py:240
  18.9 0.0 collective-permute-done.4.refs_2_
  18.9 0.0 collective-permute-done.5.refs_3_
  18.9 0.7 %far.1 = (bf16[2,2,128,128]{3,2,1,0:T(8,128)(2,1)S(1)}, f32[2,2,128,128]{3,2,1,0:T(8,128)S(1)}) custom-call(bf16[528,128]{1,0:T(8,128)(2,1)S(1)} %collective-permute-done.1.rest_3_.refs_0_, bf16[528,128]{1,0:T(8,128)(2,1)S(1)} %collective-permute-done.2.rest_4_.refs_1_, bf16[528,128]{1,0:T(8,128)(2,1)S(1)} %collective-permute-done.4.refs_2_, ...), custom_call_target="tpu_custom_call" | custom-call | flops 536870912 | bytes 1048576 | tf_op jit(solution)/shard_map/far/pallas_call | solution.py:273
  19.5 1.6 %collective-permute-start.7 = (bf16[2,2,128,128]{3,2,1,0:T(8,128)(2,1)S(1)}, bf16[2,2,128,128]{3,2,1,0:T(8,128)(2,1)S(1)}, u32[]{:S(2)}, u32[]{:S(2)}) collective-permute-start(bf16[2,2,128,128]{3,2,1,0:T(8,128)(2,1)S(1)} %get-tuple-element.20), channel_id=1, source_target_pairs={{0,2},{1,3},{2,0},{3,1},{4,6},{5,7},{6,4},{7,5},{8,10},{9,11},{10,... | collective-permute-start | bytes 393224 | tf_op jit(solution)/shard_map/ppermute | solution.py:232
  21.1 4.5 %collective-permute-done.7 = bf16[2,2,128,128]{3,2,1,0:T(8,128)(2,1)S(1)} collective-permute-done((bf16[2,2,128,128]{3,2,1,0:T(8,128)(2,1)S(1)}, bf16[2,2,128,128]{3,2,1,0:T(8,128)(2,1)S(1)}, u32[]{:S(2)}, u32[]{:S(2)}) %collective-permute-start.7) | collective-permute-done | bytes 131104 | tf_op jit(solution)/shard_map/ppermute | solution.py:232
  25.7 0.7 %add_convert_fusion = bf16[2,2,128,128]{3,2,1,0:T(8,128)(2,1)} fusion(f32[2,2,128,128]{3,2,1,0:T(8,128)S(1)} %broadcast_select_fusion, bf16[2,2,128,128]{3,2,1,0:T(8,128)(2,1)S(1)} %collective-permute-done.7), kind=kLoop, calls=%fused_computation | loop fusion | flops 196608 | bytes 524288 | tf_op jit(solution)/shard_map/convert_element_type | solution.py:299
  (7 shorter events, 0.0 us)
Async XLA Ops:
  0.0 15.2 %copy-start = (bf16[2,8,128,128]{3,2,1,0:T(8,128)(2,1)S(1)}, bf16[2,8,128,128]{3,2,1,0:T(8,128)(2,1)}, u32[]{:S(2)}) copy-start(bf16[2,8,128,128]{3,2,1,0:T(8,128)(2,1)} %rest_0_.1) | copy-start | bytes 1572868
  0.0 15.2 %copy-start.1 = (bf16[4,2,128,128]{3,2,1,0:T(8,128)(2,1)S(1)}, bf16[4,2,128,128]{3,2,1,0:T(8,128)(2,1)}, u32[]{:S(2)}) copy-start(bf16[4,2,128,128]{3,2,1,0:T(8,128)(2,1)} %rest_1_.1) | copy-start | bytes 786436
  1.2 14.0 %collective-permute-start.3 = (bf16[4,2,128,128]{3,2,1,0:T(8,128)(2,1)S(1)}, bf16[4,2,128,128]{3,2,1,0:T(8,128)(2,1)S(1)}, u32[]{:S(2)}, u32[]{:S(2)}) collective-permute-start(bf16[4,2,128,128]{3,2,1,0:T(8,128)(2,1)S(1)} %get-tuple-element.15.rest_5_.refs_4_), channel_id=1, source_target_pairs={{0,1},{1,0},{2,3},{3,2},{4,5},{5,4},{6,7},{7,6},{8,9},{9,8},{10,11... | collective-permute-start | bytes 786440 | tf_op jit(solution)/shard_map/ppermute | solution.py:232
  1.7 8.2 %collective-permute-start.1 = (bf16[528,128]{1,0:T(8,128)(2,1)S(1)}, bf16[528,128]{1,0:T(8,128)(2,1)S(1)}, u32[]{:S(2)}, u32[]{:S(2)}) collective-permute-start(bf16[528,128]{1,0:T(8,128)(2,1)S(1)} %get-tuple-element.14), channel_id=1, source_target_pairs={{0,8},{1,4},{2,10},{3,6},{4,1},{5,13},{6,3},{7,15},{8,0},{9,12},{1... | collective-permute-start | bytes 405512 | tf_op jit(solution)/shard_map/ppermute | solution.py:240
  5.4 6.4 %collective-permute-start.2 = (bf16[528,128]{1,0:T(8,128)(2,1)S(1)}, bf16[528,128]{1,0:T(8,128)(2,1)S(1)}, u32[]{:S(2)}, u32[]{:S(2)}) collective-permute-start(bf16[528,128]{1,0:T(8,128)(2,1)S(1)} %get-tuple-element.14), channel_id=1, source_target_pairs={{0,4},{1,8},{2,6},{3,10},{4,13},{5,1},{6,15},{7,3},{8,12},{9,0},{1... | collective-permute-start | bytes 405512 | tf_op jit(solution)/shard_map/ppermute | solution.py:240
  5.4 9.8 %collective-permute-start = (bf16[528,128]{1,0:T(8,128)(2,1)S(1)}, bf16[528,128]{1,0:T(8,128)(2,1)S(1)}, u32[]{:S(2)}, u32[]{:S(2)}) collective-permute-start(bf16[528,128]{1,0:T(8,128)(2,1)S(1)} %get-tuple-element.13), channel_id=1, source_target_pairs={{0,4},{1,0},{2,6},{3,2},{4,5},{5,1},{6,7},{7,3},{8,12},{9,8},{10,1... | collective-permute-start | bytes 405512 | tf_op jit(solution)/shard_map/ppermute | solution.py:240
  7.1 11.8 %collective-permute-start.6 = (bf16[544,128]{1,0:T(8,128)(2,1)S(1)}, bf16[544,128]{1,0:T(8,128)(2,1)S(1)}, u32[]{:S(2)}, u32[]{:S(2)}) collective-permute-start(bf16[544,128]{1,0:T(8,128)(2,1)S(1)} %get-tuple-element.18), channel_id=1, source_target_pairs={{0,8},{1,12},{2,10},{3,14},{4,9},{5,13},{6,11},{7,15},{8,0},{9,4},... | collective-permute-start | bytes 417800 | tf_op jit(solution)/shard_map/ppermute | solution.py:240
  9.9 8.9 %collective-permute-start.4 = (bf16[528,128]{1,0:T(8,128)(2,1)S(1)}, bf16[528,128]{1,0:T(8,128)(2,1)S(1)}, u32[]{:S(2)}, u32[]{:S(2)}) collective-permute-start(bf16[528,128]{1,0:T(8,128)(2,1)S(1)} %collective-permute-done.1.rest_3_.refs_0_), channel_id=1, source_target_pairs={{0,4},{1,0},{2,6},{3,2},{4,5},{5,1},{6,7},{7,3},{8,12},{9,8},{10,1... | collective-permute-start | bytes 405512 | tf_op jit(solution)/shard_map/ppermute | solution.py:240
  11.8 7.1 %collective-permute-start.5 = (bf16[528,128]{1,0:T(8,128)(2,1)S(1)}, bf16[528,128]{1,0:T(8,128)(2,1)S(1)}, u32[]{:S(2)}, u32[]{:S(2)}) collective-permute-start(bf16[528,128]{1,0:T(8,128)(2,1)S(1)} %collective-permute-done.2.rest_4_.refs_1_), channel_id=1, source_target_pairs={{0,4},{1,0},{2,6},{3,2},{4,5},{5,1},{6,7},{7,3},{8,12},{9,8},{10,1... | collective-permute-start | bytes 405512 | tf_op jit(solution)/shard_map/ppermute | solution.py:240
  15.2 0.7 %copy-start.2 = (s32[4,8]{1,0:T(4,128)S(1)}, s32[4,8]{1,0:T(4,128)}, u32[]{:S(2)}) copy-start(s32[4,8]{1,0:T(4,128)} %blocks_ref.1) | copy-start | bytes 388
  15.2 0.7 %copy-start.3 = (s32[8]{0:T(128)S(1)}, s32[8]{0:T(128)}, u32[]{:S(2)}) copy-start(s32[8]{0:T(128)} %lsize_ref.1) | copy-start | bytes 100
  15.2 0.7 %copy-start.4 = (s32[8]{0:T(128)S(1)}, s32[8]{0:T(128)}, u32[]{:S(2)}) copy-start(s32[8]{0:T(128)} %rsize_ref.1) | copy-start | bytes 100
  19.5 6.1 %collective-permute-start.7 = (bf16[2,2,128,128]{3,2,1,0:T(8,128)(2,1)S(1)}, bf16[2,2,128,128]{3,2,1,0:T(8,128)(2,1)S(1)}, u32[]{:S(2)}, u32[]{:S(2)}) collective-permute-start(bf16[2,2,128,128]{3,2,1,0:T(8,128)(2,1)S(1)} %get-tuple-element.20), channel_id=1, source_target_pairs={{0,2},{1,3},{2,0},{3,1},{4,6},{5,7},{6,4},{7,5},{8,10},{9,11},{10,... | collective-permute-start | bytes 393224 | tf_op jit(solution)/shard_map/ppermute | solution.py:232

commit v14 on v12

--- a/solution.py
+++ b/solution.py
@@ -287,7 +287,7 @@
     total = jax.ShapeDtypeStruct(out_shape, jnp.float32)
     near, far_mask = apply(
         near_kernel, "near", [total, block(out_shape)], sizes + (term_blocks,),
-        [psi, left_ops, side, direct_a, direct_b] + rights, 1,
+        [psi, left_ops, side, direct_a, direct_b] + rights, 96,
     )
     sent, far = apply(
         far_kernel, "far", [block(out_shape), total], (),

time: 26.4 us -> 25.8 us (0.977)
  waiting for transfers between devices: 12.8 us -> 9.44 us
  starting transfers between devices: 8.86 us -> 11.6 us
    ppermute x6, waiting for transfers between devices: 8.8 us -> 5.08 us  [over_z(): return lax.ppermute(array, ('blk', 'op'), pairs)]
    ppermute x6, starting transfers between devices: 7.13 us -> 9.88 us  [over_z(): return lax.ppermute(array, ('blk', 'op'), pairs)]
    ppermute x2, waiting for transfers between devices: 3.97 us -> 4.35 us  [over_op(): return lax.ppermute(array, 'op', [(o, o ^ step) for o in range(n)])]
where the time goes in v14:
time: 25.8 us; the launch traced here: 25.6 us
  starting transfers between devices  11.6 us (45%)
  waiting for transfers between devices  9.44 us (37%)
  Pallas kernels  3.1 us (12%)
  other arithmetic  0.73 us (3%)
  local copies, waits for them, and re-layouts  0.66 us (3%)
    ppermute x6, starting transfers between devices, over_z(): return lax.ppermute(array, ('blk', 'op'), pairs)  9.88 us
    ppermute x6, waiting for transfers between devices, over_z(): return lax.ppermute(array, ('blk', 'op'), pairs)  5.08 us
    ppermute x2, waiting for transfers between devices, over_op(): return lax.ppermute(array, 'op', [(o, o ^ step) for o in range(n)])  4.35 us
    pallas_call x2, Pallas kernels, apply(): pl.pallas_call(kernel, out_shape=outs, in_specs=[SMEM] * len(scalars) + [...  1.89 us
    ppermute x2, starting transfers between devices, over_op(): return lax.ppermute(array, 'op', [(o, o ^ step) for o in range(n)])  1.75 us
    pallas_call x1, Pallas kernels, shards(): pl.pallas_call(pack_kernel, out_shape=[block(message_shape), block(messag...  1.21 us
    convert_element_type x1, other arithmetic, shards(): return (kept + arrived.astype(jnp.float32)).astype(jnp.bfloat16)  0.69 us
    unnamed x10, local copies, waits for them, and re-layouts  0.66 us
  transfers between devices with their start and end apart: 8, of which 4 were waited for; matrix products, arithmetic and copies ran while one was open for 0% of the time, Pallas kernels for 5%

profile of v14, /device:TPU:0, one launch (start us, length us, event | category | flops | bytes accessed | tf_op | source)
XLA Modules:
  0.0 25.6 jit_solution(17002725713242000832)
XLA Ops:
  0.0 1.2 %pack.1 = (bf16[528,128]{1,0:T(8,128)(2,1)S(1)}, bf16[528,128]{1,0:T(8,128)(2,1)S(1)}, bf16[544,128]{1,0:T(8,128)(2,1)S(1)}, bf16[4,2,128,128]{3,2,1,0:T(8,128)(2,1)S(1)}) custom-call(s32[4,8]{1,0:T(4,128)} %blocks_ref.1, bf16[2,8,128,128]{3,2,1,0:T(8,128)(2,1)} %rest_0_.1, bf16[4,2,128,128]{3,2,1,0:T(8,128)(2,1)} %rest_1_.1, bf16[4,2,128,128]{3,2,1,0:T(8,128)(2,1)} %right_ref.1), custom_call_target="tpu_custom_call" | custom-call | tf_op jit(solution)/shard_map/pack/pallas_call | solution.py:246
  1.2 4.1 %collective-permute-start.1 = (bf16[528,128]{1,0:T(8,128)(2,1)S(1)}, bf16[528,128]{1,0:T(8,128)(2,1)S(1)}, u32[]{:S(2)}, u32[]{:S(2)}) collective-permute-start(bf16[528,128]{1,0:T(8,128)(2,1)S(1)} %get-tuple-element.14), channel_id=1, source_target_pairs={{0,8},{1,4},{2,10},{3,6},{4,1},{5,13},{6,3},{7,15},{8,0},{9,12},{1... | collective-permute-start | bytes 405512 | tf_op jit(solution)/shard_map/ppermute | solution.py:240
  5.3 0.0 collective-permute-start.2
  5.3 0.2 collective-permute-start.3
  5.5 0.9 %collective-permute-start = (bf16[528,128]{1,0:T(8,128)(2,1)S(1)}, bf16[528,128]{1,0:T(8,128)(2,1)S(1)}, u32[]{:S(2)}, u32[]{:S(2)}) collective-permute-start(bf16[528,128]{1,0:T(8,128)(2,1)S(1)} %get-tuple-element.13), channel_id=1, source_target_pairs={{0,4},{1,0},{2,6},{3,2},{4,5},{5,1},{6,7},{7,3},{8,12},{9,8},{10,1... | collective-permute-start | bytes 405512 | tf_op jit(solution)/shard_map/ppermute | solution.py:240
  6.5 2.5 %collective-permute-start.6 = (bf16[544,128]{1,0:T(8,128)(2,1)S(1)}, bf16[544,128]{1,0:T(8,128)(2,1)S(1)}, u32[]{:S(2)}, u32[]{:S(2)}) collective-permute-start(bf16[544,128]{1,0:T(8,128)(2,1)S(1)} %get-tuple-element.18), channel_id=1, source_target_pairs={{0,8},{1,12},{2,10},{3,14},{4,9},{5,13},{6,11},{7,15},{8,0},{9,4},... | collective-permute-start | bytes 417800 | tf_op jit(solution)/shard_map/ppermute | solution.py:240
  9.0 1.4 %collective-permute-done.1.rest_3_.refs_0_ = bf16[528,128]{1,0:T(8,128)(2,1)S(1)} collective-permute-done((bf16[528,128]{1,0:T(8,128)(2,1)S(1)}, bf16[528,128]{1,0:T(8,128)(2,1)S(1)}, u32[]{:S(2)}, u32[]{:S(2)}) %collective-permute-start.1) | collective-permute-done | bytes 135200 | tf_op jit(solution)/shard_map/ppermute | solution.py:240
  10.3 0.0 collective-permute-start.4
  10.3 2.1 %collective-permute-done.2.rest_4_.refs_1_ = bf16[528,128]{1,0:T(8,128)(2,1)S(1)} collective-permute-done((bf16[528,128]{1,0:T(8,128)(2,1)S(1)}, bf16[528,128]{1,0:T(8,128)(2,1)S(1)}, u32[]{:S(2)}, u32[]{:S(2)}) %collective-permute-start.2) | collective-permute-done | bytes 135200 | tf_op jit(solution)/shard_map/ppermute | solution.py:240
  12.5 2.3 %collective-permute-start.5 = (bf16[528,128]{1,0:T(8,128)(2,1)S(1)}, bf16[528,128]{1,0:T(8,128)(2,1)S(1)}, u32[]{:S(2)}, u32[]{:S(2)}) collective-permute-start(bf16[528,128]{1,0:T(8,128)(2,1)S(1)} %collective-permute-done.2.rest_4_.refs_1_), channel_id=1, source_target_pairs={{0,4},{1,0},{2,6},{3,2},{4,5},{5,1},{6,7},{7,3},{8,12},{9,8},{10,1... | collective-permute-start | bytes 405512 | tf_op jit(solution)/shard_map/ppermute | solution.py:240
  14.8 0.0 collective-permute-done.rest_2_
  14.8 0.0 collective-permute-done.3.rest_6_.refs_5_
  14.8 0.0 copy-done
  14.8 0.0 copy-done.1
  14.8 0.6 %copy-done.2 = s32[4,8]{1,0:T(4,128)S(1)} copy-done((s32[4,8]{1,0:T(4,128)S(1)}, s32[4,8]{1,0:T(4,128)}, u32[]{:S(2)}) %copy-start.2) | copy-done | bytes 152
  15.5 0.0 copy-done.3
  15.5 1.3 %near.1 = (f32[2,2,128,128]{3,2,1,0:T(8,128)S(1)}, bf16[2,2,128,128]{3,2,1,0:T(8,128)(2,1)S(1)}) custom-call(s32[8]{0:T(128)S(1)} %copy-done.3, s32[8]{0:T(128)S(1)} %copy-done.4, s32[4,8]{1,0:T(4,128)S(1)} %copy-done.2, bf16[2,8,128,128]{3,2,1,0:T(8,128)(2,1)S(1)} %copy-done, bf16[4,2,128,128]{3,2,1,0:T(8,128)(2,1)S(1)} %copy-done.1, ...), custom_call_target="tpu_custom_call" | custom-call | flops 56623104 | bytes 147456 | tf_op jit(solution)/shard_map/near/pallas_call | solution.py:273
  16.7 1.6 %collective-permute-done.6.refs_8_ = bf16[544,128]{1,0:T(8,128)(2,1)S(1)} collective-permute-done((bf16[544,128]{1,0:T(8,128)(2,1)S(1)}, bf16[544,128]{1,0:T(8,128)(2,1)S(1)}, u32[]{:S(2)}, u32[]{:S(2)}) %collective-permute-start.6) | collective-permute-done | bytes 139296 | tf_op jit(solution)/shard_map/ppermute | solution.py:240
  18.3 0.0 collective-permute-done.4.refs_2_
  18.3 0.0 collective-permute-done.5.refs_3_
  18.3 0.6 %far.1 = (bf16[2,2,128,128]{3,2,1,0:T(8,128)(2,1)S(1)}, f32[2,2,128,128]{3,2,1,0:T(8,128)S(1)}) custom-call(bf16[528,128]{1,0:T(8,128)(2,1)S(1)} %collective-permute-done.1.rest_3_.refs_0_, bf16[528,128]{1,0:T(8,128)(2,1)S(1)} %collective-permute-done.2.rest_4_.refs_1_, bf16[528,128]{1,0:T(8,128)(2,1)S(1)} %collective-permute-done.4.refs_2_, ...), custom_call_target="tpu_custom_call" | custom-call | flops 1073741824 | bytes 1048576 | tf_op jit(solution)/shard_map/far/pallas_call | solution.py:273
  19.0 1.6 %collective-permute-start.7 = (bf16[2,2,128,128]{3,2,1,0:T(8,128)(2,1)S(1)}, bf16[2,2,128,128]{3,2,1,0:T(8,128)(2,1)S(1)}, u32[]{:S(2)}, u32[]{:S(2)}) collective-permute-start(bf16[2,2,128,128]{3,2,1,0:T(8,128)(2,1)S(1)} %get-tuple-element.20), channel_id=1, source_target_pairs={{0,2},{1,3},{2,0},{3,1},{4,6},{5,7},{6,4},{7,5},{8,10},{9,11},{10,... | collective-permute-start | bytes 393224 | tf_op jit(solution)/shard_map/ppermute | solution.py:232
  20.6 4.4 %collective-permute-done.7 = bf16[2,2,128,128]{3,2,1,0:T(8,128)(2,1)S(1)} collective-permute-done((bf16[2,2,128,128]{3,2,1,0:T(8,128)(2,1)S(1)}, bf16[2,2,128,128]{3,2,1,0:T(8,128)(2,1)S(1)}, u32[]{:S(2)}, u32[]{:S(2)}) %collective-permute-start.7) | collective-permute-done | bytes 131104 | tf_op jit(solution)/shard_map/ppermute | solution.py:232
  24.9 0.7 %add_convert_fusion = bf16[2,2,128,128]{3,2,1,0:T(8,128)(2,1)} fusion(f32[2,2,128,128]{3,2,1,0:T(8,128)S(1)} %broadcast_select_fusion, bf16[2,2,128,128]{3,2,1,0:T(8,128)(2,1)S(1)} %collective-permute-done.7), kind=kLoop, calls=%fused_computation | loop fusion | flops 196608 | bytes 524288 | tf_op jit(solution)/shard_map/convert_element_type | solution.py:299
  (7 shorter events, 0.0 us)
Async XLA Ops:
  0.0 14.8 %copy-start = (bf16[2,8,128,128]{3,2,1,0:T(8,128)(2,1)S(1)}, bf16[2,8,128,128]{3,2,1,0:T(8,128)(2,1)}, u32[]{:S(2)}) copy-start(bf16[2,8,128,128]{3,2,1,0:T(8,128)(2,1)} %rest_0_.1) | copy-start | bytes 1572868
  0.0 14.8 %copy-start.1 = (bf16[4,2,128,128]{3,2,1,0:T(8,128)(2,1)S(1)}, bf16[4,2,128,128]{3,2,1,0:T(8,128)(2,1)}, u32[]{:S(2)}) copy-start(bf16[4,2,128,128]{3,2,1,0:T(8,128)(2,1)} %rest_1_.1) | copy-start | bytes 786436
  1.2 9.1 %collective-permute-start.1 = (bf16[528,128]{1,0:T(8,128)(2,1)S(1)}, bf16[528,128]{1,0:T(8,128)(2,1)S(1)}, u32[]{:S(2)}, u32[]{:S(2)}) collective-permute-start(bf16[528,128]{1,0:T(8,128)(2,1)S(1)} %get-tuple-element.14), channel_id=1, source_target_pairs={{0,8},{1,4},{2,10},{3,6},{4,1},{5,13},{6,3},{7,15},{8,0},{9,12},{1... | collective-permute-start | bytes 405512 | tf_op jit(solution)/shard_map/ppermute | solution.py:240
  5.3 7.2 %collective-permute-start.2 = (bf16[528,128]{1,0:T(8,128)(2,1)S(1)}, bf16[528,128]{1,0:T(8,128)(2,1)S(1)}, u32[]{:S(2)}, u32[]{:S(2)}) collective-permute-start(bf16[528,128]{1,0:T(8,128)(2,1)S(1)} %get-tuple-element.14), channel_id=1, source_target_pairs={{0,4},{1,8},{2,6},{3,10},{4,13},{5,1},{6,15},{7,3},{8,12},{9,0},{1... | collective-permute-start | bytes 405512 | tf_op jit(solution)/shard_map/ppermute | solution.py:240
  5.3 9.5 %collective-permute-start.3 = (bf16[4,2,128,128]{3,2,1,0:T(8,128)(2,1)S(1)}, bf16[4,2,128,128]{3,2,1,0:T(8,128)(2,1)S(1)}, u32[]{:S(2)}, u32[]{:S(2)}) collective-permute-start(bf16[4,2,128,128]{3,2,1,0:T(8,128)(2,1)S(1)} %get-tuple-element.15.rest_5_.refs_4_), channel_id=1, source_target_pairs={{0,1},{1,0},{2,3},{3,2},{4,5},{5,4},{6,7},{7,6},{8,9},{9,8},{10,11... | collective-permute-start | bytes 786440 | tf_op jit(solution)/shard_map/ppermute | solution.py:232
  5.5 9.3 %collective-permute-start = (bf16[528,128]{1,0:T(8,128)(2,1)S(1)}, bf16[528,128]{1,0:T(8,128)(2,1)S(1)}, u32[]{:S(2)}, u32[]{:S(2)}) collective-permute-start(bf16[528,128]{1,0:T(8,128)(2,1)S(1)} %get-tuple-element.13), channel_id=1, source_target_pairs={{0,4},{1,0},{2,6},{3,2},{4,5},{5,1},{6,7},{7,3},{8,12},{9,8},{10,1... | collective-permute-start | bytes 405512 | tf_op jit(solution)/shard_map/ppermute | solution.py:240
  6.5 11.9 %collective-permute-start.6 = (bf16[544,128]{1,0:T(8,128)(2,1)S(1)}, bf16[544,128]{1,0:T(8,128)(2,1)S(1)}, u32[]{:S(2)}, u32[]{:S(2)}) collective-permute-start(bf16[544,128]{1,0:T(8,128)(2,1)S(1)} %get-tuple-element.18), channel_id=1, source_target_pairs={{0,8},{1,12},{2,10},{3,14},{4,9},{5,13},{6,11},{7,15},{8,0},{9,4},... | collective-permute-start | bytes 417800 | tf_op jit(solution)/shard_map/ppermute | solution.py:240
  10.3 8.0 %collective-permute-start.4 = (bf16[528,128]{1,0:T(8,128)(2,1)S(1)}, bf16[528,128]{1,0:T(8,128)(2,1)S(1)}, u32[]{:S(2)}, u32[]{:S(2)}) collective-permute-start(bf16[528,128]{1,0:T(8,128)(2,1)S(1)} %collective-permute-done.1.rest_3_.refs_0_), channel_id=1, source_target_pairs={{0,4},{1,0},{2,6},{3,2},{4,5},{5,1},{6,7},{7,3},{8,12},{9,8},{10,1... | collective-permute-start | bytes 405512 | tf_op jit(solution)/shard_map/ppermute | solution.py:240
  12.5 5.8 %collective-permute-start.5 = (bf16[528,128]{1,0:T(8,128)(2,1)S(1)}, bf16[528,128]{1,0:T(8,128)(2,1)S(1)}, u32[]{:S(2)}, u32[]{:S(2)}) collective-permute-start(bf16[528,128]{1,0:T(8,128)(2,1)S(1)} %collective-permute-done.2.rest_4_.refs_1_), channel_id=1, source_target_pairs={{0,4},{1,0},{2,6},{3,2},{4,5},{5,1},{6,7},{7,3},{8,12},{9,8},{10,1... | collective-permute-start | bytes 405512 | tf_op jit(solution)/shard_map/ppermute | solution.py:240
  14.8 0.7 %copy-start.2 = (s32[4,8]{1,0:T(4,128)S(1)}, s32[4,8]{1,0:T(4,128)}, u32[]{:S(2)}) copy-start(s32[4,8]{1,0:T(4,128)} %blocks_ref.1) | copy-start | bytes 388
  14.8 0.7 %copy-start.3 = (s32[8]{0:T(128)S(1)}, s32[8]{0:T(128)}, u32[]{:S(2)}) copy-start(s32[8]{0:T(128)} %lsize_ref.1) | copy-start | bytes 100
  14.8 0.7 %copy-start.4 = (s32[8]{0:T(128)S(1)}, s32[8]{0:T(128)}, u32[]{:S(2)}) copy-start(s32[8]{0:T(128)} %rsize_ref.1) | copy-start | bytes 100
  19.0 5.9 %collective-permute-start.7 = (bf16[2,2,128,128]{3,2,1,0:T(8,128)(2,1)S(1)}, bf16[2,2,128,128]{3,2,1,0:T(8,128)(2,1)S(1)}, u32[]{:S(2)}, u32[]{:S(2)}) collective-permute-start(bf16[2,2,128,128]{3,2,1,0:T(8,128)(2,1)S(1)} %get-tuple-element.20), channel_id=1, source_target_pairs={{0,2},{1,3},{2,0},{3,1},{4,6},{5,7},{6,4},{7,5},{8,10},{9,11},{10,... | collective-permute-start | bytes 393224 | tf_op jit(solution)/shard_map/ppermute | solution.py:232
